TPU v7x, 128 devices: a whole 4x4x4 slice. The times are simulated.
128 devices in a mesh: dp: 64 (over y_hi, x, z, core), fsdp: 2 (over y_lo).
Axes of the slice: x: 4, y: 4 (y_hi: 2, y_lo: 2; y = y_hi * 2 + y_lo), z: 4, core: 2. Of those that a mesh axis runs over, the one named last changes fastest.
Arguments:
- tokens: bfloat16 [128, 192, 1024], P(('dp', 'fsdp')), may hold values from -6 to 6
- memory: float32 [128, 192, 1024], P(('dp', 'fsdp')), may hold values from -6 to 6
- compressed: float32 [128, 192, 1024], P(('dp', 'fsdp')), may hold values from -6 to 6
- cotangent: bfloat16 [128, 192, 1024], P(('dp', 'fsdp')), may hold values from -6 to 6
- ln1_g: bfloat16 [1024], P('fsdp'), may hold values from 0.5 to 1.5
- ln1_b: bfloat16 [1024], P('fsdp'), may hold values from -1.75 to 1.75
- w_q: bfloat16 [1024, 1024], P('fsdp'), may hold values from -0.1875 to 0.1875
- w_kv: bfloat16 [1024, 2048], P('fsdp'), may hold values from -0.1875 to 0.1875
- w_r: bfloat16 [1024, 1024], P('fsdp'), may hold values from -0.1875 to 0.1875
- bias_u: bfloat16 [1024], P('fsdp'), may hold values from -3 to 3
- bias_v: bfloat16 [1024], P('fsdp'), may hold values from -3 to 3
- w_o: bfloat16 [1024, 1024], P('fsdp'), may hold values from -0.75 to 0.75
- ln2_g: bfloat16 [1024], P('fsdp'), may hold values from 0.5 to 1.5
- ln2_b: bfloat16 [1024], P('fsdp'), may hold values from -1.75 to 1.75
- w_in: bfloat16 [1024, 4096], P('fsdp'), may hold values from -0.1875 to 0.1875
- b_in: bfloat16 [4096], P('fsdp'), may hold values from -1.75 to 1.75
- w_out: bfloat16 [4096, 1024], P('fsdp'), may hold values from -0.09375 to 0.09375
- b_out: bfloat16 [1024], P('fsdp'), may hold values from -1.75 to 1.75
- conv_w: bfloat16 [3072, 1024], P('fsdp'), may hold values from -0.109375 to 0.109375
- conv_b: bfloat16 [1024], P('fsdp'), may hold values from -1.75 to 1.75
Outputs:
- mixed_out: bfloat16 [128, 192, 1024], P(('dp', 'fsdp'))
- compressed_next: float32 [128, 192, 1024], P(('dp', 'fsdp'))
- recon_loss: float32 [128], P(('dp', 'fsdp'))
- grad_tokens: float32 [128, 192, 1024], P(('dp', 'fsdp'))
- grad_ln1_g: float32 [1024], P('fsdp')
- grad_ln1_b: float32 [1024], P('fsdp')
- grad_w_q: float32 [1024, 1024], P('fsdp')
- grad_w_kv: float32 [1024, 2048], P('fsdp')
- grad_w_r: float32 [1024, 1024], P('fsdp')
- grad_bias_u: float32 [1024], P('fsdp')
- grad_bias_v: float32 [1024], P('fsdp')
- grad_w_o: float32 [1024, 1024], P('fsdp')
- grad_ln2_g: float32 [1024], P('fsdp')
- grad_ln2_b: float32 [1024], P('fsdp')
- grad_w_in: float32 [1024, 4096], P('fsdp')
- grad_b_in: float32 [4096], P('fsdp')
- grad_w_out: float32 [4096, 1024], P('fsdp')
- grad_b_out: float32 [1024], P('fsdp')
- grad_conv_w: float32 [3072, 1024], P('fsdp')
- grad_conv_b: float32 [1024], P('fsdp')
All inputs are finite; a program needn't handle non-finite values.
Results may differ from a plain program's by a relative error of at most 0.015.
Values may be sent and summed in bfloat16 or wider, within the bound.
No kernel may reach another device: no remote copies, remote signals or barrier semaphores. Data moves between devices by JAX's collectives and lax.ppermute only.
A program may use at most 384 MiB of HBM per device.

v0:
```python
import jax
import jax.numpy as jnp
from jax import lax
from jax.experimental import pallas as pl
from jax.experimental.pallas import tpu as pltpu
from jax.sharding import Mesh, PartitionSpec as P

H = 8
HD = 128
D = 1024
T = 192
KEYS = 576
PAD = 640
FF = 4096
FACTOR = HD ** (-0.5)
f32 = jnp.float32
bf16 = jnp.bfloat16
AXES = ("yh", "x", "z", "c", "yl")
RING = {"x": ("x", "c"), "z": ("z", "c"), "y": ("yh", "c", "yl")}


def sinusoid(key_count, model_dim):
    distance = (key_count - 1 - jnp.arange(key_count)).astype(f32)
    inverse = 1.0 / 10000.0 ** (jnp.arange(0, model_dim, 2).astype(f32) / model_dim)
    angles = distance[:, None] * inverse[None, :]
    return jnp.concatenate([jnp.sin(angles), jnp.cos(angles)], axis=-1)


def dot(a, b):
    return jnp.dot(a, b, preferred_element_type=f32)


def dot_t(a, b):
    return lax.dot_general(a, b, (((1,), (1,)), ((), ())), preferred_element_type=f32)


def t_dot(a, b):
    return lax.dot_general(a, b, (((0,), (0,)), ((), ())), preferred_element_type=f32)


class Line:
    def __init__(self):
        self.held = []

    def hold(self, *values):
        self.held += values

    def later(self, value):
        return lax.optimization_barrier((value, *self.held))[0] if self.held else value

    def ran(self, value):
        self.held = [value]


line = Line()


def call(kernel, out, grid, in_specs, out_specs, scalars, args, scratch=()):
    result = run_kernel(
        kernel, out, grid, in_specs, out_specs, line.later(scalars), args, scratch
    )
    line.ran(jax.tree.leaves(result)[0])
    return result


def run_kernel(kernel, out, grid, in_specs, out_specs, scalars, args, scratch):
    return pl.pallas_call(
        kernel,
        out_shape=out,
        grid_spec=pltpu.PrefetchScalarGridSpec(
            num_scalar_prefetch=1,
            grid=grid,
            in_specs=in_specs,
            out_specs=out_specs,
            scratch_shapes=list(scratch),
        ),
        compiler_params=pltpu.CompilerParams(vmem_limit_bytes=56 << 20),
    )(scalars, *args)


def whole(a):
    zeros = (0,) * a.ndim
    return pl.BlockSpec(a.shape, lambda *_: zeros)


def shape(dims, dtype):
    return jax.ShapeDtypeStruct(dims, dtype)


def at(offset):
    return pl.multiple_of(offset, 128)


def center_scale(v):
    mid = v - jnp.mean(v, axis=-1, keepdims=True)
    r = lax.rsqrt(jnp.mean(mid * mid, axis=-1, keepdims=True) + 1e-5)
    return mid * r, r


def norm_back(xhat, r, g, dn):
    gd = dn * g
    return r * (
        gd
        - jnp.mean(gd, axis=-1, keepdims=True)
        - xhat * jnp.mean(gd * xhat, axis=-1, keepdims=True)
    )


def softmax(s):
    e = jnp.exp(s - jnp.max(s, axis=-1, keepdims=True))
    return e / jnp.sum(e, axis=-1, keepdims=True)


(LN1_G, LN1_B, BIAS_U, BIAS_V, LN2_G, LN2_B, B_OUT, CONV_B) = range(8)


def row(ref, i):
    return ref[i : i + 1, :]


def pack(vectors, w_in, w_out, conv_w, scalars):
    n_in, n_out, n_conv = (w.shape[0] // 32 for w in (w_in, w_out, conv_w))
    chunks = FF // D
    rows = n_out + n_in * chunks + n_conv

    def kernel(_, *refs):
        wi, wo, wc, flat, piece = refs[-5:]
        for i, ref in enumerate(refs[:8]):
            flat[i : i + 1, :] = ref[...].astype(f32).reshape(1, STEP)
        b_in = refs[8][...].astype(f32).reshape(chunks, STEP)
        flat[8 : 8 + chunks, :] = b_in
        flat[8 + chunks :, :] = jnp.zeros((16 - 8 - chunks, STEP), f32)
        piece[:n_out, :] = wo[...]
        for i in range(chunks):
            piece[n_out + i * n_in : n_out + (i + 1) * n_in, :] = wi[:, i * D : (i + 1) * D]
        piece[n_out + n_in * chunks :, :] = wc[...]

    out = (shape((16, STEP), f32), shape((rows, D), bf16))
    return call(
        kernel,
        out,
        (1,),
        [whole(v) for v in vectors]
        + [
            pl.BlockSpec((w.shape[0] // 32, w.shape[1]), lambda j, s: (s[0], 0))
            for w in (w_in, w_out, conv_w)
        ],
        [whole(o) for o in out],
        scalars,
        (*vectors, w_in, w_out, conv_w),
    )


def pack_rows(w_kv, w_q, w_r, w_o, scalars):
    n = w_q.shape[0] // 2

    def kernel(_, kv, q, r, o, kv_out, out):
        kv_out[...] = kv[...]
        for i, ref in enumerate((q, r, o)):
            out[i] = ref[...]

    out = (shape((n, 2 * D), bf16), shape((3, n, D), bf16))
    return call(
        kernel,
        out,
        (1,),
        [
            pl.BlockSpec((n, w.shape[1]), lambda j, s: (s[0], 0))
            for w in (w_kv, w_q, w_r, w_o)
        ],
        [whole(o) for o in out],
        scalars,
        (w_kv, w_q, w_r, w_o),
    )


def unpack(mine, theirs, scalars):
    half = D // 2

    def kernel(s, mine, theirs, vectors, b_in):
        a, b = mine[...], theirs[...]
        low = jnp.where(s[0] == 0, a, b)
        high = jnp.where(s[0] == 0, b, a)
        vectors[:, :half] = low[:8]
        vectors[:, half:] = high[:8]
        for i in range(FF // D):
            part, k = (low, i) if i < 2 else (high, i - 2)
            b_in[i : i + 1, :half] = part[8 + 2 * k : 9 + 2 * k]
            b_in[i : i + 1, half:] = part[9 + 2 * k : 10 + 2 * k]

    args = (mine, theirs)
    out = (shape((8, D), f32), shape((FF // D, D), f32))
    return call(
        kernel, out, (1,), [whole(a) for a in args], [whole(o) for o in out], scalars, args
    )


def relative_columns(x, s, widths):
    parts = [x[:, pl.ds(at(s[i]), width)] for i, width in enumerate(widths)]
    return jnp.concatenate(parts, axis=1)


def natural_columns(out, x, s, widths):
    start = 0
    for i, width in enumerate(widths):
        out[:, pl.ds(at(s[i]), width)] = x[:, start : start + width]
        start += width


THIRDS = (D // 2, D // 4, D // 4)


def first_norm(compressed, memory, tokens, vectors, offsets):
    def kernel(s, comp, mem, tok, vec, out, out_rel, old):
        gain, bias = row(vec, LN1_G), row(vec, LN1_B)

        def part(ref, base):
            for i in range(0, T, 32):
                xhat, r = center_scale(ref[i : i + 32, :].astype(f32))
                out[base + i : base + i + 32, :] = (xhat * gain + bias).astype(bf16)

        part(comp, 0)
        part(mem, T)
        part(tok, 2 * T)
        out_rel[...] = relative_columns(out, s, THIRDS)
        line_of = lax.broadcasted_iota(jnp.int32, (T // 3, T), 0)
        col = lax.broadcasted_iota(jnp.int32, (T // 3, T), 1)
        low = mem[...].astype(bf16)
        for tap in range(3):
            take = jnp.where(col == 3 * line_of + tap, 1.0, 0.0).astype(bf16)
            old[:, tap * D : (tap + 1) * D] = dot(take, low).astype(bf16)

    args = (compressed, memory, tokens, vectors)
    out = (shape((KEYS, D), bf16), shape((KEYS, D), bf16), shape((T // 3, 3 * D), bf16))
    return call(
        kernel, out, (1,), [whole(a) for a in args], [whole(o) for o in out], offsets, args
    )


PAIR = 2
STEPS = H // PAIR


def head(rows, row_block=0, first=0):
    return pl.BlockSpec((rows, PAIR * HD), lambda h, s: (row_block, first // PAIR + h))


def vec_head(rows=1):
    return pl.BlockSpec((rows, PAIR * HD), lambda h, s: (0, h))


def each_head(body):
    for i in range(PAIR):
        body(i, slice(i * HD, (i + 1) * HD))


def attend(queries, key_value, relative, vectors, none):
    def kernel(_, q, k, v, rel, vec, probs, out):
        pad = jnp.zeros((PAD - KEYS, HD), bf16)
        row = lax.broadcasted_iota(jnp.int32, (T, PAD), 0)
        col = lax.broadcasted_iota(jnp.int32, (T, PAD), 1)
        seen = col <= row + (KEYS - T)

        def body(i, cut):
            content = ((q[:, cut] + vec[BIAS_U : BIAS_U + 1, cut]) * FACTOR).astype(bf16)
            located = ((q[:, cut] + vec[BIAS_V : BIAS_V + 1, cut]) * FACTOR).astype(bf16)
            raw = dot_t(located, jnp.concatenate([rel[:, cut], pad], axis=0))
            raw = pltpu.roll(raw, PAD - T + 1, 1, stride=1, stride_axis=0)
            s = dot_t(content, jnp.concatenate([k[:, cut], pad], axis=0)) + raw
            p = softmax(jnp.where(seen, s, -1e30))
            probs[i] = p
            low = p.astype(bf16)
            out[:, cut] = dot(low, jnp.concatenate([v[:, cut], pad], axis=0)).astype(bf16)

        each_head(body)

    return call(
        kernel,
        (shape((H, T, PAD), f32), shape((T, D), bf16)),
        (STEPS,),
        [head(T), head(KEYS), head(KEYS, 0, H), head(KEYS), vec_head(8)],
        [pl.BlockSpec((PAIR, T, PAD), lambda h, s: (h, 0, 0)), head(T)],
        none,
        (queries, key_value, key_value, relative, vectors),
    )


def attend_back(queries, key_value, relative, vectors, probs, d_attended, scalars):
    def kernel(s, q, k, v, rel, vec, probs, d_att, d_kv, mine, give, d_rel, d_q, d_bu, d_bv):
        pad = jnp.zeros((PAD - KEYS, HD), bf16)
        row = lax.broadcasted_iota(jnp.int32, (T, T), 0)
        col = lax.broadcasted_iota(jnp.int32, (T, T), 1)
        flip = jnp.where(row + col == T - 1, 1.0, 0.0).astype(bf16)

        def body(i, cut):
            content = ((q[:, cut] + vec[BIAS_U : BIAS_U + 1, cut]) * FACTOR).astype(bf16)
            located = ((q[:, cut] + vec[BIAS_V : BIAS_V + 1, cut]) * FACTOR).astype(bf16)
            p, da = probs[i], d_att[:, cut]
            d_p = dot_t(da, jnp.concatenate([v[:, cut], pad], axis=0))
            d_v = t_dot(p.astype(bf16), da)[:KEYS].astype(bf16)
            d_s = (p * (d_p - jnp.sum(p * d_p, axis=-1, keepdims=True))).astype(bf16)
            d_c = dot(d_s, jnp.concatenate([k[:, cut], pad], axis=0)) * FACTOR
            d_k = t_dot(d_s, content)[:KEYS].astype(bf16)
            d_kv[0, :, cut] = d_k
            d_kv[1, :, cut] = d_v
            mine[:, cut] = jnp.where(s[0] == 0, d_k, d_v)
            give[:, cut] = jnp.where(s[0] == 0, d_v, d_k)
            d_raw = pltpu.roll(dot(flip, d_s), 0, 1, stride=1, stride_axis=0)
            d_raw = dot(flip, d_raw.astype(bf16)).astype(bf16)
            d_l = dot(d_raw, jnp.concatenate([rel[:, cut], pad], axis=0)) * FACTOR
            d_rel[:, cut] = t_dot(d_raw, located)[:KEYS].astype(bf16)
            d_q[:, cut] = (d_c + d_l).astype(bf16)
            d_bu[:, cut] = jnp.sum(d_c, axis=0, keepdims=True)
            d_bv[:, cut] = jnp.sum(d_l, axis=0, keepdims=True)

        each_head(body)

    return call(
        kernel,
        (
            shape((2, KEYS, D), bf16),
            shape((KEYS, D), bf16),
            shape((KEYS, D), bf16),
            shape((KEYS, D), bf16),
            shape((T, D), bf16),
            shape((1, D), f32),
            shape((1, D), f32),
        ),
        (STEPS,),
        [
            head(T),
            head(KEYS),
            head(KEYS, 0, H),
            head(KEYS),
            vec_head(8),
            pl.BlockSpec((PAIR, T, PAD), lambda h, s: (h, 0, 0)),
            head(T),
        ],
        [
            pl.BlockSpec((2, KEYS, PAIR * HD), lambda h, s: (0, 0, h)),
            head(KEYS),
            head(KEYS),
            head(KEYS),
            head(T),
            vec_head(),
            vec_head(),
        ],
        scalars,
        (queries, key_value, key_value, relative, vectors, probs, d_attended),
    )


def out_and_norm(attended, w_o, tokens, vectors, offsets):
    def kernel(s, att, w, tok, vec, res, n2, n2_rel):
        total = tok[...].astype(f32) + dot(relative_columns(att, s, THIRDS), w[...])
        res[...] = total
        xhat, r = center_scale(total)
        n2[...] = (xhat * row(vec, LN2_G) + row(vec, LN2_B)).astype(bf16)
        other = at(D // 2 - s[0])
        n2_rel[:, : D // 2] = n2[:, pl.ds(at(s[0]), D // 2)]
        n2_rel[:, D // 2 :] = n2[:, pl.ds(other, D // 2)]

    args = (attended, w_o, tokens, vectors)
    out = (shape((T, D), f32), shape((T, D), bf16), shape((T, D), bf16))
    return call(
        kernel, out, (1,), [whole(a) for a in args], [whole(o) for o in out], offsets, args
    )


STEP = 512
UNITS = 1024
HALF = FF // 2 // UNITS


def feed_forward(n2_rel, residual, cotangent, w_in, w_out, spread, b_in, vectors, scalars):
    n_in = w_in.shape[0] // 32
    n_out = w_out.shape[0] // 32
    skip = n_out // n_in
    per = UNITS // n_out
    K_NORM = 0.7978845608028654

    def natural(j, s):
        return lax.rem(j + s[0] * HALF, 2 * HALF)

    def kernel(s, n2, res, cot, wi0, wi1, wo0, wo1, bi, vec, hid, dpre, mixed, dn2, dbi, acc, back):
        j = pl.program_id(0)
        n = natural(j, s)
        win = jnp.concatenate([wi0[...], wi1[...].reshape(D // 2, UNITS)], axis=0)
        pre = dot(n2[...], win) + bi[pl.ds(n, 1), :]
        t = jnp.tanh(K_NORM * (pre + 0.044715 * (pre * pre * pre)))
        hidden = (0.5 * pre * (1.0 + t)).astype(bf16)
        slope = 0.5 * (1.0 + t) + (0.5 * K_NORM) * pre * (1.0 - t * t) * (
            1.0 + (3 * 0.044715) * (pre * pre)
        )
        hid[...] = hidden

        def rest(wo, start):
            d_pre = (dot_t(cot[...], wo) * slope).astype(bf16)
            dpre[...] = d_pre
            dbi[pl.ds(n, 1), :] = jnp.sum(d_pre.astype(f32), axis=0, keepdims=True)
            if start:
                acc[...] = dot(hidden, wo)
                back[...] = dot_t(d_pre, win)
            else:
                acc[...] += dot(hidden, wo)
                back[...] += dot_t(d_pre, win)

        @pl.when(j == 0)
        def _():
            rest(wo0[...], True)

        @pl.when((j > 0) & (j < HALF))
        def _():
            rest(wo0[...], False)

        @pl.when(j >= HALF)
        def _():
            rest(wo1[...].reshape(UNITS, D), False)

        @pl.when(j == 2 * HALF - 1)
        def _():
            mixed[...] = (res[...] + acc[...] + row(vec, B_OUT)).astype(bf16)
            dn2[:, pl.ds(at(s[0] * (D // 2)), D // 2)] = back[:, : D // 2]
            dn2[:, pl.ds(at((1 - s[0]) * (D // 2)), D // 2)] = back[:, D // 2 :]

    out = (
        shape((T, FF), bf16),
        shape((T, FF), bf16),
        shape((T, D), bf16),
        shape((T, D), f32),
        shape((2 * HALF, UNITS), f32),
    )
    by_unit = pl.BlockSpec((T, UNITS), lambda j, s: (0, natural(j, s)))
    return call(
        kernel,
        out,
        (2 * HALF,),
        [
            whole(n2_rel),
            whole(residual),
            whole(cotangent),
            pl.BlockSpec((D // 2, UNITS), lambda j, s: (0, natural(j, s))),
            pl.BlockSpec((32, n_in, UNITS), lambda j, s: (0, skip + natural(j, s), 0)),
            pl.BlockSpec((UNITS, D), lambda j, s: (jnp.minimum(j, HALF - 1), 0)),
            pl.BlockSpec(
                (per, n_out, D), lambda j, s: (jnp.maximum(j - HALF, 0), 0, 0)
            ),
            whole(b_in),
            whole(vectors),
        ],
        [by_unit, by_unit, whole(out[2]), whole(out[3]), whole(out[4])],
        scalars,
        (n2_rel, residual, cotangent, w_in, spread, w_out, spread, b_in, vectors),
        [pltpu.VMEM((T, D), f32), pltpu.VMEM((T, D), f32)],
    )


def second_norm_back(cotangent, d_n2, residual, vectors, w_o, offsets):
    def kernel(s, cot, dn, res, vec, w, d_res, d_br, d_att, dg, db, dbo):
        xhat, r = center_scale(res[...])
        dn, wide = dn[...], cot[...].astype(f32)
        dg[...] = jnp.sum(dn * xhat, axis=0, keepdims=True)
        db[...] = jnp.sum(dn, axis=0, keepdims=True)
        dbo[...] = jnp.sum(wide, axis=0, keepdims=True)
        total = wide + norm_back(xhat, r, row(vec, LN2_G), dn)
        d_res[...] = total
        low = total.astype(bf16)
        d_br[...] = low
        natural_columns(d_att, dot_t(low, w[...]).astype(bf16), s, THIRDS)

    args = (cotangent, d_n2, residual, vectors, w_o)
    out = (
        shape((T, D), f32),
        shape((T, D), bf16),
        shape((T, D), bf16),
        shape((1, D), f32),
        shape((1, D), f32),
        shape((1, D), f32),
    )
    return call(
        kernel, out, (1,), [whole(a) for a in args], [whole(o) for o in out], offsets, args
    )


def first_norm_back(d_kv, d_q, w_kv, w_q, compressed, memory, tokens, vectors, d_res, offsets):
    steps = 4
    wide, slim = 2 * D // steps, D // steps

    def kernel(s, dkv, dq, kw, qw, comp, mem, tok, vec, dres, dtok, dg, db, acc, nat):
        j = pl.program_id(0)

        @pl.when(j == 0)
        def _():
            acc[...] = dot_t(dkv[0], kw[...])

        @pl.when(j > 0)
        def _():
            acc[...] += dot_t(dkv[0], kw[...])

        acc[2 * T :, :] += dot_t(dq[...], qw[...])

        @pl.when(j == steps - 1)
        def _():
            natural_columns(nat, acc, s, THIRDS)
            gain = row(vec, LN1_G)
            sum_g = jnp.zeros((1, D), f32)
            sum_b = jnp.zeros((1, D), f32)
            for block, ref in enumerate((comp, mem, tok)):
                for i in range(0, T, 32):
                    xhat, r = center_scale(ref[i : i + 32, :].astype(f32))
                    dn = nat[block * T + i : block * T + i + 32, :]
                    sum_g += jnp.sum(dn * xhat, axis=0, keepdims=True)
                    sum_b += jnp.sum(dn, axis=0, keepdims=True)
                    if block == 2:
                        dtok[i : i + 32, :] = dres[i : i + 32, :] + norm_back(xhat, r, gain, dn)
            dg[...] = sum_g
            db[...] = sum_b

    rest = (compressed, memory, tokens, vectors, d_res)
    out = (shape((T, D), f32), shape((1, D), f32), shape((1, D), f32))
    return call(
        kernel,
        out,
        (steps,),
        [
            pl.BlockSpec((1, KEYS, wide), lambda j, s: (j // (steps // 2), 0, lax.rem(j, steps // 2))),
            pl.BlockSpec((T, slim), lambda j, s: (0, j)),
            pl.BlockSpec((D, wide), lambda j, s: (0, j)),
            pl.BlockSpec((D, slim), lambda j, s: (0, j)),
        ]
        + [whole(a) for a in rest],
        [whole(o) for o in out],
        offsets,
        (d_kv, d_q, w_kv, w_q, *rest),
        [pltpu.VMEM((KEYS, D), f32), pltpu.VMEM((KEYS, D), f32)],
    )


def compress(oldest, conv_w, spread, vectors, offsets):
    block = 256
    rows = T // 3
    n = conv_w.shape[0] // 32
    skip = (spread.shape[1] - n) // 16

    def kernel(s, x, own, w0, w1, w2, vec, compact, normed, x_rel, natural):
        j = pl.program_id(0)

        @pl.when(j == 0)
        def _():
            x_rel[...] = relative_columns(x, s, (3 * D // 2, 3 * D // 2))

        other = jnp.concatenate([w0[...], w1[...], w2[...]], axis=1).reshape(32 * n, block)
        w = jnp.concatenate([own[...], other], axis=0)
        here = pl.ds(at(j * block), block)
        compact[:, here] = dot(x_rel[...], w) + vec[CONV_B : CONV_B + 1, here]

        @pl.when(j == D // block - 1)
        def _():
            xhat, r = center_scale(compact[...])
            natural[...] = (xhat * row(vec, LN1_G) + row(vec, LN1_B)).astype(bf16)
            start = 0
            for i, width in enumerate(THIRDS):
                normed[:, start : start + width] = natural[:, pl.ds(at(s[2 + i]), width)]
                start += width

    out = (shape((rows, D), f32), shape((rows, D), bf16))
    return call(
        kernel,
        out,
        (D // block,),
        [whole(oldest), pl.BlockSpec((conv_w.shape[0], block), lambda j, s: (0, j))]
        + [
            pl.BlockSpec((32, 16, block), lambda j, s, i=i: (0, skip + i, j))
            for i in range(n // 16)
        ]
        + [whole(vectors)],
        [whole(o) for o in out],
        offsets,
        (oldest, conv_w) + (spread,) * (n // 16) + (vectors,),
        [pltpu.VMEM((rows, 3 * D), bf16), pltpu.VMEM((rows, D), bf16)],
    )


def reconstruct(queries, key_value, comp_pair, none):
    rows = T // 3

    def kernel(_, q, k, v, ck, cv, loss, dck, dcv):
        @pl.when(pl.program_id(0) == 0)
        def _():
            loss[...] = jnp.zeros_like(loss)

        def body(i, cut):
            asking = (q[:, cut] * FACTOR).astype(bf16)
            cvh = cv[:, cut]
            p = softmax(dot_t(asking, k[:, cut])).astype(bf16)
            gp = softmax(dot_t(asking, ck[:, cut]))
            low = gp.astype(bf16)
            miss = dot(p, v[:, cut]) - dot(low, cvh)
            loss[...] += jnp.sum(miss * miss, axis=0, keepdims=True)
            d_guess = ((-2.0 / (T * D)) * miss).astype(bf16)
            d_gp = dot_t(d_guess, cvh)
            dcv[:, cut] = t_dot(low, d_guess).astype(bf16)
            d_gs = (gp * (d_gp - jnp.sum(gp * d_gp, axis=-1, keepdims=True))).astype(bf16)
            dck[:, cut] = t_dot(d_gs, asking).astype(bf16)

        each_head(body)

    return call(
        kernel,
        (shape((1, HD), f32), shape((rows, D), bf16), shape((rows, D), bf16)),
        (STEPS,),
        [head(T), head(T, 1), head(T, 1, H), head(rows), head(rows, 0, H)],
        [pl.BlockSpec((1, HD), lambda h, s: (0, 0)), head(rows), head(rows)],
        none,
        (queries, key_value, key_value, comp_pair, comp_pair),
    )


def compress_back(dck, dcv, w_kv, compact, vectors, offsets):
    rows = T // 3

    def kernel(s, dck, dcv, w, compact, vec, d_compact, d_bias, dn):
        back = dot_t(jnp.concatenate([dck[...], dcv[...]], axis=1), w[...])
        natural_columns(dn, back, s, THIRDS)
        xhat, r = center_scale(compact[...])
        low = norm_back(xhat, r, row(vec, LN1_G), dn[...]).astype(bf16)
        d_compact[...] = low
        d_bias[...] = jnp.sum(low.astype(f32), axis=0, keepdims=True)

    args = (dck, dcv, w_kv, compact, vectors)
    out = (shape((rows, D), bf16), shape((1, D), f32))
    return call(
        kernel,
        out,
        (1,),
        [whole(a) for a in args],
        [whole(o) for o in out],
        offsets,
        args,
        [pltpu.VMEM((rows, D), f32)],
    )


def weight_grads(groups, scalars):
    in_specs, args, outs, out_specs, layout = [], [], [], [], []
    for ring, jobs in groups:
        first = 1 if ring == "x" else 5
        block = jobs[0][0][0].shape[1] // 8
        widths = []
        for xs, row_block, rows, dys, ready in jobs:
            width = dys[0].shape[1] // (1 if ready else 2)
            widths.append(width)
            for x in xs:
                for y in range(2):
                    in_specs.append(
                        pl.BlockSpec(
                            (rows, block),
                            lambda q, s, r=row_block, f=first, y=y: (r, y * 4 + s[f + q]),
                        )
                    )
                    args.append(x)
            for dy in dys:
                in_specs.append(
                    pl.BlockSpec((rows, width), lambda q, s, r=ready: (0, 0 if r else s[0]))
                )
                args.append(dy)
        dims = (1, 2, block, sum(widths))
        outs += [shape((2, *dims[1:]), bf16)] * 2
        out_specs += [
            pl.BlockSpec(dims, lambda q, s: (jnp.minimum(q, 1), 0, 0, 0)),
            pl.BlockSpec(dims, lambda q, s: (jnp.maximum(q - 2, 0), 0, 0, 0)),
        ]
        layout.append(widths)

    def kernel(s, *refs):
        q = pl.program_id(0)
        place = 0
        results = refs[len(in_specs) :]
        for i, widths in enumerate(layout):
            send, keep = results[2 * i : 2 * i + 2]
            block = send.shape[2]
            start = 0
            for width in widths:
                a0, a1, b0, b1, da, db = (r[...] for r in refs[place : place + 6])
                place += 6
                x = jnp.concatenate(
                    [jnp.concatenate([a0, a1], axis=1), jnp.concatenate([b0, b1], axis=1)], axis=0
                )
                value = t_dot(x, jnp.concatenate([da, db], axis=0)).astype(bf16)
                value = value.reshape(2, block, width)
                cut = slice(start, start + width)
                send[0, :, :, cut] = jnp.where(q < 2, value, send[0, :, :, cut])
                keep[0, :, :, cut] = value
                start += width

    flat = call(kernel, tuple(outs), (4,), in_specs, out_specs, scalars, args)
    return [(flat[2 * i], flat[2 * i + 1]) for i in range(len(groups))]


def widen(gathered, start, rows, columns, swapped, none):
    u = rows // 16
    sub = u // 32
    chunks = columns // 2 // STEP
    order = [x * 4 + z for z in range(4) for x in range(4)] if swapped else list(range(16))

    def kernel(_, *refs):
        out = refs[-1]
        for k, src in enumerate(refs[:-1]):
            for to, frm in enumerate(order):
                out[to, :, k * STEP : (k + 1) * STEP] = src[frm].astype(f32)

    return call(
        kernel,
        shape((16, u, columns), f32),
        (sub, 2),
        [
            pl.BlockSpec((16, 32, STEP), lambda i, c, s, k=k: (c, start // 32 + k * sub + i, 0))
            for k in range(chunks)
        ],
        pl.BlockSpec((16, 32, STEP * chunks), lambda i, c, s: (0, i, c)),
        none,
        (gathered,) * chunks,
    ).reshape(rows, columns)


def widen_near(own, twin, start, columns, swapped, scalars):
    chunks = columns // 2 // STEP
    u = D // 32

    def kernel(s, own, twin, out):
        def fill(src, base):
            for a in range(4):
                for b in range(4):
                    first, second = s[base + a], s[base + 4 + b]
                    place = second * 4 + first if swapped else first * 4 + second
                    for k in range(chunks):
                        rows = slice(start + k * u, start + (k + 1) * u)
                        value = src[a, b, rows, :].astype(f32)
                        out[pl.ds(place, 1), :, k * STEP : (k + 1) * STEP] = value[None]

        @pl.when(pl.program_id(0) == 0)
        def _():
            fill(own, 1)

        @pl.when(pl.program_id(0) == 1)
        def _():
            fill(twin, 9)

    return call(
        kernel,
        shape((16, u, columns), f32),
        (2,),
        [whole(own), whole(twin)],
        pl.BlockSpec((16, u, chunks * STEP), lambda h, s: (0, 0, lax.rem(h + s[0], 2))),
        scalars,
        (own, twin),
    ).reshape(D // 2, columns)


def core_swap(v):
    return lax.ppermute(v, "c", [(0, 1), (1, 0)])


def pair_swap(v):
    return lax.ppermute(v, "yl", [(0, 1), (1, 0)])


def exchange(v, ring, masks):
    def flat(i, c):
        return (i // 2 * 2 + c) * 2 + i % 2 if ring == "y" else 2 * i + c

    pairs = [(flat(i, c), flat(i ^ masks[c], c)) for i in range(4) for c in range(2)]
    return lax.ppermute(v, RING[ring], pairs)


def pick(v, index, axis):
    return lax.dynamic_index_in_dim(v, index, axis, keepdims=False)


def quarters(place, core):
    first = jnp.where(core == 0, 1, 3)
    second = jnp.where(core == 0, 3, 1)
    return place, place ^ first, place ^ 2, place ^ second


class Flow:
    def __init__(self, ring, pair, place, core):
        self.rings = (ring, "z" if ring == "x" else "x")
        self.place, self.core = place, core
        send, self.keep = pair
        self.got = exchange(send, ring, (1, 3))

    def onward(self, ring):
        got = line.later(self.got)
        self.near = got[0]
        value = (self.keep[1].astype(f32) + got[1].astype(f32)).astype(bf16)
        self.last = exchange(value, ring, (3, 1))
        line.hold(value)

    def settle(self):
        last = line.later(self.last)
        return self.keep[0].astype(f32) + self.near.astype(f32) + last.astype(f32)

    def second(self):
        self.onward(self.rings[0])

    def third(self):
        v = self.settle()
        y, rows, columns = v.shape
        v = v.reshape(y, 4, rows // 4, columns)
        ring = self.rings[1]
        own, first, far, second = quarters(self.place[ring], self.core)
        send = jnp.stack([pick(v, first, 1), pick(v, far, 1)]).astype(bf16)
        self.keep = (pick(v, own, 1), pick(v, second, 1))
        self.got = exchange(send, ring, (1, 3))
        line.hold(send, *self.keep)

    def fourth(self):
        self.onward(self.rings[1])

    def rows(self):
        v = self.settle()
        y, u, columns = v.shape
        v = v.reshape(y, u, columns // STEP, STEP).transpose(0, 2, 1, 3)
        return v.reshape(y, -1, STEP)


class Spread:
    def __init__(self, v, rings):
        self.rings = rings
        self.v = v
        self.got = exchange(v, rings[0], (1, 3))
        line.hold(v)

    def second(self, ring=None):
        pair = jnp.stack([self.v, line.later(self.got)])
        self.v = pair
        self.got = exchange(pair, ring or self.rings[0], (3, 1))
        line.hold(pair)

    def third(self):
        four = jnp.concatenate([self.v, line.later(self.got)])
        self.v = four
        self.got = exchange(four, self.rings[1], (1, 3))
        line.hold(four)

    def fourth(self):
        self.second(self.rings[1])

    def done(self):
        all_ = jnp.concatenate([self.v, line.later(self.got)])
        return all_, core_swap(all_)


class Finish:
    def __init__(self, parts, yl):
        v = jnp.concatenate(parts, axis=1)
        self.mine = pick(v, yl, 0)
        send = pick(v, 1 - yl, 0).astype(bf16)
        self.got = exchange(send, "y", (1, 3))
        line.hold(send, self.mine)

    def second(self):
        got = line.later(self.got)
        self.mine = (self.mine + got.astype(f32)).astype(bf16)
        self.far = lax.ppermute(self.mine, "yh", [(0, 1), (1, 0)])
        line.hold(self.mine)

    def done(self):
        far = line.later(self.far)
        return (self.mine.astype(f32) + far.astype(f32)).astype(bf16)


def per_device(
    tokens,
    memory,
    compressed,
    cotangent,
    ln1_g,
    ln1_b,
    w_q,
    w_kv,
    w_r,
    bias_u,
    bias_v,
    w_o,
    ln2_g,
    ln2_b,
    w_in,
    b_in,
    w_out,
    b_out,
    conv_w,
    conv_b,
):
    line.held = []
    tokens, memory, compressed, cotangent = tokens[0], memory[0], compressed[0], cotangent[0]
    yl, core = lax.axis_index("yl"), lax.axis_index("c")
    place = {"x": lax.axis_index("x"), "z": lax.axis_index("z")}
    none = jnp.zeros((1,), jnp.int32)
    ints = lambda *v: jnp.stack([jnp.asarray(i, jnp.int32) for i in v])

    def thirds(rows):
        half = rows // 2
        other = (1 - yl) * half
        return [yl * half, other + core * (half // 2), other + (1 - core) * (half // 2)]

    def both(v):
        return (v, core_swap(v))

    spot = (place["x"] * 4 + place["z"]) * 2 + core
    flat, piece = pack(
        (ln1_g, ln1_b, bias_u, bias_v, ln2_g, ln2_b, b_out, conv_b, b_in),
        w_in,
        w_out,
        conv_w,
        ints(spot),
    )
    piece_got = exchange(piece, "y", (1, 3))
    flat_got = exchange(flat, "y", (1, 3))

    kv_part, small = pack_rows(w_kv, w_q, w_r, w_o, ints(core))
    kv_got = exchange(kv_part, "y", (1, 3))
    small_got = exchange(small, "y", (1, 3))

    def joined(w, got, twin):
        return jnp.concatenate([w, got, twin], axis=0)

    spread = lax.all_gather(piece_got, ("x", "z", "c"), axis=0)
    thirds_d = ints(*thirds(D))
    thirds_c = ints(yl * (3 * D // 2), (1 - yl) * (3 * D // 2), *thirds(D))
    sinus_table = sinusoid(KEYS, D).astype(bf16)
    sinus_rel = jnp.concatenate(
        [
            lax.dynamic_slice_in_dim(sinus_table, thirds_d[i], width, 1)
            for i, width in enumerate(THIRDS)
        ],
        axis=1,
    )
    line.hold(sinus_rel)
    vectors, b_in = unpack(flat, flat_got, ints(yl))

    normed, normed_rel, oldest = first_norm(compressed, memory, tokens, vectors, thirds_d)
    both_normed, both_oldest, both_cot = both(normed), both(oldest), both(cotangent)
    kv_got = line.later(kv_got)
    kv_whole = joined(w_kv, kv_got, core_swap(kv_got))
    key_value = dot(normed_rel, kv_whole).astype(bf16)
    line.hold(key_value)
    small_got = line.later(small_got)
    small_twin = core_swap(small_got)
    q_whole, r_whole, o_whole = [
        joined(w, small_got[i], small_twin[i]) for i, w in enumerate((w_q, w_r, w_o))
    ]
    queries = dot(normed_rel[2 * T :], q_whole)
    relative = dot(sinus_rel, r_whole).astype(bf16)
    line.hold(queries, relative)
    probs, attended = attend(queries, key_value, relative, vectors, none)
    residual, normed2, normed2_rel = out_and_norm(attended, o_whole, tokens, vectors, thirds_d)
    both_n2, both_att = both(normed2), both(attended)

    cuts, rels, twins = [], [], []
    for ring in ("x", "z"):
        own, first, far, second = quarters(place[ring], core)
        cuts += [first, far, own, second]
        rels.append([own, first, second, far])
        twins.append([own, second, first, far])
    cuts = ints(core, *cuts)

    def flows(groups):
        pairs = weight_grads(groups, cuts)
        return [Flow(ring, pair, place, core) for (ring, _), pair in zip(groups, pairs)]

    hidden, d_pre, mixed_out, d_normed2, d_b_in = feed_forward(
        normed2_rel, residual, cotangent, w_in, w_out, spread, b_in, vectors, ints(yl)
    )
    both_hidden, both_pre = both(hidden), both(d_pre)
    d_residual, d_branch, d_attended, d_ln2_g, d_ln2_b, d_b_out = second_norm_back(
        cotangent, d_normed2, residual, vectors, o_whole, thirds_d
    )
    both_branch = both(d_branch)
    out_flow, in_flow = flows(
        [
            ("x", [(both_hidden, 0, T, both_cot, False)]),
            ("z", [(both_n2, 0, T, both_pre, False), (both_att, 0, T, both_branch, False)]),
        ]
    )

    compact, comp_normed = compress(oldest, conv_w, spread, vectors, thirds_c)
    comp_pair = dot(comp_normed, kv_whole).astype(bf16)
    loss, d_ck, d_cv = reconstruct(queries, key_value, comp_pair, none)
    recon_loss = jnp.sum(loss) / (T * D)
    compressed_next = jnp.concatenate([compressed[T // 3 :], compact], axis=0)
    d_compact, d_conv_b = compress_back(d_ck, d_cv, kv_whole, compact, vectors, thirds_d)
    both_compact = both(d_compact)
    out_flow.second()
    in_flow.second()
    d_kv, my_kv, give_kv, d_relative, d_queries, d_bias_u, d_bias_v = attend_back(
        queries, key_value, relative, vectors, probs, d_attended, ints(core)
    )
    both_kv = (my_kv, core_swap(give_kv))
    both_q, both_rel = both(d_queries), both(d_relative)
    (conv_flow,) = flows([("x", [(both_oldest, 0, T // 3, both_compact, False)])])
    out_flow.third()
    in_flow.third()
    d_tokens, d_ln1_g, d_ln1_b = first_norm_back(
        d_kv, d_queries, kv_whole, q_whole, compressed, memory, tokens, vectors, d_residual,
        thirds_d,
    )
    out_flow.fourth()
    in_flow.fourth()
    x_flow, z_flow = flows(
        [
            ("x", [(both_normed, 0, KEYS, both_kv, True)]),
            (
                "z",
                [
                    (both_normed, 2, T, both_q, False),
                    ((sinus_table, sinus_table), 0, KEYS, both_rel, False),
                ],
            ),
        ]
    )
    conv_flow.second()
    conv_flow.third()
    x_flow.second()
    z_flow.second()
    conv_flow.fourth()
    x_flow.third()
    z_flow.third()
    early = Finish([out_flow.rows(), in_flow.rows(), conv_flow.rows()], yl)
    x_flow.fourth()
    z_flow.fourth()
    early.second()

    total = jnp.concatenate(
        [d_ln1_g, d_ln1_b, d_bias_u, d_bias_v, d_ln2_g, d_ln2_b, d_b_out, d_conv_b]
        + [d_b_in]
    )
    total = jnp.concatenate(
        [total[:8].reshape(8, 2, STEP).transpose(1, 0, 2), total[8:].reshape(2, 4, STEP)], axis=1
    )
    late = Finish([x_flow.rows(), z_flow.rows(), total, jnp.zeros((2, 4, STEP), f32)], yl)
    early_done = early.done()
    line.hold(early_done)
    early_sums = lax.all_gather(early_done, ("c", "x", "z"), axis=0)
    late.second()
    late_done = late.done()
    kv_spread = Spread(late_done[:64], ("z", "x"))
    qr_spread = Spread(late_done[64:], ("x", "z"))
    kv_spread.second()
    qr_spread.second()
    kv_spread.third()
    qr_spread.third()
    kv_spread.fourth()
    qr_spread.fourth()
    (kv_own, kv_twin), (qr_own, qr_twin) = kv_spread.done(), qr_spread.done()
    x_places, z_places = rels
    x_twin, z_twin = twins
    along = ints(core, *x_places, *z_places, *x_twin, *z_twin)
    across = ints(core, *z_places, *x_places, *z_twin, *x_twin)
    g_kv = widen_near(kv_own, kv_twin, 0, 2 * D, False, along)
    g_q = widen_near(qr_own, qr_twin, 0, D, False, across)
    g_r = widen_near(qr_own, qr_twin, 32, D, False, across)
    g_out = widen(early_sums, 0, FF // 2, D, False, none)
    g_in = widen(early_sums, 128, D // 2, FF, True, none)
    g_o = widen(early_sums, 256, D // 2, D, True, none)
    g_conv = widen(early_sums, 288, 3 * D // 2, D, False, none)

    def four(v):
        return (v[0] + v[1]) + (v[2] + v[3])

    half = four(four(qr_own[:, :, 64:76].astype(f32))) + four(
        four(qr_twin[:, :, 64:76].astype(f32))
    )
    t_ln1_g, t_ln1_b, t_bu, t_bv, t_ln2_g, t_ln2_b, t_bout, t_convb = [half[i] for i in range(8)]
    t_bin = half[8:].reshape(-1)
    return (
        mixed_out[None],
        compressed_next[None],
        recon_loss[None],
        d_tokens[None],
        t_ln1_g,
        t_ln1_b,
        g_q,
        g_kv,
        g_r,
        t_bu,
        t_bv,
        g_o,
        t_ln2_g,
        t_ln2_b,
        g_in,
        t_bin,
        g_out,
        t_bout,
        g_conv,
        t_convb,
    )


def solution(mesh):
    fine = Mesh(mesh.devices.reshape(2, 4, 4, 2, 2), AXES)
    stream = P(AXES, None, None)
    vec, mat = P("yl"), P("yl", None)
    weights = (vec, vec, mat, mat, mat, vec, vec, mat, vec, vec, mat, vec, mat, vec, mat, vec)
    return jax.shard_map(
        per_device,
        mesh=fine,
        in_specs=(stream,) * 4 + weights,
        out_specs=(stream, stream, P(AXES), stream) + weights,
        check_vma=False,
    )
```

profile of v0, /device:TPU:1, one launch (start us, length us, event | category | flops | bytes accessed | tf_op | source)
XLA Modules:
  0.0 432.6 jit_solution(13467282678424794269)
XLA Ops:
  12.7 5.0 %collective-permute-done.5 = bf16[176,1024]{1,0:T(8,128)(2,1)S(1)} collective-permute-done((bf16[176,1024]{1,0:T(8,128)(2,1)}, bf16[176,1024]{1,0:T(8,128)(2,1)S(1)}, u32[]{:S(2)}, u32[]{:S(2)}) %collective-permute-start.5) | collective-permute-done | bytes 360480 | tf_op jit(solution)/shard_map/ppermute | solution.py:773
  25.2 12.5 %collective-permute-done.theirs = f32[16,512]{1,0:T(8,128)S(1)} collective-permute-done((f32[16,512]{1,0:T(8,128)S(1)}, f32[16,512]{1,0:T(8,128)S(1)}, u32[]{:S(2)}, u32[]{:S(2)}) %collective-permute-start) | collective-permute-done | bytes 32800 | tf_op jit(solution)/shard_map/ppermute | solution.py:773
  39.6 4.6 %shard_map.350 = (bf16[576,1024]{1,0:T(8,128)(2,1)}, bf16[576,1024]{1,0:T(8,128)(2,1)}, bf16[64,3072]{1,0:T(8,128)(2,1)}) custom-call(s32[3]{0:T(128)} %pad_add_fusion.s, f32[192,1024]{1,0:T(8,128)} %bitcast.256, f32[192,1024]{1,0:T(8,128)} %bitcast.273, bf16[192,1024]{1,0:T(8,128)(2,1)} %bitcast.266, f32[8,1024]{1,0:T(8,128)} %get-tuple-element.132.vec), custom_call_target="tpu_custom_call" | custom-call | tf_op jit(solution)/shard_map/pallas_call | solution.py:67
  48.9 3.9 convolution_convert_fusion.k.v
  52.7 12.7 %collective-permute-done.3 = bf16[3,256,1024]{2,1,0:T(8,128)(2,1)} collective-permute-done((bf16[3,256,1024]{2,1,0:T(8,128)(2,1)}, bf16[3,256,1024]{2,1,0:T(8,128)(2,1)}, u32[]{:S(2)}, u32[]{:S(2)}) %collective-permute-start.3) | collective-permute-done | bytes 1572896 | tf_op jit(solution)/shard_map/ppermute | solution.py:773
  65.9 4.7 %fusion.11 = (bf16[576,512]{1,0:T(8,128)(2,1)S(1)}, bf16[576,512]{1,0:T(8,128)(2,1)S(1)}) fusion(f32[512]{0:T(512)S(1)} %negate_power_fusion, f32[576]{0:T(1024)S(1)} %subtract_convert_fusion), kind=kLoop, calls=%fused_computation.32 | loop fusion | flops 884736 | bytes 1184000 | tf_op jit(solution)/shard_map/convert.31
  79.5 7.7 %shard_map.351 = (f32[8,192,640]{2,1,0:T(8,128)}, bf16[192,1024]{1,0:T(8,128)(2,1)}) custom-call(s32[1]{0:T(128)} %constant.96.clone.1._, f32[192,1024]{1,0:T(8,128)} %fusion.27.q, bf16[576,2048]{1,0:T(8,128)(2,1)} %convolution_convert_fusion.k.v, bf16[576,2048]{1,0:T(8,128)(2,1)} %convolution_convert_fusion.k.v, bf16[576,1024]{1,0:T(8,128)(2,1)} %fusion.6.rel, ...), custom_call_target="tpu_custom_call" | custom-call | tf_op jit(solution)/shard_map/pallas_call | solution.py:67
  88.7 4.1 shard_map.352
  92.9 18.1 %shard_map.353 = (bf16[192,4096]{1,0:T(8,128)(2,1)}, bf16[192,4096]{1,0:T(8,128)(2,1)}, bf16[192,1024]{1,0:T(8,128)(2,1)}, f32[192,1024]{1,0:T(8,128)}, f32[4,1024]{1,0:T(4,128)}) custom-call(s32[1]{0:T(128)} %bitcast.s, bf16[192,1024]{1,0:T(8,128)(2,1)} %get-tuple-element.145.n2, f32[192,1024]{1,0:T(8,128)} %get-tuple-element.143.res, ...), custom_call_target="tpu_custom_call" | custom-call | tf_op jit(solution)/shard_map/pallas_call | solution.py:67
  112.7 5.0 %shard_map.354 = (f32[192,1024]{1,0:T(8,128)}, bf16[192,1024]{1,0:T(8,128)(2,1)}, bf16[192,1024]{1,0:T(8,128)(2,1)}, f32[1,1024]{1,0:T(1,128)}, f32[1,1024]{1,0:T(1,128)}, /*index=5*/f32[1,1024]{1,0:T(1,128)}) custom-call(s32[3]{0:T(128)} %pad_add_fusion.s, bf16[192,1024]{1,0:T(8,128)(2,1)} %bitcast.263, f32[192,1024]{1,0:T(8,128)} %get-tuple-element.151.dn, ...), custom_call_target="tpu_custom_call" | custom-call | tf_op jit(solution)/shard_map/pallas_call | solution.py:67
  121.1 11.5 %shard_map.355 = (bf16[2,2,512,512]{3,2,1,0:T(8,128)(2,1)}, bf16[2,2,512,512]{3,2,1,0:T(8,128)(2,1)}, bf16[2,2,128,2560]{3,2,1,0:T(8,128)(2,1)}, bf16[2,2,128,2560]{3,2,1,0:T(8,128)(2,1)}) custom-call(s32[9]{0:T(128)} %stack.217.s, bf16[192,4096]{1,0:T(8,128)(2,1)} %get-tuple-element.149.refs_0_.refs_1_, ...), custom_call_target="tpu_custom_call" | custom-call | tf_op jit(solution)/shard_map/pallas_call | solution.py:67
  132.6 3.9 collective-permute-start.13
  139.6 6.5 %shard_map.356 = (f32[64,1024]{1,0:T(8,128)}, bf16[64,1024]{1,0:T(8,128)(2,1)}) custom-call(s32[5]{0:T(128)} %stack.208.s, bf16[64,3072]{1,0:T(8,128)(2,1)} %get-tuple-element.159.x.refs_0_.refs_1_, bf16[1536,1024]{1,0:T(8,128)(2,1)} %own.1, bf16[32,176,1024]{2,1,0:T(8,128)(2,1)} %bitcast.246, bf16[32,176,1024]{2,1,0:T(8,128)(2,1)} %bitcast.247, ...), custom_call_target="tpu_custom_call" | custom-call | tf_op jit(solution)/shard_map/pallas_call | solution.py:67
  148.5 8.4 %shard_map.357 = (f32[1,128]{1,0:T(1,128)}, bf16[64,1024]{1,0:T(8,128)(2,1)}, bf16[64,1024]{1,0:T(8,128)(2,1)}) custom-call(s32[1]{0:T(128)} %constant.96.clone.1._, f32[192,1024]{1,0:T(8,128)} %fusion.27.q, bf16[576,2048]{1,0:T(8,128)(2,1)} %convolution_convert_fusion.k.v, bf16[576,2048]{1,0:T(8,128)(2,1)} %convolution_convert_fusion.k.v, ...), custom_call_target="tpu_custom_call" | custom-call | tf_op jit(solution)/shard_map/pallas_call | solution.py:67
  157.0 5.4 %shard_map.358 = (bf16[64,1024]{1,0:T(8,128)(2,1)}, f32[1,1024]{1,0:T(1,128)}) custom-call(s32[3]{0:T(128)} %pad_add_fusion.s, bf16[64,1024]{1,0:T(8,128)(2,1)} %get-tuple-element.165.dck, bf16[64,1024]{1,0:T(8,128)(2,1)} %get-tuple-element.166.dcv, bf16[1024,2048]{1,0:T(8,128)(2,1)} %copy-done, f32[64,1024]{1,0:T(8,128)} %get-tuple-element.160.compact, ...), custom_call_target="tpu_custom_call" | custom-call | tf_op jit(solution)/shard_map/pallas_call | solution.py:67
  173.3 11.4 %shard_map.359 = (bf16[2,576,1024]{2,1,0:T(8,128)(2,1)}, bf16[576,1024]{1,0:T(8,128)(2,1)}, bf16[576,1024]{1,0:T(8,128)(2,1)}, bf16[576,1024]{1,0:T(8,128)(2,1)}...) custom-call(s32[1]{0:T(128)} %bitcast.4._.s, f32[192,1024]{1,0:T(8,128)} %fusion.27.q, ...), custom_call_target="tpu_custom_call" | custom-call | tf_op jit(solution)/shard_map/pallas_call | solution.py:67
  185.5 5.4 %shard_map.360 = (bf16[2,2,384,512]{3,2,1,0:T(8,128)(2,1)}, bf16[2,2,384,512]{3,2,1,0:T(8,128)(2,1)}) custom-call(s32[9]{0:T(128)} %stack.217.s, bf16[64,3072]{1,0:T(8,128)(2,1)} %get-tuple-element.159.x.refs_0_.refs_1_, bf16[64,3072]{1,0:T(8,128)(2,1)} %get-tuple-element.159.x.refs_0_.refs_1_, bf16[64,3072]{1,0:T(8,128)(2,1)} %collective-permute-done.14.refs_2_.refs_3_, ...), custom_call_target="tpu_custom_call" | custom-call | tf_op jit(solution)/shard_map/pallas_call | solution.py:67
  206.1 10.8 %shard_map.361 = (f32[192,1024]{1,0:T(8,128)}, f32[1,1024]{1,0:T(1,128)}, f32[1,1024]{1,0:T(1,128)}) custom-call(s32[3]{0:T(128)} %pad_add_fusion.s, bf16[2,576,1024]{2,1,0:T(8,128)(2,1)} %get-tuple-element.175.dkv, bf16[192,1024]{1,0:T(8,128)(2,1)} %get-tuple-element.181.dq.refs_10_, bf16[1024,2048]{1,0:T(8,128)(2,1)} %copy-done, ...), custom_call_target="tpu_custom_call" | custom-call | tf_op jit(solution)/shard_map/pallas_call | solution.py:67
  222.0 10.9 %shard_map.362 = (bf16[2,2,128,1024]{3,2,1,0:T(8,128)(2,1)}, bf16[2,2,128,1024]{3,2,1,0:T(8,128)(2,1)}, bf16[2,2,128,1024]{3,2,1,0:T(8,128)(2,1)}, bf16[2,2,128,1024]{3,2,1,0:T(8,128)(2,1)}) custom-call(s32[9]{0:T(128)} %stack.217.s, bf16[576,1024]{1,0:T(8,128)(2,1)} %get-tuple-element.134.refs_0_.refs_1_.refs_6_.refs_7_, ...), custom_call_target="tpu_custom_call" | custom-call | tf_op jit(solution)/shard_map/pallas_call | solution.py:67
  237.6 12.9 %collective-permute-done.26 = bf16[2,384,512]{2,1,0:T(8,128)(2,1)S(1)} collective-permute-done((bf16[2,384,512]{2,1,0:T(8,128)(2,1)S(1)}, bf16[2,384,512]{2,1,0:T(8,128)(2,1)S(1)}, u32[]{:S(2)}, u32[]{:S(2)}) %collective-permute-start.26) | collective-permute-done | bytes 786464 | tf_op jit(solution)/shard_map/ppermute | solution.py:773
  254.0 4.8 %collective-permute-done.24 = bf16[2,2,128,1024]{3,2,1,0:T(8,128)(2,1)S(1)} collective-permute-done((bf16[2,2,128,1024]{3,2,1,0:T(8,128)(2,1)S(1)}, bf16[2,2,128,1024]{3,2,1,0:T(8,128)(2,1)S(1)}, u32[]{:S(2)}, u32[]{:S(2)}) %collective-permute-start.24) | collective-permute-done | bytes 1048608 | tf_op jit(solution)/shard_map/ppermute | solution.py:773
  270.9 4.0 collective-permute-done.31
  298.3 4.3 collective-permute-done.40
  310.5 6.7 %collective-permute-done.41 = bf16[144,512]{1,0:T(8,128)(2,1)S(1)} collective-permute-done((bf16[144,512]{1,0:T(8,128)(2,1)S(1)}, bf16[144,512]{1,0:T(8,128)(2,1)S(1)}, u32[]{:S(2)}, u32[]{:S(2)}) %collective-permute-start.41) | collective-permute-done | bytes 147488 | tf_op jit(solution)/shard_map/ppermute | solution.py:866
  323.6 4.8 %collective-permute-done.45 = bf16[2,64,512]{2,1,0:T(8,128)(2,1)S(1)} collective-permute-done((bf16[2,64,512]{2,1,0:T(8,128)(2,1)S(1)}, bf16[2,64,512]{2,1,0:T(8,128)(2,1)S(1)}, u32[]{:S(2)}, u32[]{:S(2)}) %collective-permute-start.45) | collective-permute-done | bytes 131104 | tf_op jit(solution)/shard_map/ppermute | solution.py:773
  333.0 6.2 %collective-permute-done.47 = bf16[4,64,512]{2,1,0:T(8,128)(2,1)S(1)} collective-permute-done((bf16[4,64,512]{2,1,0:T(8,128)(2,1)S(1)}, bf16[4,64,512]{2,1,0:T(8,128)(2,1)S(1)}, u32[]{:S(2)}, u32[]{:S(2)}) %collective-permute-start.47) | collective-permute-done | bytes 262176 | tf_op jit(solution)/shard_map/ppermute | solution.py:773
  340.9 18.9 %collective-permute-done.48 = bf16[2,4,80,512]{3,2,1,0:T(8,128)(2,1)S(1)} collective-permute-done((bf16[2,4,80,512]{3,2,1,0:T(8,128)(2,1)S(1)}, bf16[2,4,80,512]{3,2,1,0:T(8,128)(2,1)S(1)}, u32[]{:S(2)}, u32[]{:S(2)}) %collective-permute-start.48) | collective-permute-done | bytes 655392 | tf_op jit(solution)/shard_map/ppermute | solution.py:773
  360.0 21.3 %collective-permute-start.49 = (bf16[4,4,80,512]{3,2,1,0:T(8,128)(2,1)S(1)}, bf16[4,4,80,512]{3,2,1,0:T(8,128)(2,1)S(1)}, u32[]{:S(2)}, u32[]{:S(2)}) collective-permute-start(bf16[4,4,80,512]{3,2,1,0:T(8,128)(2,1)S(1)} %pad_maximum_fusion.4.own), channel_id=1, source_target_pairs={{0,2},{2,0},{1,3},{3,1},{4,6},{6,4},{5,7},{7,5},{8,10},{10,8},{9,1... | collective-permute-start | bytes 3932168 | tf_op jit(solution)/shard_map/ppermute | solution.py:761
  388.1 4.4 %shard_map.363 = f32[16,32,2048]{2,1,0:T(8,128)} custom-call(s32[17]{0:T(128)} %stack.246.s, bf16[4,4,64,512]{3,2,1,0:T(8,128)(2,1)} %pad_maximum_fusion.6.own, bf16[4,4,64,512]{3,2,1,0:T(8,128)(2,1)} %collective-permute-done.51.twin), custom_call_target="tpu_custom_call" | custom-call | tf_op jit(solution)/shard_map/pallas_call | solution.py:67
  403.5 7.3 %shard_map.366 = f32[16,128,1024]{2,1,0:T(8,128)} custom-call(s32[1]{0:T(128)} %constant.96.clone.1._, bf16[32,384,512]{2,1,0:T(8,128)(2,1)} %bitcast.237), custom_call_target="tpu_custom_call" | custom-call | tf_op jit(solution)/shard_map/pallas_call | solution.py:67
  410.8 5.2 %shard_map.367 = f32[16,32,4096]{2,1,0:T(8,128)} custom-call(s32[1]{0:T(128)} %constant.96.clone.1._, bf16[32,384,512]{2,1,0:T(8,128)(2,1)} %bitcast.238, bf16[32,384,512]{2,1,0:T(8,128)(2,1)} %bitcast.239, bf16[32,384,512]{2,1,0:T(8,128)(2,1)} %bitcast.240, bf16[32,384,512]{2,1,0:T(8,128)(2,1)} %bitcast.241), custom_call_target="tpu_custom_call" | custom-call | tf_op jit(solution)/shard_map/pallas_call | solution.py:67
  418.4 5.8 %shard_map.369 = f32[16,96,1024]{2,1,0:T(8,128)} custom-call(s32[1]{0:T(128)} %constant.96.clone.1._, bf16[32,384,512]{2,1,0:T(8,128)(2,1)} %bitcast.243), custom_call_target="tpu_custom_call" | custom-call | tf_op jit(solution)/shard_map/pallas_call | solution.py:67
  (302 shorter events, 156.3 us)
Async XLA Ops:
  7.2 85.7 %all-gather.5.cloned.1.call-start = ((), (), s32[]{:S(2)}) async-start(), calls=%async_computation | async-start | bytes 11894784 | tf_op jit(solution)/shard_map/all_gather | solution.py:929
  18.5 385.0 %all-gather.7.cloned.1.call-start = ((), (), s32[]{:S(2)}) async-start(), calls=%async_computation.1 | async-start | bytes 12976128 | tf_op jit(solution)/shard_map/all_gather | solution.py:1045
  21.8 22.4 %collective-permute-start.1 = (bf16[256,2048]{1,0:T(8,128)(2,1)}, bf16[256,2048]{1,0:T(8,128)(2,1)S(1)}, u32[]{:S(2)}, u32[]{:S(2)}) collective-permute-start(bf16[256,2048]{1,0:T(8,128)(2,1)} %get-tuple-element.130), channel_id=1, source_target_pairs={{0,1},{2,67},{1,0},{3,66},{64,65},{66,3},{65,64},{67,2},{4,5},{6,7... | collective-permute-start | bytes 3145736 | tf_op jit(solution)/shard_map/ppermute | solution.py:773
  24.5 13.1 %collective-permute-start = (f32[16,512]{1,0:T(8,128)S(1)}, f32[16,512]{1,0:T(8,128)S(1)}, u32[]{:S(2)}, u32[]{:S(2)}) collective-permute-start(f32[16,512]{1,0:T(8,128)S(1)} %copy-done.39), channel_id=1, source_target_pairs={{0,1},{2,67},{1,0},{3,66},{64,65},{66,3},{65,64},{67,2},{4,5},{6,7... | collective-permute-start | bytes 98312 | tf_op jit(solution)/shard_map/ppermute | solution.py:773
  44.2 21.2 %collective-permute-start.3 = (bf16[3,256,1024]{2,1,0:T(8,128)(2,1)}, bf16[3,256,1024]{2,1,0:T(8,128)(2,1)}, u32[]{:S(2)}, u32[]{:S(2)}) collective-permute-start(bf16[3,256,1024]{2,1,0:T(8,128)(2,1)} %get-tuple-element.137), channel_id=1, source_target_pairs={{0,1},{2,67},{1,0},{3,66},{64,65},{66,3},{65,64},{67,2},{4,5},{6,7... | collective-permute-start | bytes 4718600 | tf_op jit(solution)/shard_map/ppermute | solution.py:773
  111.0 9.4 %collective-permute-start.6 = (bf16[192,4096]{1,0:T(8,128)(2,1)}, bf16[192,4096]{1,0:T(8,128)(2,1)}, u32[]{:S(2)}, u32[]{:S(2)}) collective-permute-start(bf16[192,4096]{1,0:T(8,128)(2,1)} %get-tuple-element.149.refs_0_.refs_1_), channel_id=1, source_target_pairs={{0,2},{2,0},{1,3},{3,1},{4,6},{6,4},{5,7},{7,5},{8,10},{10,8},{9,1... | collective-permute-start | bytes 4718600 | tf_op jit(solution)/shard_map/ppermute | solution.py:761
  132.6 33.2 %collective-permute-start.13 = (bf16[2,2,128,2560]{3,2,1,0:T(8,128)(2,1)}, bf16[2,2,128,2560]{3,2,1,0:T(8,128)(2,1)}, u32[]{:S(2)}, u32[]{:S(2)}) collective-permute-start(bf16[2,2,128,2560]{3,2,1,0:T(8,128)(2,1)} %get-tuple-element.171), channel_id=1, source_target_pairs={{0,4},{2,14},{4,0},{6,10},{8,12},{10,6},{12,8},{14,2},{1,5},{3,15}... | collective-permute-start | bytes 7864328 | tf_op jit(solution)/shard_map/ppermute | solution.py:773
  136.5 26.4 %collective-permute-start.12 = (bf16[2,2,512,512]{3,2,1,0:T(8,128)(2,1)}, bf16[2,2,512,512]{3,2,1,0:T(8,128)(2,1)}, u32[]{:S(2)}, u32[]{:S(2)}) collective-permute-start(bf16[2,2,512,512]{3,2,1,0:T(8,128)(2,1)} %get-tuple-element.157), channel_id=1, source_target_pairs={{0,16},{2,50},{16,0},{18,34},{32,48},{34,18},{48,32},{50,2},{1,17}... | collective-permute-start | bytes 6291464 | tf_op jit(solution)/shard_map/ppermute | solution.py:773
  165.7 27.6 %collective-permute-start.16 = (bf16[2,512,512]{2,1,0:T(8,128)(2,1)}, bf16[2,512,512]{2,1,0:T(8,128)(2,1)}, u32[]{:S(2)}, u32[]{:S(2)}) collective-permute-start(bf16[2,512,512]{2,1,0:T(8,128)(2,1)} %fusion.12), channel_id=1, source_target_pairs={{0,48},{2,18},{16,32},{18,2},{32,16},{34,50},{48,0},{50,34},{1,49}... | collective-permute-start | bytes 3145736 | tf_op jit(solution)/shard_map/ppermute | solution.py:773
  168.6 28.4 %collective-permute-start.17 = (bf16[2,128,2560]{2,1,0:T(8,128)(2,1)}, bf16[2,128,2560]{2,1,0:T(8,128)(2,1)}, u32[]{:S(2)}, u32[]{:S(2)}) collective-permute-start(bf16[2,128,2560]{2,1,0:T(8,128)(2,1)} %fusion.9), channel_id=1, source_target_pairs={{0,12},{2,6},{4,8},{6,2},{8,4},{10,14},{12,0},{14,10},{1,13},{3,7}... | collective-permute-start | bytes 3932168 | tf_op jit(solution)/shard_map/ppermute | solution.py:773
  168.6 16.2 %collective-permute-start.14 = (bf16[64,3072]{1,0:T(8,128)(2,1)}, bf16[64,3072]{1,0:T(8,128)(2,1)}, u32[]{:S(2)}, u32[]{:S(2)}) collective-permute-start(bf16[64,3072]{1,0:T(8,128)(2,1)} %get-tuple-element.159.x.refs_0_.refs_1_), channel_id=1, source_target_pairs={{0,2},{2,0},{1,3},{3,1},{4,6},{6,4},{5,7},{7,5},{8,10},{10,8},{9,1... | collective-permute-start | bytes 1179656 | tf_op jit(solution)/shard_map/ppermute | solution.py:761
  171.6 13.2 %collective-permute-start.15 = (bf16[64,1024]{1,0:T(8,128)(2,1)S(1)}, bf16[64,1024]{1,0:T(8,128)(2,1)S(1)}, u32[]{:S(2)}, u32[]{:S(2)}) collective-permute-start(bf16[64,1024]{1,0:T(8,128)(2,1)S(1)} %copy-done.37), channel_id=1, source_target_pairs={{0,2},{2,0},{1,3},{3,1},{4,6},{6,4},{5,7},{7,5},{8,10},{10,8},{9,1... | collective-permute-start | bytes 393224 | tf_op jit(solution)/shard_map/ppermute | solution.py:761
  172.8 47.6 %collective-permute-start.20 = (bf16[576,1024]{1,0:T(8,128)(2,1)S(1)}, bf16[576,1024]{1,0:T(8,128)(2,1)S(1)}, u32[]{:S(2)}, u32[]{:S(2)}) collective-permute-start(bf16[576,1024]{1,0:T(8,128)(2,1)S(1)} %copy-done.2), channel_id=1, source_target_pairs={{0,2},{2,0},{1,3},{3,1},{4,6},{6,4},{5,7},{7,5},{8,10},{10,8},{9,1... | collective-permute-start | bytes 3538952 | tf_op jit(solution)/shard_map/ppermute | solution.py:761
  190.9 42.1 %collective-permute-start.25 = (bf16[2,2,384,512]{3,2,1,0:T(8,128)(2,1)}, bf16[2,2,384,512]{3,2,1,0:T(8,128)(2,1)}, u32[]{:S(2)}, u32[]{:S(2)}) collective-permute-start(bf16[2,2,384,512]{3,2,1,0:T(8,128)(2,1)} %get-tuple-element.177), channel_id=1, source_target_pairs={{0,16},{2,50},{16,0},{18,34},{32,48},{34,18},{48,32},{50,2},{1,17}... | collective-permute-start | bytes 4718600 | tf_op jit(solution)/shard_map/ppermute | solution.py:773
  195.8 9.5 %collective-permute-start.18 = (bf16[2,2,128,512]{3,2,1,0:T(8,128)(2,1)S(1)}, bf16[2,2,128,512]{3,2,1,0:T(8,128)(2,1)S(1)}, u32[]{:S(2)}, u32[]{:S(2)}) collective-permute-start(bf16[2,2,128,512]{3,2,1,0:T(8,128)(2,1)S(1)} %pad_maximum_fusion.9), channel_id=1, source_target_pairs={{0,4},{2,14},{4,0},{6,10},{8,12},{10,6},{12,8},{14,2},{1,5},{3,15}... | collective-permute-start | bytes 1572872 | tf_op jit(solution)/shard_map/ppermute | solution.py:773
  200.7 18.0 %collective-permute-start.19 = (bf16[2,2,32,2560]{3,2,1,0:T(8,128)(2,1)}, bf16[2,2,32,2560]{3,2,1,0:T(8,128)(2,1)}, u32[]{:S(2)}, u32[]{:S(2)}) collective-permute-start(bf16[2,2,32,2560]{3,2,1,0:T(8,128)(2,1)} %pad_maximum_fusion.7), channel_id=1, source_target_pairs={{0,16},{2,50},{16,0},{18,34},{32,48},{34,18},{48,32},{50,2},{1,17}... | collective-permute-start | bytes 1966088 | tf_op jit(solution)/shard_map/ppermute | solution.py:773
  202.7 17.8 %collective-permute-start.21 = (bf16[576,1024]{1,0:T(8,128)(2,1)}, bf16[576,1024]{1,0:T(8,128)(2,1)S(1)}, u32[]{:S(2)}, u32[]{:S(2)}) collective-permute-start(bf16[576,1024]{1,0:T(8,128)(2,1)} %get-tuple-element.187), channel_id=1, source_target_pairs={{0,2},{2,0},{1,3},{3,1},{4,6},{6,4},{5,7},{7,5},{8,10},{10,8},{9,1... | collective-permute-start | bytes 3538952 | tf_op jit(solution)/shard_map/ppermute | solution.py:761
  205.3 15.2 %collective-permute-start.23 = (bf16[576,1024]{1,0:T(8,128)(2,1)}, bf16[576,1024]{1,0:T(8,128)(2,1)}, u32[]{:S(2)}, u32[]{:S(2)}) collective-permute-start(bf16[576,1024]{1,0:T(8,128)(2,1)} %get-tuple-element.188.refs_16_), channel_id=1, source_target_pairs={{0,2},{2,0},{1,3},{3,1},{4,6},{6,4},{5,7},{7,5},{8,10},{10,8},{9,1... | collective-permute-start | bytes 3538952 | tf_op jit(solution)/shard_map/ppermute | solution.py:761
  234.4 16.1 %collective-permute-start.26 = (bf16[2,384,512]{2,1,0:T(8,128)(2,1)S(1)}, bf16[2,384,512]{2,1,0:T(8,128)(2,1)S(1)}, u32[]{:S(2)}, u32[]{:S(2)}) collective-permute-start(bf16[2,384,512]{2,1,0:T(8,128)(2,1)S(1)} %fusion.13), channel_id=1, source_target_pairs={{0,48},{2,18},{16,32},{18,2},{32,16},{34,50},{48,0},{50,34},{1,49}... | collective-permute-start | bytes 2359304 | tf_op jit(solution)/shard_map/ppermute | solution.py:773
  235.5 23.2 %collective-permute-start.24 = (bf16[2,2,128,1024]{3,2,1,0:T(8,128)(2,1)S(1)}, bf16[2,2,128,1024]{3,2,1,0:T(8,128)(2,1)S(1)}, u32[]{:S(2)}, u32[]{:S(2)}) collective-permute-start(bf16[2,2,128,1024]{3,2,1,0:T(8,128)(2,1)S(1)} %copy-done.51), channel_id=1, source_target_pairs={{0,16},{2,50},{16,0},{18,34},{32,48},{34,18},{48,32},{50,2},{1,17}... | collective-permute-start | bytes 3145736 | tf_op jit(solution)/shard_map/ppermute | solution.py:773
  237.4 24.8 %collective-permute-start.28 = (bf16[2,2,128,1024]{3,2,1,0:T(8,128)(2,1)}, bf16[2,2,128,1024]{3,2,1,0:T(8,128)(2,1)}, u32[]{:S(2)}, u32[]{:S(2)}) collective-permute-start(bf16[2,2,128,1024]{3,2,1,0:T(8,128)(2,1)} %get-tuple-element.196), channel_id=1, source_target_pairs={{0,4},{2,14},{4,0},{6,10},{8,12},{10,6},{12,8},{14,2},{1,5},{3,15}... | collective-permute-start | bytes 3145736 | tf_op jit(solution)/shard_map/ppermute | solution.py:773
  252.9 12.1 %collective-permute-start.29 = (bf16[2,2,96,512]{3,2,1,0:T(8,128)(2,1)}, bf16[2,2,96,512]{3,2,1,0:T(8,128)(2,1)}, u32[]{:S(2)}, u32[]{:S(2)}) collective-permute-start(bf16[2,2,96,512]{3,2,1,0:T(8,128)(2,1)} %pad_maximum_fusion.11), channel_id=1, source_target_pairs={{0,4},{2,14},{4,0},{6,10},{8,12},{10,6},{12,8},{14,2},{1,5},{3,15}... | collective-permute-start | bytes 1179656 | tf_op jit(solution)/shard_map/ppermute | solution.py:773
  259.9 23.5 %collective-permute-start.32 = (bf16[2,128,512]{2,1,0:T(8,128)(2,1)}, bf16[2,128,512]{2,1,0:T(8,128)(2,1)}, u32[]{:S(2)}, u32[]{:S(2)}) collective-permute-start(bf16[2,128,512]{2,1,0:T(8,128)(2,1)} %fusion.23), channel_id=1, source_target_pairs={{0,12},{2,6},{4,8},{6,2},{8,4},{10,14},{12,0},{14,10},{1,13},{3,7}... | collective-permute-start | bytes 786440 | tf_op jit(solution)/shard_map/ppermute | solution.py:773
  260.7 19.7 %collective-permute-start.33 = (bf16[2,32,2560]{2,1,0:T(8,128)(2,1)}, bf16[2,32,2560]{2,1,0:T(8,128)(2,1)S(1)}, u32[]{:S(2)}, u32[]{:S(2)}) collective-permute-start(bf16[2,32,2560]{2,1,0:T(8,128)(2,1)} %fusion.17), channel_id=1, source_target_pairs={{0,48},{2,18},{16,32},{18,2},{32,16},{34,50},{48,0},{50,34},{1,49}... | collective-permute-start | bytes 983048 | tf_op jit(solution)/shard_map/ppermute | solution.py:773
  263.4 11.5 %collective-permute-start.31 = (bf16[2,128,1024]{2,1,0:T(8,128)(2,1)S(1)}, bf16[2,128,1024]{2,1,0:T(8,128)(2,1)S(1)}, u32[]{:S(2)}, u32[]{:S(2)}) collective-permute-start(bf16[2,128,1024]{2,1,0:T(8,128)(2,1)S(1)} %fusion.21), channel_id=1, source_target_pairs={{0,12},{2,6},{4,8},{6,2},{8,4},{10,14},{12,0},{14,10},{1,13},{3,7}... | collective-permute-start | bytes 1572872 | tf_op jit(solution)/shard_map/ppermute | solution.py:773
  265.9 15.6 %collective-permute-start.34 = (bf16[2,96,512]{2,1,0:T(8,128)(2,1)S(1)}, bf16[2,96,512]{2,1,0:T(8,128)(2,1)}, u32[]{:S(2)}, u32[]{:S(2)}) collective-permute-start(bf16[2,96,512]{2,1,0:T(8,128)(2,1)S(1)} %fusion.26), channel_id=1, source_target_pairs={{0,12},{2,6},{4,8},{6,2},{8,4},{10,14},{12,0},{14,10},{1,13},{3,7}... | collective-permute-start | bytes 589832 | tf_op jit(solution)/shard_map/ppermute | solution.py:773
  270.6 16.7 %collective-permute-start.30 = (bf16[2,2,32,1024]{3,2,1,0:T(8,128)(2,1)}, bf16[2,2,32,1024]{3,2,1,0:T(8,128)(2,1)}, u32[]{:S(2)}, u32[]{:S(2)}) collective-permute-start(bf16[2,2,32,1024]{3,2,1,0:T(8,128)(2,1)} %pad_maximum_fusion.13), channel_id=1, source_target_pairs={{0,4},{2,14},{4,0},{6,10},{8,12},{10,6},{12,8},{14,2},{1,5},{3,15}... | collective-permute-start | bytes 786440 | tf_op jit(solution)/shard_map/ppermute | solution.py:773
  277.0 11.3 %collective-permute-start.36 = (bf16[2,2,32,1024]{3,2,1,0:T(8,128)(2,1)}, bf16[2,2,32,1024]{3,2,1,0:T(8,128)(2,1)}, u32[]{:S(2)}, u32[]{:S(2)}) collective-permute-start(bf16[2,2,32,1024]{3,2,1,0:T(8,128)(2,1)} %pad_maximum_fusion.14), channel_id=1, source_target_pairs={{0,16},{2,50},{16,0},{18,34},{32,48},{34,18},{48,32},{50,2},{1,17}... | collective-permute-start | bytes 786440 | tf_op jit(solution)/shard_map/ppermute | solution.py:773
  328.5 10.7 %collective-permute-start.47 = (bf16[4,64,512]{2,1,0:T(8,128)(2,1)S(1)}, bf16[4,64,512]{2,1,0:T(8,128)(2,1)S(1)}, u32[]{:S(2)}, u32[]{:S(2)}) collective-permute-start(bf16[4,64,512]{2,1,0:T(8,128)(2,1)S(1)} %get-tuple-element.267), channel_id=1, source_target_pairs={{0,16},{2,50},{16,0},{18,34},{32,48},{34,18},{48,32},{50,2},{1,17}... | collective-permute-start | bytes 786440 | tf_op jit(solution)/shard_map/ppermute | solution.py:773
  339.6 20.3 %collective-permute-start.48 = (bf16[2,4,80,512]{3,2,1,0:T(8,128)(2,1)S(1)}, bf16[2,4,80,512]{3,2,1,0:T(8,128)(2,1)S(1)}, u32[]{:S(2)}, u32[]{:S(2)}) collective-permute-start(bf16[2,4,80,512]{3,2,1,0:T(8,128)(2,1)S(1)} %pad_maximum_fusion.8), channel_id=1, source_target_pairs={{0,12},{2,6},{4,8},{6,2},{8,4},{10,14},{12,0},{14,10},{1,13},{3,7}... | collective-permute-start | bytes 1966088 | tf_op jit(solution)/shard_map/ppermute | solution.py:773
  340.1 41.2 %collective-permute-start.50 = (bf16[2,4,64,512]{3,2,1,0:T(8,128)(2,1)S(1)}, bf16[2,4,64,512]{3,2,1,0:T(8,128)(2,1)S(1)}, u32[]{:S(2)}, u32[]{:S(2)}) collective-permute-start(bf16[2,4,64,512]{3,2,1,0:T(8,128)(2,1)S(1)} %pad_maximum_fusion.10), channel_id=1, source_target_pairs={{0,48},{2,18},{16,32},{18,2},{32,16},{34,50},{48,0},{50,34},{1,49}... | collective-permute-start | bytes 1572872 | tf_op jit(solution)/shard_map/ppermute | solution.py:773
  360.0 32.5 %collective-permute-start.49 = (bf16[4,4,80,512]{3,2,1,0:T(8,128)(2,1)S(1)}, bf16[4,4,80,512]{3,2,1,0:T(8,128)(2,1)S(1)}, u32[]{:S(2)}, u32[]{:S(2)}) collective-permute-start(bf16[4,4,80,512]{3,2,1,0:T(8,128)(2,1)S(1)} %pad_maximum_fusion.4.own), channel_id=1, source_target_pairs={{0,2},{2,0},{1,3},{3,1},{4,6},{6,4},{5,7},{7,5},{8,10},{10,8},{9,1... | collective-permute-start | bytes 3932168 | tf_op jit(solution)/shard_map/ppermute | solution.py:761
  (75 other events, 534.9 us)
Sparse Core Ops, SparseCore 0:
  18.6 63.1 all-gather.4
  304.6 80.7 all-gather.6
where the time goes:
time: 438 us; the launch traced here: 433 us
  Pallas kernels  149 us (34%)
  waiting for transfers between devices  111 us (25%)
  starting transfers between devices  71 us (16%)
  other arithmetic  50.4 us (12%)
  local copies, waits for them, and re-layouts  22.5 us (5%)
  between operations  17.3 us (4%)
  matrix products  11.3 us (3%)
    pallas_call x23, Pallas kernels, run_kernel(): pl.pallas_call(kernel, out_shape=out, grid_spec=pltpu.PrefetchScalarGridS...  149 us
    ppermute x34, waiting for transfers between devices, exchange(): return lax.ppermute(v, RING[ring], pairs)  98.8 us
    ppermute x34, starting transfers between devices, exchange(): return lax.ppermute(v, RING[ring], pairs)  42 us
    ppermute x16, starting transfers between devices, core_swap(): return lax.ppermute(v, 'c', [(0, 1), (1, 0)])  27.4 us
    convert_element_type x10, other arithmetic, onward(): value = (self.keep[1].astype(f32) + got[1].astype(f32)).astype(bf16)  15.4 us
    add x10, other arithmetic, settle(): return self.keep[0].astype(f32) + self.near.astype(f32) + last.astype(f32)  13.6 us
    dot_general x4, matrix products, dot(): return jnp.dot(a, b, preferred_element_type=f32)  11.3 us
    ppermute x2, waiting for transfers between devices, second(): self.far = lax.ppermute(self.mine, 'yh', [(0, 1), (1, 0)])  10.9 us
  transfers between devices with their start and end apart: 54, of which 23 were waited for; matrix products, arithmetic and copies ran while one was open for 17% of the time, Pallas kernels for 22%

commit v1 on v0

--- a/solution.py
+++ b/solution.py
@@ -48,34 +48,30 @@
     def later(self, value):
         return lax.optimization_barrier((value, *self.held))[0] if self.held else value
 
-    def ran(self, value):
-        self.held = [value]
-
 
 line = Line()
 
 
 def call(kernel, out, grid, in_specs, out_specs, scalars, args, scratch=()):
-    result = run_kernel(
-        kernel, out, grid, in_specs, out_specs, line.later(scalars), args, scratch
-    )
-    line.ran(jax.tree.leaves(result)[0])
-    return result
-
-
-def run_kernel(kernel, out, grid, in_specs, out_specs, scalars, args, scratch):
-    return pl.pallas_call(
-        kernel,
+    held, n = line.held, len(args)
+
+    def body(s, *refs):
+        kernel(s, *refs[:n], *refs[n + len(held) :])
+
+    result = pl.pallas_call(
+        body,
         out_shape=out,
         grid_spec=pltpu.PrefetchScalarGridSpec(
             num_scalar_prefetch=1,
             grid=grid,
-            in_specs=in_specs,
+            in_specs=list(in_specs) + [pl.BlockSpec(memory_space=pl.ANY)] * len(held),
             out_specs=out_specs,
             scratch_shapes=list(scratch),
         ),
         compiler_params=pltpu.CompilerParams(vmem_limit_bytes=56 << 20),
-    )(scalars, *args)
+    )(scalars, *args, *held)
+    line.held = [jax.tree.leaves(result)[0]]
+    return result
 
 
 def whole(a):
@@ -122,20 +118,21 @@
     n_in, n_out, n_conv = (w.shape[0] // 32 for w in (w_in, w_out, conv_w))
     chunks = FF // D
     rows = n_out + n_in * chunks + n_conv
+    half = D // 2
 
     def kernel(_, *refs):
-        wi, wo, wc, flat, piece = refs[-5:]
+        wi, wo, wc, piece, flat = refs[-5:]
+        flat[...] = jnp.zeros_like(flat)
         for i, ref in enumerate(refs[:8]):
-            flat[i : i + 1, :] = ref[...].astype(f32).reshape(1, STEP)
-        b_in = refs[8][...].astype(f32).reshape(chunks, STEP)
-        flat[8 : 8 + chunks, :] = b_in
-        flat[8 + chunks :, :] = jnp.zeros((16 - 8 - chunks, STEP), f32)
+            flat[i : i + 1, :half] = ref[...].astype(f32).reshape(1, half)
+        flat[8 : 8 + FF // 2 // D, :] = refs[8][...].astype(f32).reshape(FF // 2 // D, D)
         piece[:n_out, :] = wo[...]
         for i in range(chunks):
             piece[n_out + i * n_in : n_out + (i + 1) * n_in, :] = wi[:, i * D : (i + 1) * D]
-        piece[n_out + n_in * chunks :, :] = wc[...]
-
-    out = (shape((16, STEP), f32), shape((rows, D), bf16))
+        piece[n_out + n_in * chunks : rows, :] = wc[...]
+        piece[rows:, :] = flat[...].astype(bf16)
+
+    out = shape((rows + 16, D), bf16)
     return call(
         kernel,
         out,
@@ -145,9 +142,10 @@
             pl.BlockSpec((w.shape[0] // 32, w.shape[1]), lambda j, s: (s[0], 0))
             for w in (w_in, w_out, conv_w)
         ],
-        [whole(o) for o in out],
+        whole(out),
         scalars,
         (*vectors, w_in, w_out, conv_w),
+        [pltpu.VMEM((16, D), f32)],
     )
 
 
@@ -176,22 +174,22 @@
 
 def unpack(mine, theirs, scalars):
     half = D // 2
+    at_row = mine.shape[0] // 16 - 1
+    tail = pl.BlockSpec((16, D), lambda j, s: (at_row, 0))
 
     def kernel(s, mine, theirs, vectors, b_in):
-        a, b = mine[...], theirs[...]
+        a, b = mine[...].astype(f32), theirs[...].astype(f32)
         low = jnp.where(s[0] == 0, a, b)
         high = jnp.where(s[0] == 0, b, a)
-        vectors[:, :half] = low[:8]
-        vectors[:, half:] = high[:8]
-        for i in range(FF // D):
-            part, k = (low, i) if i < 2 else (high, i - 2)
-            b_in[i : i + 1, :half] = part[8 + 2 * k : 9 + 2 * k]
-            b_in[i : i + 1, half:] = part[9 + 2 * k : 10 + 2 * k]
-
-    args = (mine, theirs)
+        vectors[:, :half] = low[:8, :half]
+        vectors[:, half:] = high[:8, :half]
+        rows = FF // 2 // D
+        b_in[:rows] = low[8 : 8 + rows]
+        b_in[rows:] = high[8 : 8 + rows]
+
     out = (shape((8, D), f32), shape((FF // D, D), f32))
     return call(
-        kernel, out, (1,), [whole(a) for a in args], [whole(o) for o in out], scalars, args
+        kernel, out, (1,), [tail, tail], [whole(o) for o in out], scalars, (mine, theirs)
     )
 
 
@@ -723,9 +721,9 @@
     ).reshape(rows, columns)
 
 
-def widen_near(own, twin, start, columns, swapped, scalars):
+def widen_near(own, twin, start, rows, columns, swapped, scalars):
     chunks = columns // 2 // STEP
-    u = D // 32
+    u = rows // 16
 
     def kernel(s, own, twin, out):
         def fill(src, base):
@@ -734,8 +732,7 @@
                     first, second = s[base + a], s[base + 4 + b]
                     place = second * 4 + first if swapped else first * 4 + second
                     for k in range(chunks):
-                        rows = slice(start + k * u, start + (k + 1) * u)
-                        value = src[a, b, rows, :].astype(f32)
+                        value = src[a, b, start + k * u : start + (k + 1) * u, :].astype(f32)
                         out[pl.ds(place, 1), :, k * STEP : (k + 1) * STEP] = value[None]
 
         @pl.when(pl.program_id(0) == 0)
@@ -754,7 +751,7 @@
         pl.BlockSpec((16, u, chunks * STEP), lambda h, s: (0, 0, lax.rem(h + s[0], 2))),
         scalars,
         (own, twin),
-    ).reshape(D // 2, columns)
+    ).reshape(rows, columns)
 
 
 def core_swap(v):
@@ -784,45 +781,118 @@
 
 
 class Flow:
-    def __init__(self, ring, pair, place, core):
-        self.rings = (ring, "z" if ring == "x" else "x")
-        self.place, self.core = place, core
+    def __init__(self, ring, pair):
+        self.ring, self.other = ring, "z" if ring == "x" else "x"
         send, self.keep = pair
         self.got = exchange(send, ring, (1, 3))
 
-    def onward(self, ring):
-        got = line.later(self.got)
-        self.near = got[0]
-        value = (self.keep[1].astype(f32) + got[1].astype(f32)).astype(bf16)
-        self.last = exchange(value, ring, (3, 1))
-        line.hold(value)
-
-    def settle(self):
-        last = line.later(self.last)
-        return self.keep[0].astype(f32) + self.near.astype(f32) + last.astype(f32)
+
+def onward(flows, none):
+    def kernel(_, *refs):
+        n = len(flows)
+        for i in range(n):
+            keep, got = refs[2 * i : 2 * i + 2]
+            refs[2 * n + i][0] = (keep[0, 0].astype(f32) + got[0, 0].astype(f32)).astype(bf16)
+
+    dims = [f.keep.shape[2:] for f in flows]
+    sums = call(
+        kernel,
+        tuple(shape((2, *d), bf16) for d in dims),
+        (2,),
+        [pl.BlockSpec((1, 1, *d), lambda y, s: (1, y, 0, 0)) for d in dims for _ in range(2)],
+        [pl.BlockSpec((1, *d), lambda y, s: (y, 0, 0)) for d in dims],
+        none,
+        [a for f in flows for a in (f.keep, f.got)],
+    )
+    for f, v in zip(flows, sums):
+        f.last = exchange(v, f.ring, (3, 1))
+
+
+def turn(flows, cuts):
+    in_specs, outs, out_specs, args = [], [], [], []
+    for f in flows:
+        first = 1 if f.other == "x" else 5
+        rows, columns = f.keep.shape[2] // 4, f.keep.shape[3]
+        in_specs += [
+            pl.BlockSpec((1, 2, rows, columns), lambda q, s, i=first: (0, 0, s[i + q], 0))
+        ] * 2 + [pl.BlockSpec((2, rows, columns), lambda q, s, i=first: (0, s[i + q], 0))]
+        args += [f.keep, f.got, f.last]
+        dims = (1, 2, rows, columns)
+        outs += [shape((2, *dims[1:]), bf16), shape((2, *dims[1:]), f32)]
+        out_specs += [
+            pl.BlockSpec(dims, lambda q, s: (jnp.minimum(q, 1), 0, 0, 0)),
+            pl.BlockSpec(dims, lambda q, s: (jnp.maximum(q - 2, 0), 0, 0, 0)),
+        ]
+
+    def kernel(_, *refs):
+        n = len(flows)
+        q = pl.program_id(0)
+        for i in range(n):
+            keep, got, last = refs[3 * i : 3 * i + 3]
+            send, kept = refs[3 * n + 2 * i : 3 * n + 2 * i + 2]
+            value = keep[0].astype(f32) + got[0].astype(f32) + last[...].astype(f32)
+            send[0] = jnp.where(q < 2, value.astype(bf16), send[0])
+            kept[0] = value
+
+    out = call(kernel, tuple(outs), (4,), in_specs, out_specs, cuts, args)
+    for i, f in enumerate(flows):
+        f.ring = f.other
+        f.keep = out[2 * i + 1]
+        f.got = exchange(out[2 * i], f.ring, (1, 3))
+
+
+class Finish:
+    def __init__(self, flows, extra, scalars):
+        sizes = [(f.keep.shape[2], f.keep.shape[3] // STEP) for f in flows]
+        rows = sum(u * n for u, n in sizes) + sum(e.shape[1] for e in extra)
+
+        def kernel(s, *refs):
+            send, mine = refs[-2:]
+            zero = s[0] == 0
+            start = 0
+            for i, (u, n) in enumerate(sizes):
+                keep, got, last = refs[3 * i : 3 * i + 3]
+                v = [
+                    keep[0, y].astype(f32) + got[0, y].astype(f32) + last[y].astype(f32)
+                    for y in range(2)
+                ]
+                near = jnp.where(zero, v[0], v[1])
+                away = jnp.where(zero, v[1], v[0]).astype(bf16)
+                for k in range(n):
+                    cut = slice(k * STEP, (k + 1) * STEP)
+                    mine[start : start + u, :] = near[:, cut]
+                    send[start : start + u, :] = away[:, cut]
+                    start += u
+            for ref in refs[3 * len(sizes) : -2]:
+                u = ref.shape[1]
+                mine[start : start + u, :] = jnp.where(zero, ref[0], ref[1])
+                send[start : start + u, :] = jnp.where(zero, ref[1], ref[0]).astype(bf16)
+                start += u
+
+        in_specs, args = [], []
+        for f in flows:
+            dims = (1, *f.keep.shape[1:])
+            in_specs += [pl.BlockSpec(dims, lambda j, s: (0, 0, 0, 0))] * 2 + [whole(f.last)]
+            args += [f.keep, f.got, f.last]
+        out = (shape((rows, STEP), bf16), shape((rows, STEP), f32))
+        send, self.mine = call(
+            kernel,
+            out,
+            (1,),
+            in_specs + [whole(e) for e in extra],
+            [whole(o) for o in out],
+            scalars,
+            args + list(extra),
+        )
+        self.got = exchange(send, "y", (1, 3))
 
     def second(self):
-        self.onward(self.rings[0])
-
-    def third(self):
-        v = self.settle()
-        y, rows, columns = v.shape
-        v = v.reshape(y, 4, rows // 4, columns)
-        ring = self.rings[1]
-        own, first, far, second = quarters(self.place[ring], self.core)
-        send = jnp.stack([pick(v, first, 1), pick(v, far, 1)]).astype(bf16)
-        self.keep = (pick(v, own, 1), pick(v, second, 1))
-        self.got = exchange(send, ring, (1, 3))
-        line.hold(send, *self.keep)
-
-    def fourth(self):
-        self.onward(self.rings[1])
-
-    def rows(self):
-        v = self.settle()
-        y, u, columns = v.shape
-        v = v.reshape(y, u, columns // STEP, STEP).transpose(0, 2, 1, 3)
-        return v.reshape(y, -1, STEP)
+        self.mine = (self.mine + self.got.astype(f32)).astype(bf16)
+        self.far = lax.ppermute(self.mine, "yh", [(0, 1), (1, 0)])
+        line.hold(self.mine)
+
+    def done(self):
+        return (self.mine.astype(f32) + self.far.astype(f32)).astype(bf16)
 
 
 class Spread:
@@ -833,13 +903,13 @@
         line.hold(v)
 
     def second(self, ring=None):
-        pair = jnp.stack([self.v, line.later(self.got)])
+        pair = jnp.stack([self.v, self.got])
         self.v = pair
         self.got = exchange(pair, ring or self.rings[0], (3, 1))
         line.hold(pair)
 
     def third(self):
-        four = jnp.concatenate([self.v, line.later(self.got)])
+        four = jnp.concatenate([self.v, self.got])
         self.v = four
         self.got = exchange(four, self.rings[1], (1, 3))
         line.hold(four)
@@ -848,27 +918,8 @@
         self.second(self.rings[1])
 
     def done(self):
-        all_ = jnp.concatenate([self.v, line.later(self.got)])
+        all_ = jnp.concatenate([self.v, self.got])
         return all_, core_swap(all_)
-
-
-class Finish:
-    def __init__(self, parts, yl):
-        v = jnp.concatenate(parts, axis=1)
-        self.mine = pick(v, yl, 0)
-        send = pick(v, 1 - yl, 0).astype(bf16)
-        self.got = exchange(send, "y", (1, 3))
-        line.hold(send, self.mine)
-
-    def second(self):
-        got = line.later(self.got)
-        self.mine = (self.mine + got.astype(f32)).astype(bf16)
-        self.far = lax.ppermute(self.mine, "yh", [(0, 1), (1, 0)])
-        line.hold(self.mine)
-
-    def done(self):
-        far = line.later(self.far)
-        return (self.mine.astype(f32) + far.astype(f32)).astype(bf16)
 
 
 def per_device(
@@ -909,7 +960,7 @@
         return (v, core_swap(v))
 
     spot = (place["x"] * 4 + place["z"]) * 2 + core
-    flat, piece = pack(
+    piece = pack(
         (ln1_g, ln1_b, bias_u, bias_v, ln2_g, ln2_b, b_out, conv_b, b_in),
         w_in,
         w_out,
@@ -917,7 +968,6 @@
         ints(spot),
     )
     piece_got = exchange(piece, "y", (1, 3))
-    flat_got = exchange(flat, "y", (1, 3))
 
     kv_part, small = pack_rows(w_kv, w_q, w_r, w_o, ints(core))
     kv_got = exchange(kv_part, "y", (1, 3))
@@ -926,7 +976,7 @@
     def joined(w, got, twin):
         return jnp.concatenate([w, got, twin], axis=0)
 
-    spread = lax.all_gather(piece_got, ("x", "z", "c"), axis=0)
+    spread = lax.all_gather(piece_got[:-16], ("x", "z", "c"), axis=0)
     thirds_d = ints(*thirds(D))
     thirds_c = ints(yl * (3 * D // 2), (1 - yl) * (3 * D // 2), *thirds(D))
     sinus_table = sinusoid(KEYS, D).astype(bf16)
@@ -938,15 +988,13 @@
         axis=1,
     )
     line.hold(sinus_rel)
-    vectors, b_in = unpack(flat, flat_got, ints(yl))
+    vectors, b_in = unpack(piece, piece_got, ints(yl))
 
     normed, normed_rel, oldest = first_norm(compressed, memory, tokens, vectors, thirds_d)
     both_normed, both_oldest, both_cot = both(normed), both(oldest), both(cotangent)
-    kv_got = line.later(kv_got)
     kv_whole = joined(w_kv, kv_got, core_swap(kv_got))
     key_value = dot(normed_rel, kv_whole).astype(bf16)
     line.hold(key_value)
-    small_got = line.later(small_got)
     small_twin = core_swap(small_got)
     q_whole, r_whole, o_whole = [
         joined(w, small_got[i], small_twin[i]) for i, w in enumerate((w_q, w_r, w_o))
@@ -968,7 +1016,7 @@
 
     def flows(groups):
         pairs = weight_grads(groups, cuts)
-        return [Flow(ring, pair, place, core) for (ring, _), pair in zip(groups, pairs)]
+        return [Flow(ring, pair) for (ring, _), pair in zip(groups, pairs)]
 
     hidden, d_pre, mixed_out, d_normed2, d_b_in = feed_forward(
         normed2_rel, residual, cotangent, w_in, w_out, spread, b_in, vectors, ints(yl)
@@ -978,37 +1026,22 @@
         cotangent, d_normed2, residual, vectors, o_whole, thirds_d
     )
     both_branch = both(d_branch)
-    out_flow, in_flow = flows(
+    large = flows(
         [
             ("x", [(both_hidden, 0, T, both_cot, False)]),
             ("z", [(both_n2, 0, T, both_pre, False), (both_att, 0, T, both_branch, False)]),
         ]
     )
+    d_kv, my_kv, give_kv, d_relative, d_queries, d_bias_u, d_bias_v = attend_back(
+        queries, key_value, relative, vectors, probs, d_attended, ints(core)
+    )
+    both_kv = (my_kv, core_swap(give_kv))
+    both_q, both_rel = both(d_queries), both(d_relative)
 
     compact, comp_normed = compress(oldest, conv_w, spread, vectors, thirds_c)
     comp_pair = dot(comp_normed, kv_whole).astype(bf16)
-    loss, d_ck, d_cv = reconstruct(queries, key_value, comp_pair, none)
-    recon_loss = jnp.sum(loss) / (T * D)
     compressed_next = jnp.concatenate([compressed[T // 3 :], compact], axis=0)
-    d_compact, d_conv_b = compress_back(d_ck, d_cv, kv_whole, compact, vectors, thirds_d)
-    both_compact = both(d_compact)
-    out_flow.second()
-    in_flow.second()
-    d_kv, my_kv, give_kv, d_relative, d_queries, d_bias_u, d_bias_v = attend_back(
-        queries, key_value, relative, vectors, probs, d_attended, ints(core)
-    )
-    both_kv = (my_kv, core_swap(give_kv))
-    both_q, both_rel = both(d_queries), both(d_relative)
-    (conv_flow,) = flows([("x", [(both_oldest, 0, T // 3, both_compact, False)])])
-    out_flow.third()
-    in_flow.third()
-    d_tokens, d_ln1_g, d_ln1_b = first_norm_back(
-        d_kv, d_queries, kv_whole, q_whole, compressed, memory, tokens, vectors, d_residual,
-        thirds_d,
-    )
-    out_flow.fourth()
-    in_flow.fourth()
-    x_flow, z_flow = flows(
+    near = flows(
         [
             ("x", [(both_normed, 0, KEYS, both_kv, True)]),
             (
@@ -1020,57 +1053,71 @@
             ),
         ]
     )
-    conv_flow.second()
-    conv_flow.third()
-    x_flow.second()
-    z_flow.second()
-    conv_flow.fourth()
-    x_flow.third()
-    z_flow.third()
-    early = Finish([out_flow.rows(), in_flow.rows(), conv_flow.rows()], yl)
-    x_flow.fourth()
-    z_flow.fourth()
+    onward(large, none)
+    loss, d_ck, d_cv = reconstruct(queries, key_value, comp_pair, none)
+    recon_loss = jnp.sum(loss) / (T * D)
+    d_compact, d_conv_b = compress_back(d_ck, d_cv, kv_whole, compact, vectors, thirds_d)
+    both_compact = both(d_compact)
+    turn(large, cuts)
+    onward(near, none)
+    conv = flows([("x", [(both_oldest, 0, T // 3, both_compact, False)])])
+    d_tokens, d_ln1_g, d_ln1_b = first_norm_back(
+        d_kv, d_queries, kv_whole, q_whole, compressed, memory, tokens, vectors, d_residual,
+        thirds_d,
+    )
+    onward(large, none)
+    turn(near, cuts)
+    early = Finish(large, [], ints(yl))
+    onward(conv, none)
+    onward(near, none)
     early.second()
+    turn(conv, cuts)
+    early_done = early.done()
+    line.hold(early_done)
+    early_sums = lax.all_gather(early_done, ("c", "x", "z"), axis=0)
+    onward(conv, none)
 
     total = jnp.concatenate(
         [d_ln1_g, d_ln1_b, d_bias_u, d_bias_v, d_ln2_g, d_ln2_b, d_b_out, d_conv_b]
         + [d_b_in]
     )
     total = jnp.concatenate(
-        [total[:8].reshape(8, 2, STEP).transpose(1, 0, 2), total[8:].reshape(2, 4, STEP)], axis=1
-    )
-    late = Finish([x_flow.rows(), z_flow.rows(), total, jnp.zeros((2, 4, STEP), f32)], yl)
-    early_done = early.done()
-    line.hold(early_done)
-    early_sums = lax.all_gather(early_done, ("c", "x", "z"), axis=0)
+        [
+            total[:8].reshape(8, 2, STEP).transpose(1, 0, 2),
+            total[8:].reshape(2, 4, STEP),
+            jnp.zeros((2, 4, STEP), f32),
+        ],
+        axis=1,
+    )
+    late = Finish([*near, *conv], [total], ints(yl))
     late.second()
     late_done = late.done()
-    kv_spread = Spread(late_done[:64], ("z", "x"))
-    qr_spread = Spread(late_done[64:], ("x", "z"))
-    kv_spread.second()
-    qr_spread.second()
-    kv_spread.third()
-    qr_spread.third()
-    kv_spread.fourth()
-    qr_spread.fourth()
-    (kv_own, kv_twin), (qr_own, qr_twin) = kv_spread.done(), qr_spread.done()
+    one = Spread(late_done[:128], ("z", "x"))
+    two = Spread(late_done[128:], ("x", "z"))
+    one.second()
+    two.second()
+    one.third()
+    two.third()
+    one.fourth()
+    two.fourth()
+    (one_own, one_twin), (two_own, two_twin) = one.done(), two.done()
     x_places, z_places = rels
     x_twin, z_twin = twins
     along = ints(core, *x_places, *z_places, *x_twin, *z_twin)
     across = ints(core, *z_places, *x_places, *z_twin, *x_twin)
-    g_kv = widen_near(kv_own, kv_twin, 0, 2 * D, False, along)
-    g_q = widen_near(qr_own, qr_twin, 0, D, False, across)
-    g_r = widen_near(qr_own, qr_twin, 32, D, False, across)
+    g_kv = widen_near(one_own, one_twin, 0, D // 2, 2 * D, False, along)
+    g_q = widen_near(one_own, one_twin, 64, D // 2, D, True, along)
+    g_r = widen_near(one_own, one_twin, 96, D // 2, D, True, along)
+    g_conv = widen_near(two_own, two_twin, 0, 3 * D // 2, D, True, across)
     g_out = widen(early_sums, 0, FF // 2, D, False, none)
     g_in = widen(early_sums, 128, D // 2, FF, True, none)
     g_o = widen(early_sums, 256, D // 2, D, True, none)
-    g_conv = widen(early_sums, 288, 3 * D // 2, D, False, none)
 
     def four(v):
         return (v[0] + v[1]) + (v[2] + v[3])
 
-    half = four(four(qr_own[:, :, 64:76].astype(f32))) + four(
-        four(qr_twin[:, :, 64:76].astype(f32))
+    half = four(four(two_own[:, :, 96:108].astype(f32))) + four(
+        four(two_twin[:, :, 96:108].astype(f32))
     )
     t_ln1_g, t_ln1_b, t_bu, t_bv, t_ln2_g, t_ln2_b, t_bout, t_convb = [half[i] for i in range(8)]
     t_bin = half[8:].reshape(-1)

time: 438 us -> 490 us (1.12)
  Pallas kernels: 149 us -> 185 us
  other arithmetic: 50.4 us -> 20.6 us
  starting transfers between devices: 71 us -> 94.1 us
  waiting for transfers between devices: 111 us -> 134 us
    pallas_call x23 -> x34, Pallas kernels: 149 us -> 185 us  [call(): pl.pallas_call(body, out_shape=out, grid_spec=pltpu.PrefetchScalarGridSpe...]
    ppermute x34 -> x33, waiting for transfers between devices: 98.8 us -> 121 us  [exchange(): return lax.ppermute(v, RING[ring], pairs)]
    convert_element_type x16 -> x6, other arithmetic: 19.3 us -> 5.12 us  [the longest x2 2.26 us: second(): self.mine = (self.mine + self.got.astype(f32)).astype(bf16)]
    ppermute x16, starting transfers between devices: 27.4 us -> 41.2 us  [core_swap(): return lax.ppermute(v, 'c', [(0, 1), (1, 0)])]
    add x11 -> x1, other arithmetic: 13.6 us -> 0.02 us  [per_device(): four(four(two_own[:, :, 96:108].astype(f32)))]
    ppermute x34 -> x33, starting transfers between devices: 42 us -> 50.7 us  [exchange(): return lax.ppermute(v, RING[ring], pairs)]
    unnamed x110 -> x146, local copies, waits for them, and re-layouts: 10.3 us -> 15.8 us
  transfers between devices with their start and end apart: 54 -> 53, of which waited for: 23 -> 20; matrix products, arithmetic and copies ran while one was open for 17% -> 8% of each run, Pallas kernels for 22% -> 27%
where the time goes in v1:
time: 490 us; the launch traced here: 485 us
  Pallas kernels  185 us (38%)
  waiting for transfers between devices  134 us (27%)
  starting transfers between devices  94.1 us (19%)
  local copies, waits for them, and re-layouts  24.9 us (5%)
  other arithmetic  20.6 us (4%)
  between operations  17 us (3%)
  matrix products  9.42 us (2%)
    pallas_call x34, Pallas kernels, call(): pl.pallas_call(body, out_shape=out, grid_spec=pltpu.PrefetchScalarGridSpe...  185 us
    ppermute x33, waiting for transfers between devices, exchange(): return lax.ppermute(v, RING[ring], pairs)  121 us
    ppermute x33, starting transfers between devices, exchange(): return lax.ppermute(v, RING[ring], pairs)  50.7 us
    ppermute x16, starting transfers between devices, core_swap(): return lax.ppermute(v, 'c', [(0, 1), (1, 0)])  41.2 us
    unnamed x146, local copies, waits for them, and re-layouts  15.8 us
    ppermute x2, waiting for transfers between devices, second(): self.far = lax.ppermute(self.mine, 'yh', [(0, 1), (1, 0)])  12 us
  transfers between devices with their start and end apart: 53, of which 20 were waited for; matrix products, arithmetic and copies ran while one was open for 8% of the time, Pallas kernels for 27%

profile of v1, /device:TPU:1, one launch (start us, length us, event | category | flops | bytes accessed | tf_op | source)
XLA Modules:
  0.0 485.2 jit_solution(7900257741954447826)
XLA Ops:
  12.8 5.4 %collective-permute-done.refs_1_ = bf16[192,1024]{1,0:T(8,128)(2,1)S(1)} collective-permute-done((bf16[192,1024]{1,0:T(8,128)(2,1)}, bf16[192,1024]{1,0:T(8,128)(2,1)S(1)}, u32[]{:S(2)}, u32[]{:S(2)}) %collective-permute-start) | collective-permute-done | bytes 393248 | tf_op jit(solution)/shard_map/ppermute | solution.py:770
  25.0 4.7 fusion.10
  30.2 24.1 %collective-permute-done.3 = bf16[256,2048]{1,0:T(8,128)(2,1)} collective-permute-done((bf16[256,2048]{1,0:T(8,128)(2,1)}, bf16[256,2048]{1,0:T(8,128)(2,1)}, u32[]{:S(2)}, u32[]{:S(2)}) %collective-permute-start.3) | collective-permute-done | bytes 1048608 | tf_op jit(solution)/shard_map/ppermute | solution.py:770
  58.5 4.7 shard_map.350
  77.5 7.6 %shard_map.351 = (f32[8,192,640]{2,1,0:T(8,128)}, bf16[192,1024]{1,0:T(8,128)(2,1)}) custom-call(s32[1]{0:T(128)} %constant.10.clone.1.s, f32[192,1024]{1,0:T(8,128)} %fusion.12.refs_0_.refs_7_, bf16[576,2048]{1,0:T(8,128)(2,1)} %convolution_convert_fusion.refs_1_.refs_2_.refs_6_, bf16[576,2048]{1,0:T(8,128)(2,1)} %convolution_convert_fusion.refs_1_.refs_2_.refs_6_, ...), custom_call_target="tpu_custom_call" | custom-call | tf_op jit(solution)/shard_map/pallas_call | solution.py:61
  90.8 18.3 %shard_map.353 = (bf16[192,4096]{1,0:T(8,128)(2,1)}, bf16[192,4096]{1,0:T(8,128)(2,1)}, bf16[192,1024]{1,0:T(8,128)(2,1)}, f32[192,1024]{1,0:T(8,128)}, f32[4,1024]{1,0:T(4,128)}) custom-call(s32[1]{0:T(128)} %bitcast.s, bf16[192,1024]{1,0:T(8,128)(2,1)} %get-tuple-element.99.refs_0_, f32[192,1024]{1,0:T(8,128)} %get-tuple-element.100.refs_1_.refs_9_.refs_2_, ...), custom_call_target="tpu_custom_call" | custom-call | tf_op jit(solution)/shard_map/pallas_call | solution.py:61
  110.9 5.0 %shard_map.354 = (f32[192,1024]{1,0:T(8,128)}, bf16[192,1024]{1,0:T(8,128)(2,1)}, bf16[192,1024]{1,0:T(8,128)(2,1)}, f32[1,1024]{1,0:T(1,128)}, f32[1,1024]{1,0:T(1,128)}, /*index=5*/f32[1,1024]{1,0:T(1,128)}) custom-call(s32[3]{0:T(128)} %pad_add_fusion.s, bf16[192,1024]{1,0:T(8,128)(2,1)} %bitcast.100, f32[192,1024]{1,0:T(8,128)} %get-tuple-element.104.refs_1_, ...), custom_call_target="tpu_custom_call" | custom-call | tf_op jit(solution)/shard_map/pallas_call | solution.py:61
  119.9 11.6 %shard_map.355 = (bf16[2,2,512,512]{3,2,1,0:T(8,128)(2,1)}, bf16[2,2,512,512]{3,2,1,0:T(8,128)(2,1)}, bf16[2,2,128,2560]{3,2,1,0:T(8,128)(2,1)}, bf16[2,2,128,2560]{3,2,1,0:T(8,128)(2,1)}) custom-call(s32[9]{0:T(128)} %stack.159.s, bf16[192,4096]{1,0:T(8,128)(2,1)} %get-tuple-element.105.refs_5_.refs_0_.refs_1_, ...), custom_call_target="tpu_custom_call" | custom-call | tf_op jit(solution)/shard_map/pallas_call | solution.py:61
  137.9 11.4 %shard_map.356 = (bf16[2,576,1024]{2,1,0:T(8,128)(2,1)}, bf16[576,1024]{1,0:T(8,128)(2,1)}, bf16[576,1024]{1,0:T(8,128)(2,1)}, bf16[576,1024]{1,0:T(8,128)(2,1)}...) custom-call(s32[1]{0:T(128)} %bitcast.8.s, f32[192,1024]{1,0:T(8,128)} %fusion.12.refs_0_.refs_7_, ...), custom_call_target="tpu_custom_call" | custom-call | tf_op jit(solution)/shard_map/pallas_call | solution.py:61
  152.4 6.0 %shard_map.357 = (f32[64,1024]{1,0:T(8,128)}, bf16[64,1024]{1,0:T(8,128)(2,1)}) custom-call(s32[5]{0:T(128)} %stack.150.s, bf16[64,3072]{1,0:T(8,128)(2,1)} %get-tuple-element.103.refs_0_.refs_1_, bf16[1536,1024]{1,0:T(8,128)(2,1)} %refs_1_.5, bf16[32,176,1024]{2,1,0:T(8,128)(2,1)} %bitcast.88, bf16[32,176,1024]{2,1,0:T(8,128)(2,1)} %bitcast.89, ...), custom_call_target="tpu_custom_call" | custom-call | tf_op jit(solution)/shard_map/pallas_call | solution.py:61
  159.4 10.8 %shard_map.358 = (bf16[2,2,128,1024]{3,2,1,0:T(8,128)(2,1)}, bf16[2,2,128,1024]{3,2,1,0:T(8,128)(2,1)}, bf16[2,2,128,1024]{3,2,1,0:T(8,128)(2,1)}, bf16[2,2,128,1024]{3,2,1,0:T(8,128)(2,1)}) custom-call(s32[9]{0:T(128)} %stack.159.s, bf16[576,1024]{1,0:T(8,128)(2,1)} %get-tuple-element.96.refs_5_.refs_0_.refs_1_.refs_6_.refs_7_, ...), custom_call_target="tpu_custom_call" | custom-call | tf_op jit(solution)/shard_map/pallas_call | solution.py:61
  179.2 8.4 %shard_map.360 = (f32[1,128]{1,0:T(1,128)}, bf16[64,1024]{1,0:T(8,128)(2,1)}, bf16[64,1024]{1,0:T(8,128)(2,1)}) custom-call(s32[1]{0:T(128)} %constant.10.clone.1.s, f32[192,1024]{1,0:T(8,128)} %fusion.12.refs_0_.refs_7_, bf16[576,2048]{1,0:T(8,128)(2,1)} %convolution_convert_fusion.refs_1_.refs_2_.refs_6_, ...), custom_call_target="tpu_custom_call" | custom-call | tf_op jit(solution)/shard_map/pallas_call | solution.py:61
  187.7 5.3 %shard_map.361 = (bf16[64,1024]{1,0:T(8,128)(2,1)}, f32[1,1024]{1,0:T(1,128)}) custom-call(s32[3]{0:T(128)} %pad_add_fusion.s, bf16[64,1024]{1,0:T(8,128)(2,1)} %get-tuple-element.125.refs_0_, bf16[64,1024]{1,0:T(8,128)(2,1)} %get-tuple-element.126.refs_1_, bf16[1024,2048]{1,0:T(8,128)(2,1)} %copy-done, f32[64,1024]{1,0:T(8,128)} %get-tuple-element.113.refs_18_.refs_3_, ...), custom_call_target="tpu_custom_call" | custom-call | tf_op jit(solution)/shard_map/pallas_call | solution.py:61
  202.7 6.1 %shard_map.362 = (bf16[2,2,128,512]{3,2,1,0:T(8,128)(2,1)}, f32[2,2,128,512]{3,2,1,0:T(8,128)}, bf16[2,2,32,2560]{3,2,1,0:T(8,128)(2,1)}, f32[2,2,32,2560]{3,2,1,0:T(8,128)}) custom-call(s32[9]{0:T(128)} %stack.159.s, bf16[2,2,512,512]{3,2,1,0:T(8,128)(2,1)} %get-tuple-element.115.refs_0_, bf16[2,2,512,512]{3,2,1,0:T(8,128)(2,1)} %collective-permute-done.11.refs_1_, ...), custom_call_target="tpu_custom_call" | custom-call | tf_op jit(solution)/shard_map/pallas_call | solution.py:61
  221.3 5.4 %shard_map.364 = (bf16[2,2,384,512]{3,2,1,0:T(8,128)(2,1)}, bf16[2,2,384,512]{3,2,1,0:T(8,128)(2,1)}) custom-call(s32[9]{0:T(128)} %stack.159.s, bf16[64,3072]{1,0:T(8,128)(2,1)} %get-tuple-element.103.refs_0_.refs_1_, bf16[64,3072]{1,0:T(8,128)(2,1)} %get-tuple-element.103.refs_0_.refs_1_, bf16[64,3072]{1,0:T(8,128)(2,1)} %copy-done.30, ...), custom_call_target="tpu_custom_call" | custom-call | tf_op jit(solution)/shard_map/pallas_call | solution.py:61
  226.7 10.7 %shard_map.365 = (f32[192,1024]{1,0:T(8,128)}, f32[1,1024]{1,0:T(1,128)}, f32[1,1024]{1,0:T(1,128)}) custom-call(s32[3]{0:T(128)} %pad_add_fusion.s, bf16[2,576,1024]{2,1,0:T(8,128)(2,1)} %get-tuple-element.112.refs_6_.refs_0_, bf16[192,1024]{1,0:T(8,128)(2,1)} %get-tuple-element.120.refs_10_.refs_1_, bf16[1024,2048]{1,0:T(8,128)(2,1)} %copy-done, ...), custom_call_target="tpu_custom_call" | custom-call | tf_op jit(solution)/shard_map/pallas_call | solution.py:61
  242.9 4.8 shard_map.367
  261.5 5.5 %collective-permute-done.37 = bf16[288,512]{1,0:T(8,128)(2,1)S(1)} collective-permute-done((bf16[288,512]{1,0:T(8,128)(2,1)S(1)}, bf16[288,512]{1,0:T(8,128)(2,1)S(1)}, u32[]{:S(2)}, u32[]{:S(2)}) %collective-permute-start.37) | collective-permute-done | bytes 294944 | tf_op jit(solution)/shard_map/ppermute | solution.py:891
  269.7 22.6 %collective-permute-done.29.refs_1_ = bf16[2,2,384,512]{3,2,1,0:T(8,128)(2,1)S(1)} collective-permute-done((bf16[2,2,384,512]{3,2,1,0:T(8,128)(2,1)S(1)}, bf16[2,2,384,512]{3,2,1,0:T(8,128)(2,1)S(1)}, u32[]{:S(2)}, u32[]{:S(2)}) %collective-permute-start.29) | collective-permute-done | bytes 1572896 | tf_op jit(solution)/shard_map/ppermute | solution.py:770
  305.9 8.5 %collective-permute-done.28.refs_3_.refs_4_ = bf16[2,2,32,1024]{3,2,1,0:T(8,128)(2,1)S(1)} collective-permute-done((bf16[2,2,32,1024]{3,2,1,0:T(8,128)(2,1)S(1)}, bf16[2,2,32,1024]{3,2,1,0:T(8,128)(2,1)S(1)}, u32[]{:S(2)}, u32[]{:S(2)}) %collective-permute-start.28) | collective-permute-done | bytes 262176 | tf_op jit(solution)/shard_map/ppermute | solution.py:770
  317.9 4.9 %shard_map.371 = (bf16[2,2,96,512]{3,2,1,0:T(8,128)(2,1)}, f32[2,2,96,512]{3,2,1,0:T(8,128)}) custom-call(s32[9]{0:T(128)} %stack.159.s, bf16[2,2,384,512]{3,2,1,0:T(8,128)(2,1)} %get-tuple-element.145.refs_0_, bf16[2,2,384,512]{3,2,1,0:T(8,128)(2,1)} %copy-done.7, bf16[2,384,512]{2,1,0:T(8,128)(2,1)} %copy-done.42, ...), custom_call_target="tpu_custom_call" | custom-call | tf_op jit(solution)/shard_map/pallas_call | solution.py:61
  336.7 5.4 %collective-permute-done.38.refs_8_ = bf16[2,96,512]{2,1,0:T(8,128)(2,1)S(1)} collective-permute-done((bf16[2,96,512]{2,1,0:T(8,128)(2,1)}, bf16[2,96,512]{2,1,0:T(8,128)(2,1)S(1)}, u32[]{:S(2)}, u32[]{:S(2)}) %collective-permute-start.38) | collective-permute-done | bytes 196640 | tf_op jit(solution)/shard_map/ppermute | solution.py:770
  352.9 6.5 %collective-permute-done.40 = bf16[240,512]{1,0:T(8,128)(2,1)S(1)} collective-permute-done((bf16[240,512]{1,0:T(8,128)(2,1)S(1)}, bf16[240,512]{1,0:T(8,128)(2,1)S(1)}, u32[]{:S(2)}, u32[]{:S(2)}) %collective-permute-start.40) | collective-permute-done | bytes 245792 | tf_op jit(solution)/shard_map/ppermute | solution.py:891
  373.3 7.1 %collective-permute-done.46 = bf16[128,512]{1,0:T(8,128)(2,1)S(1)} collective-permute-done((bf16[128,512]{1,0:T(8,128)(2,1)S(1)}, bf16[128,512]{1,0:T(8,128)(2,1)S(1)}, u32[]{:S(2)}, u32[]{:S(2)}) %collective-permute-start.46) | collective-permute-done | bytes 131104 | tf_op jit(solution)/shard_map/ppermute | solution.py:770
  388.6 6.6 %collective-permute-done.48 = bf16[4,128,512]{2,1,0:T(8,128)(2,1)S(1)} collective-permute-done((bf16[4,128,512]{2,1,0:T(8,128)(2,1)S(1)}, bf16[4,128,512]{2,1,0:T(8,128)(2,1)S(1)}, u32[]{:S(2)}, u32[]{:S(2)}) %collective-permute-start.48) | collective-permute-done | bytes 524320 | tf_op jit(solution)/shard_map/ppermute | solution.py:770
  395.4 6.5 %collective-permute-done.44 = bf16[2,4,112,512]{3,2,1,0:T(8,128)(2,1)S(1)} collective-permute-done((bf16[2,4,112,512]{3,2,1,0:T(8,128)(2,1)S(1)}, bf16[2,4,112,512]{3,2,1,0:T(8,128)(2,1)S(1)}, u32[]{:S(2)}, u32[]{:S(2)}) %collective-permute-start.44) | collective-permute-done | bytes 917536 | tf_op jit(solution)/shard_map/ppermute | solution.py:770
  403.4 20.6 %collective-permute-start.45 = (bf16[4,4,112,512]{3,2,1,0:T(8,128)(2,1)}, bf16[4,4,112,512]{3,2,1,0:T(8,128)(2,1)}, u32[]{:S(2)}, u32[]{:S(2)}) collective-permute-start(bf16[4,4,112,512]{3,2,1,0:T(8,128)(2,1)} %pad_maximum_fusion.3.refs_0_), channel_id=1, source_target_pairs={{0,2},{2,0},{1,3},{3,1},{4,6},{6,4},{5,7},{7,5},{8,10},{10,8},{9,1... | collective-permute-start | bytes 5505032 | tf_op jit(solution)/shard_map/ppermute | solution.py:758
  424.2 11.8 %collective-permute-start.50 = (bf16[4,4,128,512]{3,2,1,0:T(8,128)(2,1)S(1)}, bf16[4,4,128,512]{3,2,1,0:T(8,128)(2,1)}, u32[]{:S(2)}, u32[]{:S(2)}) collective-permute-start(bf16[4,4,128,512]{3,2,1,0:T(8,128)(2,1)S(1)} %pad_maximum_fusion.2.refs_0_), channel_id=1, source_target_pairs={{0,2},{2,0},{1,3},{3,1},{4,6},{6,4},{5,7},{7,5},{8,10},{10,8},{9,1... | collective-permute-start | bytes 6291464 | tf_op jit(solution)/shard_map/ppermute | solution.py:758
  442.8 5.1 %shard_map.374.refs_2_ = f32[16,32,2048]{2,1,0:T(8,128)} custom-call(s32[17]{0:T(128)} %stack.166.s, bf16[4,4,128,512]{3,2,1,0:T(8,128)(2,1)} %copy-done.2, bf16[4,4,128,512]{3,2,1,0:T(8,128)(2,1)} %collective-permute-done.50.refs_1_, bf16[240,512]{1,0:T(8,128)(2,1)} %get-tuple-element.163.refs_2_, bf16[240,512]{1,0:T(8,128)(2,1)} %copy-done.22, ...), custom_call_target="tpu_custom_call" | custom-call | tf_op jit(solution)/shard_map/pallas_call | solution.py:61
  456.5 5.7 %shard_map.377.refs_1_ = f32[16,96,1024]{2,1,0:T(8,128)} custom-call(s32[17]{0:T(128)} %stack.173.s, bf16[4,4,112,512]{3,2,1,0:T(8,128)(2,1)} %pad_maximum_fusion.3.refs_0_, bf16[4,4,112,512]{3,2,1,0:T(8,128)(2,1)} %collective-permute-done.45.refs_1_, f32[16,32,1024]{2,1,0:T(8,128)} %shard_map.376.refs_2_), custom_call_target="tpu_custom_call" | custom-call | tf_op jit(solution)/shard_map/pallas_call | solution.py:61
  462.1 7.3 %shard_map.378.refs_4_ = f32[16,128,1024]{2,1,0:T(8,128)} custom-call(s32[1]{0:T(128)} %constant.10.clone.1.s, bf16[32,288,512]{2,1,0:T(8,128)(2,1)} %bitcast.80, f32[16,96,1024]{2,1,0:T(8,128)} %shard_map.377.refs_1_), custom_call_target="tpu_custom_call" | custom-call | tf_op jit(solution)/shard_map/pallas_call | solution.py:61
  469.4 5.2 %shard_map.379.refs_1_ = f32[16,32,4096]{2,1,0:T(8,128)} custom-call(s32[1]{0:T(128)} %constant.10.clone.1.s, bf16[32,288,512]{2,1,0:T(8,128)(2,1)} %bitcast.81, bf16[32,288,512]{2,1,0:T(8,128)(2,1)} %bitcast.82, bf16[32,288,512]{2,1,0:T(8,128)(2,1)} %bitcast.83, bf16[32,288,512]{2,1,0:T(8,128)(2,1)} %bitcast.84, f32[16,128,1024]{2,1,0:T(8,128)} %shard_map.378.refs_4_), custom_call_target="tpu_custom_call" | custom-call | tf_op jit(solution)/shard_map/pallas_call | solution.py:61
  (306 shorter events, 189.0 us)
Async XLA Ops:
  7.2 83.6 %all-gather.5.cloned.1.call-start = ((), (), s32[]{:S(2)}) async-start(), calls=%async_computation | async-start | bytes 11894784 | tf_op jit(solution)/shard_map/all_gather | solution.py:979
  19.0 443.2 %all-gather.7.cloned.1.call-start = ((), (), s32[]{:S(2)}) async-start(), calls=%async_computation.1 | async-start | bytes 9732096 | tf_op jit(solution)/shard_map/all_gather | solution.py:1077
  22.2 32.6 %collective-permute-start.1 = (bf16[3,256,1024]{2,1,0:T(8,128)(2,1)}, bf16[3,256,1024]{2,1,0:T(8,128)(2,1)}, u32[]{:S(2)}, u32[]{:S(2)}) collective-permute-start(bf16[3,256,1024]{2,1,0:T(8,128)(2,1)} %get-tuple-element.95), channel_id=1, source_target_pairs={{0,1},{2,67},{1,0},{3,66},{64,65},{66,3},{65,64},{67,2},{4,5},{6,7... | collective-permute-start | bytes 4718600 | tf_op jit(solution)/shard_map/ppermute | solution.py:770
  24.9 29.4 %collective-permute-start.3 = (bf16[256,2048]{1,0:T(8,128)(2,1)}, bf16[256,2048]{1,0:T(8,128)(2,1)}, u32[]{:S(2)}, u32[]{:S(2)}) collective-permute-start(bf16[256,2048]{1,0:T(8,128)(2,1)} %get-tuple-element.92.refs_2_), channel_id=1, source_target_pairs={{0,1},{2,67},{1,0},{3,66},{64,65},{66,3},{65,64},{67,2},{4,5},{6,7... | collective-permute-start | bytes 3145736 | tf_op jit(solution)/shard_map/ppermute | solution.py:770
  54.3 12.0 %collective-permute-start.4 = (bf16[256,2048]{1,0:T(8,128)(2,1)}, bf16[256,2048]{1,0:T(8,128)(2,1)}, u32[]{:S(2)}, u32[]{:S(2)}) collective-permute-start(bf16[256,2048]{1,0:T(8,128)(2,1)} %collective-permute-done.3), channel_id=1, source_target_pairs={{0,2},{2,0},{1,3},{3,1},{4,6},{6,4},{5,7},{7,5},{8,10},{10,8},{9,1... | collective-permute-start | bytes 3145736 | tf_op jit(solution)/shard_map/ppermute | solution.py:758
  54.8 17.0 %collective-permute-start.2 = (bf16[3,256,1024]{2,1,0:T(8,128)(2,1)}, bf16[3,256,1024]{2,1,0:T(8,128)(2,1)}, u32[]{:S(2)}, u32[]{:S(2)}) collective-permute-start(bf16[3,256,1024]{2,1,0:T(8,128)(2,1)} %collective-permute-done.1), channel_id=1, source_target_pairs={{0,2},{2,0},{1,3},{3,1},{4,6},{6,4},{5,7},{7,5},{8,10},{10,8},{9,1... | collective-permute-start | bytes 4718600 | tf_op jit(solution)/shard_map/ppermute | solution.py:758
  109.0 9.6 %collective-permute-start.5 = (bf16[192,4096]{1,0:T(8,128)(2,1)}, bf16[192,4096]{1,0:T(8,128)(2,1)S(1)}, u32[]{:S(2)}, u32[]{:S(2)}) collective-permute-start(bf16[192,4096]{1,0:T(8,128)(2,1)} %get-tuple-element.105.refs_5_.refs_0_.refs_1_), channel_id=1, source_target_pairs={{0,2},{2,0},{1,3},{3,1},{4,6},{6,4},{5,7},{7,5},{8,10},{10,8},{9,1... | collective-permute-start | bytes 4718600 | tf_op jit(solution)/shard_map/ppermute | solution.py:758
  109.4 9.3 %collective-permute-start.8 = (bf16[192,4096]{1,0:T(8,128)(2,1)}, bf16[192,4096]{1,0:T(8,128)(2,1)}, u32[]{:S(2)}, u32[]{:S(2)}) collective-permute-start(bf16[192,4096]{1,0:T(8,128)(2,1)} %get-tuple-element.108.refs_10_), channel_id=1, source_target_pairs={{0,2},{2,0},{1,3},{3,1},{4,6},{6,4},{5,7},{7,5},{8,10},{10,8},{9,1... | collective-permute-start | bytes 4718600 | tf_op jit(solution)/shard_map/ppermute | solution.py:758
  131.4 38.7 %collective-permute-start.12 = (bf16[2,2,128,2560]{3,2,1,0:T(8,128)(2,1)}, bf16[2,2,128,2560]{3,2,1,0:T(8,128)(2,1)}, u32[]{:S(2)}, u32[]{:S(2)}) collective-permute-start(bf16[2,2,128,2560]{3,2,1,0:T(8,128)(2,1)} %get-tuple-element.117), channel_id=1, source_target_pairs={{0,4},{2,14},{4,0},{6,10},{8,12},{10,6},{12,8},{14,2},{1,5},{3,15}... | collective-permute-start | bytes 7864328 | tf_op jit(solution)/shard_map/ppermute | solution.py:770
  135.5 34.7 %collective-permute-start.11 = (bf16[2,2,512,512]{3,2,1,0:T(8,128)(2,1)}, bf16[2,2,512,512]{3,2,1,0:T(8,128)(2,1)}, u32[]{:S(2)}, u32[]{:S(2)}) collective-permute-start(bf16[2,2,512,512]{3,2,1,0:T(8,128)(2,1)} %get-tuple-element.111.refs_7_), channel_id=1, source_target_pairs={{0,16},{2,50},{16,0},{18,34},{32,48},{34,18},{48,32},{50,2},{1,17}... | collective-permute-start | bytes 6291464 | tf_op jit(solution)/shard_map/ppermute | solution.py:770
  137.9 12.1 %collective-permute-start.13 = (bf16[576,1024]{1,0:T(8,128)(2,1)S(1)}, bf16[576,1024]{1,0:T(8,128)(2,1)S(1)}, u32[]{:S(2)}, u32[]{:S(2)}) collective-permute-start(bf16[576,1024]{1,0:T(8,128)(2,1)S(1)} %copy-done.3), channel_id=1, source_target_pairs={{0,2},{2,0},{1,3},{3,1},{4,6},{6,4},{5,7},{7,5},{8,10},{10,8},{9,1... | collective-permute-start | bytes 3538952 | tf_op jit(solution)/shard_map/ppermute | solution.py:758
  149.4 9.0 %collective-permute-start.14 = (bf16[576,1024]{1,0:T(8,128)(2,1)}, bf16[576,1024]{1,0:T(8,128)(2,1)S(1)}, u32[]{:S(2)}, u32[]{:S(2)}) collective-permute-start(bf16[576,1024]{1,0:T(8,128)(2,1)} %get-tuple-element.119), channel_id=1, source_target_pairs={{0,2},{2,0},{1,3},{3,1},{4,6},{6,4},{5,7},{7,5},{8,10},{10,8},{9,1... | collective-permute-start | bytes 3538952 | tf_op jit(solution)/shard_map/ppermute | solution.py:758
  173.9 27.7 %collective-permute-start.22 = (bf16[2,128,2560]{2,1,0:T(8,128)(2,1)}, bf16[2,128,2560]{2,1,0:T(8,128)(2,1)S(1)}, u32[]{:S(2)}, u32[]{:S(2)}) collective-permute-start(bf16[2,128,2560]{2,1,0:T(8,128)(2,1)} %get-tuple-element.131), channel_id=1, source_target_pairs={{0,12},{2,6},{4,8},{6,2},{8,4},{10,14},{12,0},{14,10},{1,13},{3,7}... | collective-permute-start | bytes 3932168 | tf_op jit(solution)/shard_map/ppermute | solution.py:770
  173.9 23.2 %collective-permute-start.21 = (bf16[2,512,512]{2,1,0:T(8,128)(2,1)}, bf16[2,512,512]{2,1,0:T(8,128)(2,1)}, u32[]{:S(2)}, u32[]{:S(2)}) collective-permute-start(bf16[2,512,512]{2,1,0:T(8,128)(2,1)} %get-tuple-element.123.refs_5_), channel_id=1, source_target_pairs={{0,48},{2,18},{16,32},{18,2},{32,16},{34,50},{48,0},{50,34},{1,49}... | collective-permute-start | bytes 3145736 | tf_op jit(solution)/shard_map/ppermute | solution.py:770
  174.0 37.8 %collective-permute-start.19 = (bf16[2,2,128,1024]{3,2,1,0:T(8,128)(2,1)}, bf16[2,2,128,1024]{3,2,1,0:T(8,128)(2,1)S(1)}, u32[]{:S(2)}, u32[]{:S(2)}) collective-permute-start(bf16[2,2,128,1024]{3,2,1,0:T(8,128)(2,1)} %get-tuple-element.122.refs_4_), channel_id=1, source_target_pairs={{0,16},{2,50},{16,0},{18,34},{32,48},{34,18},{48,32},{50,2},{1,17}... | collective-permute-start | bytes 3145736 | tf_op jit(solution)/shard_map/ppermute | solution.py:770
  174.7 37.1 %collective-permute-start.20 = (bf16[2,2,128,1024]{3,2,1,0:T(8,128)(2,1)}, bf16[2,2,128,1024]{3,2,1,0:T(8,128)(2,1)S(1)}, u32[]{:S(2)}, u32[]{:S(2)}) collective-permute-start(bf16[2,2,128,1024]{3,2,1,0:T(8,128)(2,1)} %get-tuple-element.130), channel_id=1, source_target_pairs={{0,4},{2,14},{4,0},{6,10},{8,12},{10,6},{12,8},{14,2},{1,5},{3,15}... | collective-permute-start | bytes 3145736 | tf_op jit(solution)/shard_map/ppermute | solution.py:770
  208.7 28.7 %collective-permute-start.26 = (bf16[2,2,32,2560]{3,2,1,0:T(8,128)(2,1)}, bf16[2,2,32,2560]{3,2,1,0:T(8,128)(2,1)S(1)}, u32[]{:S(2)}, u32[]{:S(2)}) collective-permute-start(bf16[2,2,32,2560]{3,2,1,0:T(8,128)(2,1)} %get-tuple-element.139), channel_id=1, source_target_pairs={{0,16},{2,50},{16,0},{18,34},{32,48},{34,18},{48,32},{50,2},{1,17}... | collective-permute-start | bytes 1966088 | tf_op jit(solution)/shard_map/ppermute | solution.py:770
  211.8 25.6 %collective-permute-start.25 = (bf16[2,2,128,512]{3,2,1,0:T(8,128)(2,1)}, bf16[2,2,128,512]{3,2,1,0:T(8,128)(2,1)S(1)}, u32[]{:S(2)}, u32[]{:S(2)}) collective-permute-start(bf16[2,2,128,512]{3,2,1,0:T(8,128)(2,1)} %get-tuple-element.132.refs_4_), channel_id=1, source_target_pairs={{0,4},{2,14},{4,0},{6,10},{8,12},{10,6},{12,8},{14,2},{1,5},{3,15}... | collective-permute-start | bytes 1572872 | tf_op jit(solution)/shard_map/ppermute | solution.py:770
  215.7 25.6 %collective-permute-start.23 = (bf16[2,128,1024]{2,1,0:T(8,128)(2,1)}, bf16[2,128,1024]{2,1,0:T(8,128)(2,1)S(1)}, u32[]{:S(2)}, u32[]{:S(2)}) collective-permute-start(bf16[2,128,1024]{2,1,0:T(8,128)(2,1)} %get-tuple-element.133.refs_6_), channel_id=1, source_target_pairs={{0,48},{2,18},{16,32},{18,2},{32,16},{34,50},{48,0},{50,34},{1,49}... | collective-permute-start | bytes 1572872 | tf_op jit(solution)/shard_map/ppermute | solution.py:770
  217.3 24.0 %collective-permute-start.24 = (bf16[2,128,1024]{2,1,0:T(8,128)(2,1)}, bf16[2,128,1024]{2,1,0:T(8,128)(2,1)S(1)}, u32[]{:S(2)}, u32[]{:S(2)}) collective-permute-start(bf16[2,128,1024]{2,1,0:T(8,128)(2,1)} %get-tuple-element.136), channel_id=1, source_target_pairs={{0,12},{2,6},{4,8},{6,2},{8,4},{10,14},{12,0},{14,10},{1,13},{3,7}... | collective-permute-start | bytes 1572872 | tf_op jit(solution)/shard_map/ppermute | solution.py:770
  267.8 24.5 %collective-permute-start.29 = (bf16[2,2,384,512]{3,2,1,0:T(8,128)(2,1)S(1)}, bf16[2,2,384,512]{3,2,1,0:T(8,128)(2,1)S(1)}, u32[]{:S(2)}, u32[]{:S(2)}) collective-permute-start(bf16[2,2,384,512]{3,2,1,0:T(8,128)(2,1)S(1)} %copy-done.32), channel_id=1, source_target_pairs={{0,16},{2,50},{16,0},{18,34},{32,48},{34,18},{48,32},{50,2},{1,17}... | collective-permute-start | bytes 4718600 | tf_op jit(solution)/shard_map/ppermute | solution.py:770
  295.7 21.2 %collective-permute-start.34 = (bf16[2,384,512]{2,1,0:T(8,128)(2,1)}, bf16[2,384,512]{2,1,0:T(8,128)(2,1)S(1)}, u32[]{:S(2)}, u32[]{:S(2)}) collective-permute-start(bf16[2,384,512]{2,1,0:T(8,128)(2,1)} %shard_map.369.refs_4_), channel_id=1, source_target_pairs={{0,48},{2,18},{16,32},{18,2},{32,16},{34,50},{48,0},{50,34},{1,49}... | collective-permute-start | bytes 2359304 | tf_op jit(solution)/shard_map/ppermute | solution.py:770
  300.7 13.6 %collective-permute-start.28 = (bf16[2,2,32,1024]{3,2,1,0:T(8,128)(2,1)S(1)}, bf16[2,2,32,1024]{3,2,1,0:T(8,128)(2,1)S(1)}, u32[]{:S(2)}, u32[]{:S(2)}) collective-permute-start(bf16[2,2,32,1024]{3,2,1,0:T(8,128)(2,1)S(1)} %copy-done.69), channel_id=1, source_target_pairs={{0,16},{2,50},{16,0},{18,34},{32,48},{34,18},{48,32},{50,2},{1,17}... | collective-permute-start | bytes 786440 | tf_op jit(solution)/shard_map/ppermute | solution.py:770
  322.8 10.5 %collective-permute-start.36 = (bf16[2,2,96,512]{3,2,1,0:T(8,128)(2,1)}, bf16[2,2,96,512]{3,2,1,0:T(8,128)(2,1)S(1)}, u32[]{:S(2)}, u32[]{:S(2)}) collective-permute-start(bf16[2,2,96,512]{3,2,1,0:T(8,128)(2,1)} %get-tuple-element.152.refs_2_), channel_id=1, source_target_pairs={{0,4},{2,14},{4,0},{6,10},{8,12},{10,6},{12,8},{14,2},{1,5},{3,15}... | collective-permute-start | bytes 1179656 | tf_op jit(solution)/shard_map/ppermute | solution.py:770
  326.6 10.1 %collective-permute-start.32 = (bf16[2,32,1024]{2,1,0:T(8,128)(2,1)S(1)}, bf16[2,32,1024]{2,1,0:T(8,128)(2,1)S(1)}, u32[]{:S(2)}, u32[]{:S(2)}) collective-permute-start(bf16[2,32,1024]{2,1,0:T(8,128)(2,1)S(1)} %copy-done.53), channel_id=1, source_target_pairs={{0,12},{2,6},{4,8},{6,2},{8,4},{10,14},{12,0},{14,10},{1,13},{3,7}... | collective-permute-start | bytes 393224 | tf_op jit(solution)/shard_map/ppermute | solution.py:770
  326.7 10.0 %collective-permute-start.33 = (bf16[2,32,1024]{2,1,0:T(8,128)(2,1)S(1)}, bf16[2,32,1024]{2,1,0:T(8,128)(2,1)S(1)}, u32[]{:S(2)}, u32[]{:S(2)}) collective-permute-start(bf16[2,32,1024]{2,1,0:T(8,128)(2,1)S(1)} %copy-done.70), channel_id=1, source_target_pairs={{0,48},{2,18},{16,32},{18,2},{32,16},{34,50},{48,0},{50,34},{1,49}... | collective-permute-start | bytes 393224 | tf_op jit(solution)/shard_map/ppermute | solution.py:770
  369.6 11.0 %collective-permute-start.43 = (bf16[4,112,512]{2,1,0:T(8,128)(2,1)S(1)}, bf16[4,112,512]{2,1,0:T(8,128)(2,1)S(1)}, u32[]{:S(2)}, u32[]{:S(2)}) collective-permute-start(bf16[4,112,512]{2,1,0:T(8,128)(2,1)S(1)} %get-tuple-element.175.refs_9_), channel_id=1, source_target_pairs={{0,4},{2,14},{4,0},{6,10},{8,12},{10,6},{12,8},{14,2},{1,5},{3,15}... | collective-permute-start | bytes 1376264 | tf_op jit(solution)/shard_map/ppermute | solution.py:770
  380.7 21.2 %collective-permute-start.44 = (bf16[2,4,112,512]{3,2,1,0:T(8,128)(2,1)S(1)}, bf16[2,4,112,512]{3,2,1,0:T(8,128)(2,1)S(1)}, u32[]{:S(2)}, u32[]{:S(2)}) collective-permute-start(bf16[2,4,112,512]{3,2,1,0:T(8,128)(2,1)S(1)} %pad_maximum_fusion.7.refs_11_), channel_id=1, source_target_pairs={{0,12},{2,6},{4,8},{6,2},{8,4},{10,14},{12,0},{14,10},{1,13},{3,7}... | collective-permute-start | bytes 2752520 | tf_op jit(solution)/shard_map/ppermute | solution.py:770
  385.9 9.3 %collective-permute-start.48 = (bf16[4,128,512]{2,1,0:T(8,128)(2,1)S(1)}, bf16[4,128,512]{2,1,0:T(8,128)(2,1)S(1)}, u32[]{:S(2)}, u32[]{:S(2)}) collective-permute-start(bf16[4,128,512]{2,1,0:T(8,128)(2,1)S(1)} %get-tuple-element.173.refs_8_), channel_id=1, source_target_pairs={{0,16},{2,50},{16,0},{18,34},{32,48},{34,18},{48,32},{50,2},{1,17}... | collective-permute-start | bytes 1572872 | tf_op jit(solution)/shard_map/ppermute | solution.py:770
  395.3 28.6 %collective-permute-start.49 = (bf16[2,4,128,512]{3,2,1,0:T(8,128)(2,1)S(1)}, bf16[2,4,128,512]{3,2,1,0:T(8,128)(2,1)S(1)}, u32[]{:S(2)}, u32[]{:S(2)}) collective-permute-start(bf16[2,4,128,512]{3,2,1,0:T(8,128)(2,1)S(1)} %pad_maximum_fusion.6.refs_10_), channel_id=1, source_target_pairs={{0,48},{2,18},{16,32},{18,2},{32,16},{34,50},{48,0},{50,34},{1,49}... | collective-permute-start | bytes 3145736 | tf_op jit(solution)/shard_map/ppermute | solution.py:770
  403.4 37.1 %collective-permute-start.45 = (bf16[4,4,112,512]{3,2,1,0:T(8,128)(2,1)}, bf16[4,4,112,512]{3,2,1,0:T(8,128)(2,1)}, u32[]{:S(2)}, u32[]{:S(2)}) collective-permute-start(bf16[4,4,112,512]{3,2,1,0:T(8,128)(2,1)} %pad_maximum_fusion.3.refs_0_), channel_id=1, source_target_pairs={{0,2},{2,0},{1,3},{3,1},{4,6},{6,4},{5,7},{7,5},{8,10},{10,8},{9,1... | collective-permute-start | bytes 5505032 | tf_op jit(solution)/shard_map/ppermute | solution.py:758
  424.2 18.6 %collective-permute-start.50 = (bf16[4,4,128,512]{3,2,1,0:T(8,128)(2,1)S(1)}, bf16[4,4,128,512]{3,2,1,0:T(8,128)(2,1)}, u32[]{:S(2)}, u32[]{:S(2)}) collective-permute-start(bf16[4,4,128,512]{3,2,1,0:T(8,128)(2,1)S(1)} %pad_maximum_fusion.2.refs_0_), channel_id=1, source_target_pairs={{0,2},{2,0},{1,3},{3,1},{4,6},{6,4},{5,7},{7,5},{8,10},{10,8},{9,1... | collective-permute-start | bytes 6291464 | tf_op jit(solution)/shard_map/ppermute | solution.py:758
  (92 other events, 746.1 us)
Sparse Core Ops, SparseCore 0:
  19.1 63.1 all-gather.4
  267.9 68.5 all-gather.6

commit v2 on v1

--- a/solution.py
+++ b/solution.py
@@ -40,10 +40,17 @@
 
 class Line:
     def __init__(self):
-        self.held = []
+        self.held, self.due = [], {}
 
     def hold(self, *values):
         self.held += values
+
+    def expect(self, gap, *values):
+        self.due.setdefault(gap, []).extend(values)
+
+    def ran(self, result):
+        self.held = [result, *self.due.get(1, [])]
+        self.due = {gap - 1: values for gap, values in self.due.items() if gap > 1}
 
     def later(self, value):
         return lax.optimization_barrier((value, *self.held))[0] if self.held else value
@@ -69,9 +76,21 @@
             scratch_shapes=list(scratch),
         ),
         compiler_params=pltpu.CompilerParams(vmem_limit_bytes=56 << 20),
+        cost_estimate=pl.CostEstimate(flops=1, bytes_accessed=1, transcendentals=0),
     )(scalars, *args, *held)
-    line.held = [jax.tree.leaves(result)[0]]
+    line.ran(jax.tree.leaves(result)[0])
     return result
+
+
+def gate(value, *after):
+    anywhere = pl.BlockSpec(memory_space=pl.ANY)
+    return pl.pallas_call(
+        lambda *refs: None,
+        out_shape=jax.ShapeDtypeStruct(value.shape, value.dtype),
+        in_specs=[anywhere] * (1 + len(after)),
+        out_specs=anywhere,
+        input_output_aliases={0: 0},
+    )(value, *after)
 
 
 def whole(a):
@@ -721,39 +740,6 @@
     ).reshape(rows, columns)
 
 
-def widen_near(own, twin, start, rows, columns, swapped, scalars):
-    chunks = columns // 2 // STEP
-    u = rows // 16
-
-    def kernel(s, own, twin, out):
-        def fill(src, base):
-            for a in range(4):
-                for b in range(4):
-                    first, second = s[base + a], s[base + 4 + b]
-                    place = second * 4 + first if swapped else first * 4 + second
-                    for k in range(chunks):
-                        value = src[a, b, start + k * u : start + (k + 1) * u, :].astype(f32)
-                        out[pl.ds(place, 1), :, k * STEP : (k + 1) * STEP] = value[None]
-
-        @pl.when(pl.program_id(0) == 0)
-        def _():
-            fill(own, 1)
-
-        @pl.when(pl.program_id(0) == 1)
-        def _():
-            fill(twin, 9)
-
-    return call(
-        kernel,
-        shape((16, u, columns), f32),
-        (2,),
-        [whole(own), whole(twin)],
-        pl.BlockSpec((16, u, chunks * STEP), lambda h, s: (0, 0, lax.rem(h + s[0], 2))),
-        scalars,
-        (own, twin),
-    ).reshape(rows, columns)
-
-
 def core_swap(v):
     return lax.ppermute(v, "c", [(0, 1), (1, 0)])
 
@@ -839,6 +825,14 @@
         f.ring = f.other
         f.keep = out[2 * i + 1]
         f.got = exchange(out[2 * i], f.ring, (1, 3))
+
+
+def add(a, b, none):
+    def kernel(_, a, b, out):
+        out[...] = (a[...].astype(f32) + b[...].astype(f32)).astype(bf16)
+
+    out = shape(a.shape, bf16)
+    return call(kernel, out, (1,), [whole(a), whole(b)], whole(out), none, (a, b))
 
 
 class Finish:
@@ -886,40 +880,12 @@
         )
         self.got = exchange(send, "y", (1, 3))
 
-    def second(self):
-        self.mine = (self.mine + self.got.astype(f32)).astype(bf16)
+    def second(self, none):
+        self.mine = add(self.mine, self.got, none)
         self.far = lax.ppermute(self.mine, "yh", [(0, 1), (1, 0)])
-        line.hold(self.mine)
-
-    def done(self):
-        return (self.mine.astype(f32) + self.far.astype(f32)).astype(bf16)
-
-
-class Spread:
-    def __init__(self, v, rings):
-        self.rings = rings
-        self.v = v
-        self.got = exchange(v, rings[0], (1, 3))
-        line.hold(v)
-
-    def second(self, ring=None):
-        pair = jnp.stack([self.v, self.got])
-        self.v = pair
-        self.got = exchange(pair, ring or self.rings[0], (3, 1))
-        line.hold(pair)
-
-    def third(self):
-        four = jnp.concatenate([self.v, self.got])
-        self.v = four
-        self.got = exchange(four, self.rings[1], (1, 3))
-        line.hold(four)
-
-    def fourth(self):
-        self.second(self.rings[1])
-
-    def done(self):
-        all_ = jnp.concatenate([self.v, self.got])
-        return all_, core_swap(all_)
+
+    def gather(self, none):
+        return lax.all_gather(add(self.mine, self.far, none), ("c", "x", "z"), axis=0)
 
 
 def per_device(
@@ -944,7 +910,7 @@
     conv_w,
     conv_b,
 ):
-    line.held = []
+    line.held, line.due = [], {}
     tokens, memory, compressed, cotangent = tokens[0], memory[0], compressed[0], cotangent[0]
     yl, core = lax.axis_index("yl"), lax.axis_index("c")
     place = {"x": lax.axis_index("x"), "z": lax.axis_index("z")}
@@ -992,9 +958,11 @@
 
     normed, normed_rel, oldest = first_norm(compressed, memory, tokens, vectors, thirds_d)
     both_normed, both_oldest, both_cot = both(normed), both(oldest), both(cotangent)
+    kv_got = gate(kv_got, normed)
     kv_whole = joined(w_kv, kv_got, core_swap(kv_got))
     key_value = dot(normed_rel, kv_whole).astype(bf16)
     line.hold(key_value)
+    small_got = gate(small_got, key_value)
     small_twin = core_swap(small_got)
     q_whole, r_whole, o_whole = [
         joined(w, small_got[i], small_twin[i]) for i, w in enumerate((w_q, w_r, w_o))
@@ -1053,29 +1021,29 @@
             ),
         ]
     )
-    onward(large, none)
     loss, d_ck, d_cv = reconstruct(queries, key_value, comp_pair, none)
     recon_loss = jnp.sum(loss) / (T * D)
+    onward(large, none)
     d_compact, d_conv_b = compress_back(d_ck, d_cv, kv_whole, compact, vectors, thirds_d)
     both_compact = both(d_compact)
-    turn(large, cuts)
     onward(near, none)
     conv = flows([("x", [(both_oldest, 0, T // 3, both_compact, False)])])
+    turn(large, cuts)
+    turn(near, cuts)
+    line.expect(1, *[f.got for f in near])
     d_tokens, d_ln1_g, d_ln1_b = first_norm_back(
         d_kv, d_queries, kv_whole, q_whole, compressed, memory, tokens, vectors, d_residual,
         thirds_d,
     )
     onward(large, none)
-    turn(near, cuts)
-    early = Finish(large, [], ints(yl))
     onward(conv, none)
     onward(near, none)
-    early.second()
+    line.expect(2, *[f.last for f in near])
+    early = Finish(large, [], ints(yl))
     turn(conv, cuts)
-    early_done = early.done()
-    line.hold(early_done)
-    early_sums = lax.all_gather(early_done, ("c", "x", "z"), axis=0)
+    early.second(none)
     onward(conv, none)
+    early_sums = early.gather(none)
 
     total = jnp.concatenate(
         [d_ln1_g, d_ln1_b, d_bias_u, d_bias_v, d_ln2_g, d_ln2_b, d_b_out, d_conv_b]
@@ -1090,35 +1058,17 @@
         axis=1,
     )
     late = Finish([*near, *conv], [total], ints(yl))
-    late.second()
-    late_done = late.done()
-    one = Spread(late_done[:128], ("z", "x"))
-    two = Spread(late_done[128:], ("x", "z"))
-    one.second()
-    two.second()
-    one.third()
-    two.third()
-    one.fourth()
-    two.fourth()
-    (one_own, one_twin), (two_own, two_twin) = one.done(), two.done()
-    x_places, z_places = rels
-    x_twin, z_twin = twins
-    along = ints(core, *x_places, *z_places, *x_twin, *z_twin)
-    across = ints(core, *z_places, *x_places, *z_twin, *x_twin)
-    g_kv = widen_near(one_own, one_twin, 0, D // 2, 2 * D, False, along)
-    g_q = widen_near(one_own, one_twin, 64, D // 2, D, True, along)
-    g_r = widen_near(one_own, one_twin, 96, D // 2, D, True, along)
-    g_conv = widen_near(two_own, two_twin, 0, 3 * D // 2, D, True, across)
+    late.second(none)
+    late_sums = late.gather(none)
+
+    g_in = widen(early_sums, 128, D // 2, FF, True, none)
     g_out = widen(early_sums, 0, FF // 2, D, False, none)
-    g_in = widen(early_sums, 128, D // 2, FF, True, none)
     g_o = widen(early_sums, 256, D // 2, D, True, none)
-
-    def four(v):
-        return (v[0] + v[1]) + (v[2] + v[3])
-
-    half = four(four(two_own[:, :, 96:108].astype(f32))) + four(
-        four(two_twin[:, :, 96:108].astype(f32))
-    )
+    g_conv = widen(late_sums, 128, 3 * D // 2, D, False, none)
+    g_kv = widen(late_sums, 0, D // 2, 2 * D, False, none)
+    g_q = widen(late_sums, 64, D // 2, D, True, none)
+    g_r = widen(late_sums, 96, D // 2, D, True, none)
+    half = jnp.sum(late_sums[:, 224:236].astype(f32), axis=0)
     t_ln1_g, t_ln1_b, t_bu, t_bv, t_ln2_g, t_ln2_b, t_bout, t_convb = [half[i] for i in range(8)]
     t_bin = half[8:].reshape(-1)
     return (

time: 490 us -> 424 us (0.87)
  starting transfers between devices: 94.1 us -> 38.2 us
  waiting for transfers between devices: 134 us -> 122 us
    ppermute x33 -> x25, waiting for transfers between devices: 121 us -> 41.9 us  [exchange(): return lax.ppermute(v, RING[ring], pairs)]
    all_gather x1 -> x2, waiting for transfers between devices: 0.01 us -> 67.6 us  [gather(): lax.all_gather(add(self.mine, self.far, none), ('c', 'x', 'z'), axis=0)]
    ppermute x16 -> x14, starting transfers between devices: 41.2 us -> 4.84 us  [core_swap(): return lax.ppermute(v, 'c', [(0, 1), (1, 0)])]
    ppermute x33 -> x25, starting transfers between devices: 50.7 us -> 33.2 us  [exchange(): return lax.ppermute(v, RING[ring], pairs)]
    convert_element_type x6 -> x0, other arithmetic: 5.12 us -> none  [the longest x2 2.26 us: second(): self.mine = (self.mine + self.got.astype(f32)).astype(bf16)]
    concatenate x2 -> x3, other arithmetic: 2.98 us -> 7.95 us  [joined(): return jnp.concatenate([w, got, twin], axis=0)]
    unnamed x146 -> x144, local copies, waits for them, and re-layouts: 15.8 us -> 17.8 us
    pallas_call x34 -> x38, Pallas kernels: 185 us -> 187 us  [call(): pl.pallas_call(body, out_shape=out, grid_spec=pltpu.PrefetchScalarGridSpe...]
  transfers between devices with their start and end apart: 53 -> 44, of which waited for: 20 -> 15; matrix products, arithmetic and copies ran while one was open for 8% -> 8% of each run, Pallas kernels for 27% -> 33%
where the time goes in v2:
time: 424 us; the launch traced here: 416 us
  Pallas kernels  187 us (44%)
  waiting for transfers between devices  122 us (29%)
  starting transfers between devices  38.2 us (9%)
  local copies, waits for them, and re-layouts  22.4 us (5%)
  other arithmetic  19.6 us (5%)
  between operations  16.4 us (4%)
  matrix products  10.6 us (2%)
    pallas_call x38, Pallas kernels, call(): pl.pallas_call(body, out_shape=out, grid_spec=pltpu.PrefetchScalarGridSpe...  187 us
    all_gather x2, waiting for transfers between devices, gather(): lax.all_gather(add(self.mine, self.far, none), ('c', 'x', 'z'), axis=0)  67.6 us
    ppermute x25, waiting for transfers between devices, exchange(): return lax.ppermute(v, RING[ring], pairs)  41.9 us
    ppermute x25, starting transfers between devices, exchange(): return lax.ppermute(v, RING[ring], pairs)  33.2 us
    unnamed x144, local copies, waits for them, and re-layouts  17.8 us
    dot_general x4, matrix products, dot(): return jnp.dot(a, b, preferred_element_type=f32)  10.6 us
  transfers between devices with their start and end apart: 44, of which 15 were waited for; matrix products, arithmetic and copies ran while one was open for 8% of the time, Pallas kernels for 33%

profile of v2, /device:TPU:1, one launch (start us, length us, event | category | flops | bytes accessed | tf_op | source)
XLA Modules:
  0.0 416.1 jit_solution(13111200470358027871)
XLA Ops:
  12.8 5.4 %collective-permute-done.refs_1_ = bf16[192,1024]{1,0:T(8,128)(2,1)S(1)} collective-permute-done((bf16[192,1024]{1,0:T(8,128)(2,1)}, bf16[192,1024]{1,0:T(8,128)(2,1)S(1)}, u32[]{:S(2)}, u32[]{:S(2)}) %collective-permute-start) | collective-permute-done | bytes 393248 | tf_op jit(solution)/shard_map/ppermute | solution.py:756
  25.5 4.7 %fusion.10 = (bf16[576,512]{1,0:T(8,128)(2,1)S(1)}, bf16[576,512]{1,0:T(8,128)(2,1)S(1)}) fusion(f32[512]{0:T(512)S(1)} %negate_power_fusion, f32[576]{0:T(1024)S(1)} %subtract_convert_fusion), kind=kLoop, calls=%fused_computation.22 | loop fusion | flops 884736 | bytes 1184000 | tf_op jit(solution)/shard_map/convert.1
  33.9 4.5 %shard_map.350 = (bf16[576,1024]{1,0:T(8,128)(2,1)}, bf16[576,1024]{1,0:T(8,128)(2,1)}, bf16[64,3072]{1,0:T(8,128)(2,1)}) custom-call(s32[3]{0:T(128)} %pad_add_fusion.s, f32[192,1024]{1,0:T(8,128)} %bitcast.90, f32[192,1024]{1,0:T(8,128)} %bitcast.99, bf16[192,1024]{1,0:T(8,128)(2,1)} %bitcast.96, ...), custom_call_target="tpu_custom_call" | custom-call | flops 1 | bytes 1 | tf_op jit(solution)/shard_map/pallas_call | solution.py:68
  41.4 5.0 %pad_maximum_fusion.refs_2_ = bf16[1024,2048]{1,0:T(8,128)(2,1)S(1)} fusion(bf16[256,2048]{1,0:T(8,128)(2,1)S(1)} %collective-permute-done.3, bf16[256,2048]{1,0:T(8,128)(2,1)} %shard_map.351, bf16[512,2048]{1,0:T(8,128)(2,1)S(1)} %copy-done.4), kind=kLoop, calls=%fused_computation | loop fusion | flops 12582912 | bytes 8388608 | tf_op jit(solution)/shard_map/concatenate | solution.py:943
  46.4 3.8 convolution_convert_fusion.refs_1_.refs_2_.refs_6_
  50.2 9.5 %collective-permute-done.1.refs_0_ = bf16[3,256,1024]{2,1,0:T(8,128)(2,1)} collective-permute-done((bf16[3,256,1024]{2,1,0:T(8,128)(2,1)}, bf16[3,256,1024]{2,1,0:T(8,128)(2,1)}, u32[]{:S(2)}, u32[]{:S(2)}) %collective-permute-start.1) | collective-permute-done | bytes 1572896 | tf_op jit(solution)/shard_map/ppermute | solution.py:756
  69.0 7.7 %shard_map.353 = (f32[8,192,640]{2,1,0:T(8,128)}, bf16[192,1024]{1,0:T(8,128)(2,1)}) custom-call(s32[1]{0:T(128)} %constant.10.clone.1.s, f32[192,1024]{1,0:T(8,128)} %fusion.12.refs_0_.refs_7_, bf16[576,2048]{1,0:T(8,128)(2,1)} %convolution_convert_fusion.refs_1_.refs_2_.refs_6_, bf16[576,2048]{1,0:T(8,128)(2,1)} %convolution_convert_fusion.refs_1_.refs_2_.refs_6_, ...), custom_call_target="tpu_custom_call" | custom-call | flops 1 | bytes 1 | tf_op jit(solution)/shard_map/pallas_call | solution.py:68
  78.2 4.1 shard_map.354
  82.3 18.2 %shard_map.355 = (bf16[192,4096]{1,0:T(8,128)(2,1)}, bf16[192,4096]{1,0:T(8,128)(2,1)}, bf16[192,1024]{1,0:T(8,128)(2,1)}, f32[192,1024]{1,0:T(8,128)}, f32[4,1024]{1,0:T(4,128)}) custom-call(s32[1]{0:T(128)} %bitcast.s, bf16[192,1024]{1,0:T(8,128)(2,1)} %get-tuple-element.99.refs_0_, f32[192,1024]{1,0:T(8,128)} %get-tuple-element.100.refs_1_.refs_9_.refs_2_, ...), custom_call_target="tpu_custom_call" | custom-call | flops 1 | bytes 1 | tf_op jit(solution)/shard_map/pallas_call | solution.py:68
  102.0 5.0 %shard_map.356 = (f32[192,1024]{1,0:T(8,128)}, bf16[192,1024]{1,0:T(8,128)(2,1)}, bf16[192,1024]{1,0:T(8,128)(2,1)}, f32[1,1024]{1,0:T(1,128)}, f32[1,1024]{1,0:T(1,128)}, /*index=5*/f32[1,1024]{1,0:T(1,128)}) custom-call(s32[3]{0:T(128)} %pad_add_fusion.s, bf16[192,1024]{1,0:T(8,128)(2,1)} %bitcast.93, f32[192,1024]{1,0:T(8,128)} %get-tuple-element.104.refs_1_, ...), custom_call_target="tpu_custom_call" | custom-call | flops 1 | bytes 1 | tf_op jit(solution)/shard_map/pallas_call | solution.py:68
  111.3 11.6 %shard_map.357 = (bf16[2,2,512,512]{3,2,1,0:T(8,128)(2,1)}, bf16[2,2,512,512]{3,2,1,0:T(8,128)(2,1)}, bf16[2,2,128,2560]{3,2,1,0:T(8,128)(2,1)}, bf16[2,2,128,2560]{3,2,1,0:T(8,128)(2,1)}) custom-call(s32[9]{0:T(128)} %stack.83.s, bf16[192,4096]{1,0:T(8,128)(2,1)} %get-tuple-element.105.refs_5_.refs_0_.refs_1_, ...), custom_call_target="tpu_custom_call" | custom-call | flops 1 | bytes 1 | tf_op jit(solution)/shard_map/pallas_call | solution.py:68
  122.9 4.3 %collective-permute-start.18 = (bf16[2,2,128,2560]{3,2,1,0:T(8,128)(2,1)}, bf16[2,2,128,2560]{3,2,1,0:T(8,128)(2,1)}, u32[]{:S(2)}, u32[]{:S(2)}) collective-permute-start(bf16[2,2,128,2560]{3,2,1,0:T(8,128)(2,1)} %get-tuple-element.128), channel_id=1, source_target_pairs={{0,4},{2,14},{4,0},{6,10},{8,12},{10,6},{12,8},{14,2},{1,5},{3,15}... | collective-permute-start | bytes 7864328 | tf_op jit(solution)/shard_map/ppermute | solution.py:756
  129.5 11.4 %shard_map.358 = (bf16[2,576,1024]{2,1,0:T(8,128)(2,1)}, bf16[576,1024]{1,0:T(8,128)(2,1)}, bf16[576,1024]{1,0:T(8,128)(2,1)}, bf16[576,1024]{1,0:T(8,128)(2,1)}...) custom-call(s32[1]{0:T(128)} %bitcast.8.s, f32[192,1024]{1,0:T(8,128)} %fusion.12.refs_0_.refs_7_, ...), custom_call_target="tpu_custom_call" | custom-call | flops 1 | bytes 1 | tf_op jit(solution)/shard_map/pallas_call | solution.py:68
  143.7 6.0 %shard_map.359 = (f32[64,1024]{1,0:T(8,128)}, bf16[64,1024]{1,0:T(8,128)(2,1)}) custom-call(s32[5]{0:T(128)} %stack.74.s, bf16[64,3072]{1,0:T(8,128)(2,1)} %get-tuple-element.103.refs_0_.refs_1_, bf16[1536,1024]{1,0:T(8,128)(2,1)} %refs_1_.5, bf16[32,176,1024]{2,1,0:T(8,128)(2,1)} %bitcast.75, bf16[32,176,1024]{2,1,0:T(8,128)(2,1)} %bitcast.76, ...), custom_call_target="tpu_custom_call" | custom-call | flops 1 | bytes 1 | tf_op jit(solution)/shard_map/pallas_call | solution.py:68
  150.7 11.2 %shard_map.360 = (bf16[2,2,128,1024]{3,2,1,0:T(8,128)(2,1)}, bf16[2,2,128,1024]{3,2,1,0:T(8,128)(2,1)}, bf16[2,2,128,1024]{3,2,1,0:T(8,128)(2,1)}, bf16[2,2,128,1024]{3,2,1,0:T(8,128)(2,1)}) custom-call(s32[9]{0:T(128)} %stack.83.s, bf16[576,1024]{1,0:T(8,128)(2,1)} %get-tuple-element.96.refs_1_.refs_5_.refs_0_.refs_6_.refs_7_, ...), custom_call_target="tpu_custom_call" | custom-call | flops 1 | bytes 1 | tf_op jit(solution)/shard_map/pallas_call | solution.py:68
  165.3 8.4 %shard_map.361 = (f32[1,128]{1,0:T(1,128)}, bf16[64,1024]{1,0:T(8,128)(2,1)}, bf16[64,1024]{1,0:T(8,128)(2,1)}) custom-call(s32[1]{0:T(128)} %constant.10.clone.1.s, f32[192,1024]{1,0:T(8,128)} %fusion.12.refs_0_.refs_7_, bf16[576,2048]{1,0:T(8,128)(2,1)} %convolution_convert_fusion.refs_1_.refs_2_.refs_6_, ...), custom_call_target="tpu_custom_call" | custom-call | flops 1 | bytes 1 | tf_op jit(solution)/shard_map/pallas_call | solution.py:68
  180.2 5.3 %shard_map.363 = (bf16[64,1024]{1,0:T(8,128)(2,1)}, f32[1,1024]{1,0:T(1,128)}) custom-call(s32[3]{0:T(128)} %pad_add_fusion.s, bf16[64,1024]{1,0:T(8,128)(2,1)} %get-tuple-element.124.refs_0_, bf16[64,1024]{1,0:T(8,128)(2,1)} %get-tuple-element.125.refs_1_, bf16[1024,2048]{1,0:T(8,128)(2,1)} %copy-done, f32[64,1024]{1,0:T(8,128)} %get-tuple-element.113.refs_18_.refs_3_, ...), custom_call_target="tpu_custom_call" | custom-call | flops 1 | bytes 1 | tf_op jit(solution)/shard_map/pallas_call | solution.py:68
  190.3 5.4 %shard_map.365 = (bf16[2,2,384,512]{3,2,1,0:T(8,128)(2,1)}, bf16[2,2,384,512]{3,2,1,0:T(8,128)(2,1)}) custom-call(s32[9]{0:T(128)} %stack.83.s, bf16[64,3072]{1,0:T(8,128)(2,1)} %get-tuple-element.103.refs_0_.refs_1_, bf16[64,3072]{1,0:T(8,128)(2,1)} %get-tuple-element.103.refs_0_.refs_1_, bf16[64,3072]{1,0:T(8,128)(2,1)} %copy-done.27, ...), custom_call_target="tpu_custom_call" | custom-call | flops 1 | bytes 1 | tf_op jit(solution)/shard_map/pallas_call | solution.py:68
  199.6 6.0 %shard_map.366 = (bf16[2,2,128,512]{3,2,1,0:T(8,128)(2,1)}, f32[2,2,128,512]{3,2,1,0:T(8,128)}, bf16[2,2,32,2560]{3,2,1,0:T(8,128)(2,1)}, f32[2,2,32,2560]{3,2,1,0:T(8,128)}) custom-call(s32[9]{0:T(128)} %stack.83.s, bf16[2,2,512,512]{3,2,1,0:T(8,128)(2,1)} %get-tuple-element.126.refs_0_, bf16[2,2,512,512]{3,2,1,0:T(8,128)(2,1)} %collective-permute-done.17.refs_1_, ...), custom_call_target="tpu_custom_call" | custom-call | flops 1 | bytes 1 | tf_op jit(solution)/shard_map/pallas_call | solution.py:68
  212.8 4.8 %shard_map.367 = (bf16[2,2,32,1024]{3,2,1,0:T(8,128)(2,1)}, f32[2,2,32,1024]{3,2,1,0:T(8,128)}, bf16[2,2,32,1024]{3,2,1,0:T(8,128)(2,1)}, f32[2,2,32,1024]{3,2,1,0:T(8,128)}) custom-call(s32[9]{0:T(128)} %stack.83.s, bf16[2,2,128,1024]{3,2,1,0:T(8,128)(2,1)} %get-tuple-element.121.refs_0_, bf16[2,2,128,1024]{3,2,1,0:T(8,128)(2,1)} %copy-done.8, ...), custom_call_target="tpu_custom_call" | custom-call | flops 1 | bytes 1 | tf_op jit(solution)/shard_map/pallas_call | solution.py:68
  221.6 10.7 %shard_map.368 = (f32[192,1024]{1,0:T(8,128)}, f32[1,1024]{1,0:T(1,128)}, f32[1,1024]{1,0:T(1,128)}) custom-call(s32[3]{0:T(128)} %pad_add_fusion.s, bf16[2,576,1024]{2,1,0:T(8,128)(2,1)} %get-tuple-element.112.refs_6_.refs_0_, bf16[192,1024]{1,0:T(8,128)(2,1)} %get-tuple-element.117.refs_10_.refs_1_, bf16[1024,2048]{1,0:T(8,128)(2,1)} %copy-done, ...), custom_call_target="tpu_custom_call" | custom-call | flops 1 | bytes 1 | tf_op jit(solution)/shard_map/pallas_call | solution.py:68
  246.0 7.9 %collective-permute-done.34.refs_5_ = bf16[2,32,2560]{2,1,0:T(8,128)(2,1)S(1)} collective-permute-done((bf16[2,32,2560]{2,1,0:T(8,128)(2,1)S(1)}, bf16[2,32,2560]{2,1,0:T(8,128)(2,1)S(1)}, u32[]{:S(2)}, u32[]{:S(2)}) %collective-permute-start.34) | collective-permute-done | bytes 327712 | tf_op jit(solution)/shard_map/ppermute | solution.py:756
  261.1 4.6 %shard_map.373 = (bf16[2,2,96,512]{3,2,1,0:T(8,128)(2,1)}, f32[2,2,96,512]{3,2,1,0:T(8,128)}) custom-call(s32[9]{0:T(128)} %stack.83.s, bf16[2,2,384,512]{3,2,1,0:T(8,128)(2,1)} %get-tuple-element.141.refs_0_, bf16[2,2,384,512]{3,2,1,0:T(8,128)(2,1)} %copy-done.6, bf16[2,384,512]{2,1,0:T(8,128)(2,1)} %copy-done.39, bf16[288,512]{1,0:T(8,128)(2,1)} %get-tuple-element.149.refs_3_), custom_call_target="tpu_custom_call" | custom-call | flops 1 | bytes 1 | tf_op jit(solution)/shard_map/pallas_call | solution.py:68
  269.8 3.9 collective-permute-done.35.refs_1_.refs_7_
  281.5 4.0 collective-permute-done.37.refs_8_
  288.8 6.5 %collective-permute-done.39.refs_1_ = bf16[240,512]{1,0:T(8,128)(2,1)S(1)} collective-permute-done((bf16[240,512]{1,0:T(8,128)(2,1)}, bf16[240,512]{1,0:T(8,128)(2,1)S(1)}, u32[]{:S(2)}, u32[]{:S(2)}) %collective-permute-start.39) | collective-permute-done | bytes 245792 | tf_op jit(solution)/shard_map/ppermute | solution.py:756
  297.8 6.8 %collective-permute-done.40.refs_1_ = bf16[240,512]{1,0:T(8,128)(2,1)S(1)} collective-permute-done((bf16[240,512]{1,0:T(8,128)(2,1)}, bf16[240,512]{1,0:T(8,128)(2,1)S(1)}, u32[]{:S(2)}, u32[]{:S(2)}) %collective-permute-start.40) | collective-permute-done | bytes 245792 | tf_op jit(solution)/shard_map/ppermute | solution.py:885
  308.1 29.6 %all-gather.11.cloned.1.call-done = bf16[9216,512]{1,0:T(8,128)(2,1)} async-done(((bf16[288,512]{1,0:T(8,128)(2,1)}), bf16[9216,512]{1,0:T(8,128)(2,1)}) %all-gather.11.cloned.1.call-update) | async-done | bytes 9437200 | tf_op jit(solution)/shard_map/all_gather | solution.py:888
  337.7 5.2 %shard_map.380.refs_1_ = f32[16,32,4096]{2,1,0:T(8,128)} custom-call(s32[1]{0:T(128)} %constant.10.clone.1.s, bf16[32,288,512]{2,1,0:T(8,128)(2,1)} %bitcast.67, bf16[32,288,512]{2,1,0:T(8,128)(2,1)} %bitcast.68, bf16[32,288,512]{2,1,0:T(8,128)(2,1)} %bitcast.69, bf16[32,288,512]{2,1,0:T(8,128)(2,1)} %bitcast.70, bf16[240,512]{1,0:T(8,128)(2,1)} %shard_map.379.refs_4_), custom_call_target="tpu_custom_call" | custom-call | flops 1 | bytes 1 | tf_op jit(solution)/shard_map/pallas_call | solution.py:68
  343.5 7.3 %shard_map.381.refs_1_ = f32[16,128,1024]{2,1,0:T(8,128)} custom-call(s32[1]{0:T(128)} %constant.10.clone.1.s, bf16[32,288,512]{2,1,0:T(8,128)(2,1)} %bitcast.71, f32[16,32,4096]{2,1,0:T(8,128)} %shard_map.380.refs_1_), custom_call_target="tpu_custom_call" | custom-call | flops 1 | bytes 1 | tf_op jit(solution)/shard_map/pallas_call | solution.py:68
  353.9 38.0 %all-gather.9.cloned.1.call-done = bf16[7680,512]{1,0:T(8,128)(2,1)} async-done(((bf16[240,512]{1,0:T(8,128)(2,1)}), bf16[7680,512]{1,0:T(8,128)(2,1)}) %all-gather.9.cloned.1.call-update) | async-done | bytes 7864336 | tf_op jit(solution)/shard_map/all_gather | solution.py:888
  393.1 5.8 %shard_map.383.refs_2_ = f32[16,96,1024]{2,1,0:T(8,128)} custom-call(s32[1]{0:T(128)} %constant.10.clone.1.s, bf16[32,240,512]{2,1,0:T(8,128)(2,1)} %bitcast.79, f32[16,32,1024]{2,1,0:T(8,128)} %shard_map.382.refs_1_), custom_call_target="tpu_custom_call" | custom-call | flops 1 | bytes 1 | tf_op jit(solution)/shard_map/pallas_call | solution.py:68
  (273 shorter events, 127.3 us)
Async XLA Ops:
  7.2 75.1 %all-gather.7.cloned.1.call-start = ((), (), s32[]{:S(2)}) async-start(), calls=%async_computation | async-start | bytes 11894784 | tf_op jit(solution)/shard_map/all_gather | solution.py:945
  9.2 8.9 %collective-permute-start = (bf16[192,1024]{1,0:T(8,128)(2,1)}, bf16[192,1024]{1,0:T(8,128)(2,1)S(1)}, u32[]{:S(2)}, u32[]{:S(2)}) collective-permute-start(bf16[192,1024]{1,0:T(8,128)(2,1)} %shard_map.347.refs_4_.refs_0_), channel_id=1, source_target_pairs={{0,1},{2,67},{1,0},{3,66},{64,65},{66,3},{65,64},{67,2},{4,5},{6,7... | collective-permute-start | bytes 1179656 | tf_op jit(solution)/shard_map/ppermute | solution.py:756
  19.0 318.7 %all-gather.11.cloned.1.call-start = ((), (), s32[]{:S(2)}) async-start(), calls=%async_computation.2 | async-start | bytes 9732096 | tf_op jit(solution)/shard_map/all_gather | solution.py:888
  22.3 16.2 %collective-permute-start.2 = (bf16[256,2048]{1,0:T(8,128)(2,1)}, bf16[256,2048]{1,0:T(8,128)(2,1)}, u32[]{:S(2)}, u32[]{:S(2)}) collective-permute-start(bf16[256,2048]{1,0:T(8,128)(2,1)} %get-tuple-element.92.refs_2_), channel_id=1, source_target_pairs={{0,1},{2,67},{1,0},{3,66},{64,65},{66,3},{65,64},{67,2},{4,5},{6,7... | collective-permute-start | bytes 3145736 | tf_op jit(solution)/shard_map/ppermute | solution.py:756
  38.5 21.2 %collective-permute-start.1 = (bf16[3,256,1024]{2,1,0:T(8,128)(2,1)}, bf16[3,256,1024]{2,1,0:T(8,128)(2,1)}, u32[]{:S(2)}, u32[]{:S(2)}) collective-permute-start(bf16[3,256,1024]{2,1,0:T(8,128)(2,1)} %get-tuple-element.95), channel_id=1, source_target_pairs={{0,1},{2,67},{1,0},{3,66},{64,65},{66,3},{65,64},{67,2},{4,5},{6,7... | collective-permute-start | bytes 4718600 | tf_op jit(solution)/shard_map/ppermute | solution.py:756
  100.5 9.7 %collective-permute-start.5 = (bf16[192,4096]{1,0:T(8,128)(2,1)}, bf16[192,4096]{1,0:T(8,128)(2,1)S(1)}, u32[]{:S(2)}, u32[]{:S(2)}) collective-permute-start(bf16[192,4096]{1,0:T(8,128)(2,1)} %get-tuple-element.105.refs_5_.refs_0_.refs_1_), channel_id=1, source_target_pairs={{0,2},{2,0},{1,3},{3,1},{4,6},{6,4},{5,7},{7,5},{8,10},{10,8},{9,1... | collective-permute-start | bytes 4718600 | tf_op jit(solution)/shard_map/ppermute | solution.py:744
  101.0 9.2 %collective-permute-start.8 = (bf16[192,4096]{1,0:T(8,128)(2,1)}, bf16[192,4096]{1,0:T(8,128)(2,1)}, u32[]{:S(2)}, u32[]{:S(2)}) collective-permute-start(bf16[192,4096]{1,0:T(8,128)(2,1)} %get-tuple-element.108.refs_10_), channel_id=1, source_target_pairs={{0,2},{2,0},{1,3},{3,1},{4,6},{6,4},{5,7},{7,5},{8,10},{10,8},{9,1... | collective-permute-start | bytes 4718600 | tf_op jit(solution)/shard_map/ppermute | solution.py:744
  122.9 50.9 %collective-permute-start.18 = (bf16[2,2,128,2560]{3,2,1,0:T(8,128)(2,1)}, bf16[2,2,128,2560]{3,2,1,0:T(8,128)(2,1)}, u32[]{:S(2)}, u32[]{:S(2)}) collective-permute-start(bf16[2,2,128,2560]{3,2,1,0:T(8,128)(2,1)} %get-tuple-element.128), channel_id=1, source_target_pairs={{0,4},{2,14},{4,0},{6,10},{8,12},{10,6},{12,8},{14,2},{1,5},{3,15}... | collective-permute-start | bytes 7864328 | tf_op jit(solution)/shard_map/ppermute | solution.py:756
  127.2 14.3 %collective-permute-start.11 = (bf16[576,1024]{1,0:T(8,128)(2,1)S(1)}, bf16[576,1024]{1,0:T(8,128)(2,1)S(1)}, u32[]{:S(2)}, u32[]{:S(2)}) collective-permute-start(bf16[576,1024]{1,0:T(8,128)(2,1)S(1)} %copy-done.2), channel_id=1, source_target_pairs={{0,2},{2,0},{1,3},{3,1},{4,6},{6,4},{5,7},{7,5},{8,10},{10,8},{9,1... | collective-permute-start | bytes 3538952 | tf_op jit(solution)/shard_map/ppermute | solution.py:744
  127.2 46.5 %collective-permute-start.17 = (bf16[2,2,512,512]{3,2,1,0:T(8,128)(2,1)}, bf16[2,2,512,512]{3,2,1,0:T(8,128)(2,1)}, u32[]{:S(2)}, u32[]{:S(2)}) collective-permute-start(bf16[2,2,512,512]{3,2,1,0:T(8,128)(2,1)} %get-tuple-element.111.refs_7_), channel_id=1, source_target_pairs={{0,16},{2,50},{16,0},{18,34},{32,48},{34,18},{48,32},{50,2},{1,17}... | collective-permute-start | bytes 6291464 | tf_op jit(solution)/shard_map/ppermute | solution.py:756
  141.0 8.7 %collective-permute-start.12 = (bf16[576,1024]{1,0:T(8,128)(2,1)}, bf16[576,1024]{1,0:T(8,128)(2,1)S(1)}, u32[]{:S(2)}, u32[]{:S(2)}) collective-permute-start(bf16[576,1024]{1,0:T(8,128)(2,1)} %get-tuple-element.116), channel_id=1, source_target_pairs={{0,2},{2,0},{1,3},{3,1},{4,6},{6,4},{5,7},{7,5},{8,10},{10,8},{9,1... | collective-permute-start | bytes 3538952 | tf_op jit(solution)/shard_map/ppermute | solution.py:744
  141.2 8.6 %collective-permute-start.14 = (bf16[576,1024]{1,0:T(8,128)(2,1)}, bf16[576,1024]{1,0:T(8,128)(2,1)}, u32[]{:S(2)}, u32[]{:S(2)}) collective-permute-start(bf16[576,1024]{1,0:T(8,128)(2,1)} %get-tuple-element.118.refs_16_), channel_id=1, source_target_pairs={{0,2},{2,0},{1,3},{3,1},{4,6},{6,4},{5,7},{7,5},{8,10},{10,8},{9,1... | collective-permute-start | bytes 3538952 | tf_op jit(solution)/shard_map/ppermute | solution.py:744
  141.6 8.1 %collective-permute-start.13 = (bf16[192,1024]{1,0:T(8,128)(2,1)}, bf16[192,1024]{1,0:T(8,128)(2,1)}, u32[]{:S(2)}, u32[]{:S(2)}) collective-permute-start(bf16[192,1024]{1,0:T(8,128)(2,1)} %get-tuple-element.117.refs_10_.refs_1_), channel_id=1, source_target_pairs={{0,2},{2,0},{1,3},{3,1},{4,6},{6,4},{5,7},{7,5},{8,10},{10,8},{9,1... | collective-permute-start | bytes 1179656 | tf_op jit(solution)/shard_map/ppermute | solution.py:744
  162.0 23.5 %collective-permute-start.15 = (bf16[2,2,128,1024]{3,2,1,0:T(8,128)(2,1)}, bf16[2,2,128,1024]{3,2,1,0:T(8,128)(2,1)S(1)}, u32[]{:S(2)}, u32[]{:S(2)}) collective-permute-start(bf16[2,2,128,1024]{3,2,1,0:T(8,128)(2,1)} %get-tuple-element.119.refs_5_), channel_id=1, source_target_pairs={{0,16},{2,50},{16,0},{18,34},{32,48},{34,18},{48,32},{50,2},{1,17}... | collective-permute-start | bytes 3145736 | tf_op jit(solution)/shard_map/ppermute | solution.py:756
  163.7 22.4 %collective-permute-start.16 = (bf16[2,2,128,1024]{3,2,1,0:T(8,128)(2,1)}, bf16[2,2,128,1024]{3,2,1,0:T(8,128)(2,1)S(1)}, u32[]{:S(2)}, u32[]{:S(2)}) collective-permute-start(bf16[2,2,128,1024]{3,2,1,0:T(8,128)(2,1)} %get-tuple-element.123), channel_id=1, source_target_pairs={{0,4},{2,14},{4,0},{6,10},{8,12},{10,6},{12,8},{14,2},{1,5},{3,15}... | collective-permute-start | bytes 3145736 | tf_op jit(solution)/shard_map/ppermute | solution.py:756
  177.4 20.2 %collective-permute-start.22 = (bf16[2,128,2560]{2,1,0:T(8,128)(2,1)}, bf16[2,128,2560]{2,1,0:T(8,128)(2,1)S(1)}, u32[]{:S(2)}, u32[]{:S(2)}) collective-permute-start(bf16[2,128,2560]{2,1,0:T(8,128)(2,1)} %get-tuple-element.133), channel_id=1, source_target_pairs={{0,12},{2,6},{4,8},{6,2},{8,4},{10,14},{12,0},{14,10},{1,13},{3,7}... | collective-permute-start | bytes 3932168 | tf_op jit(solution)/shard_map/ppermute | solution.py:756
  178.1 11.3 %collective-permute-start.23 = (bf16[64,3072]{1,0:T(8,128)(2,1)S(1)}, bf16[64,3072]{1,0:T(8,128)(2,1)S(1)}, u32[]{:S(2)}, u32[]{:S(2)}) collective-permute-start(bf16[64,3072]{1,0:T(8,128)(2,1)S(1)} %copy-done.13), channel_id=1, source_target_pairs={{0,2},{2,0},{1,3},{3,1},{4,6},{6,4},{5,7},{7,5},{8,10},{10,8},{9,1... | collective-permute-start | bytes 1179656 | tf_op jit(solution)/shard_map/ppermute | solution.py:744
  179.2 18.3 %collective-permute-start.21 = (bf16[2,512,512]{2,1,0:T(8,128)(2,1)}, bf16[2,512,512]{2,1,0:T(8,128)(2,1)S(1)}, u32[]{:S(2)}, u32[]{:S(2)}) collective-permute-start(bf16[2,512,512]{2,1,0:T(8,128)(2,1)} %get-tuple-element.129.refs_5_), channel_id=1, source_target_pairs={{0,48},{2,18},{16,32},{18,2},{32,16},{34,50},{48,0},{50,34},{1,49}... | collective-permute-start | bytes 3145736 | tf_op jit(solution)/shard_map/ppermute | solution.py:756
  195.7 40.0 %collective-permute-start.27 = (bf16[2,2,384,512]{3,2,1,0:T(8,128)(2,1)}, bf16[2,2,384,512]{3,2,1,0:T(8,128)(2,1)S(1)}, u32[]{:S(2)}, u32[]{:S(2)}) collective-permute-start(bf16[2,2,384,512]{3,2,1,0:T(8,128)(2,1)} %get-tuple-element.134.refs_6_), channel_id=1, source_target_pairs={{0,16},{2,50},{16,0},{18,34},{32,48},{34,18},{48,32},{50,2},{1,17}... | collective-permute-start | bytes 4718600 | tf_op jit(solution)/shard_map/ppermute | solution.py:756
  197.3 13.9 %collective-permute-start.19 = (bf16[2,128,1024]{2,1,0:T(8,128)(2,1)S(1)}, bf16[2,128,1024]{2,1,0:T(8,128)(2,1)S(1)}, u32[]{:S(2)}, u32[]{:S(2)}) collective-permute-start(bf16[2,128,1024]{2,1,0:T(8,128)(2,1)S(1)} %copy-done.40), channel_id=1, source_target_pairs={{0,48},{2,18},{16,32},{18,2},{32,16},{34,50},{48,0},{50,34},{1,49}... | collective-permute-start | bytes 1572872 | tf_op jit(solution)/shard_map/ppermute | solution.py:756
  197.3 13.9 %collective-permute-start.20 = (bf16[2,128,1024]{2,1,0:T(8,128)(2,1)S(1)}, bf16[2,128,1024]{2,1,0:T(8,128)(2,1)S(1)}, u32[]{:S(2)}, u32[]{:S(2)}) collective-permute-start(bf16[2,128,1024]{2,1,0:T(8,128)(2,1)S(1)} %copy-done.68), channel_id=1, source_target_pairs={{0,12},{2,6},{4,8},{6,2},{8,4},{10,14},{12,0},{14,10},{1,13},{3,7}... | collective-permute-start | bytes 1572872 | tf_op jit(solution)/shard_map/ppermute | solution.py:756
  205.6 26.8 %collective-permute-start.29 = (bf16[2,2,32,2560]{3,2,1,0:T(8,128)(2,1)}, bf16[2,2,32,2560]{3,2,1,0:T(8,128)(2,1)S(1)}, u32[]{:S(2)}, u32[]{:S(2)}) collective-permute-start(bf16[2,2,32,2560]{3,2,1,0:T(8,128)(2,1)} %get-tuple-element.144), channel_id=1, source_target_pairs={{0,16},{2,50},{16,0},{18,34},{32,48},{34,18},{48,32},{50,2},{1,17}... | collective-permute-start | bytes 1966088 | tf_op jit(solution)/shard_map/ppermute | solution.py:756
  207.5 24.8 %collective-permute-start.28 = (bf16[2,2,128,512]{3,2,1,0:T(8,128)(2,1)}, bf16[2,2,128,512]{3,2,1,0:T(8,128)(2,1)S(1)}, u32[]{:S(2)}, u32[]{:S(2)}) collective-permute-start(bf16[2,2,128,512]{3,2,1,0:T(8,128)(2,1)} %get-tuple-element.135.refs_6_), channel_id=1, source_target_pairs={{0,4},{2,14},{4,0},{6,10},{8,12},{10,6},{12,8},{14,2},{1,5},{3,15}... | collective-permute-start | bytes 1572872 | tf_op jit(solution)/shard_map/ppermute | solution.py:756
  217.6 14.7 %collective-permute-start.25 = (bf16[2,2,32,1024]{3,2,1,0:T(8,128)(2,1)}, bf16[2,2,32,1024]{3,2,1,0:T(8,128)(2,1)S(1)}, u32[]{:S(2)}, u32[]{:S(2)}) collective-permute-start(bf16[2,2,32,1024]{3,2,1,0:T(8,128)(2,1)} %get-tuple-element.136.refs_9_), channel_id=1, source_target_pairs={{0,4},{2,14},{4,0},{6,10},{8,12},{10,6},{12,8},{14,2},{1,5},{3,15}... | collective-permute-start | bytes 786440 | tf_op jit(solution)/shard_map/ppermute | solution.py:756
  219.0 13.3 %collective-permute-start.26 = (bf16[2,2,32,1024]{3,2,1,0:T(8,128)(2,1)}, bf16[2,2,32,1024]{3,2,1,0:T(8,128)(2,1)S(1)}, u32[]{:S(2)}, u32[]{:S(2)}) collective-permute-start(bf16[2,2,32,1024]{3,2,1,0:T(8,128)(2,1)} %get-tuple-element.140), channel_id=1, source_target_pairs={{0,16},{2,50},{16,0},{18,34},{32,48},{34,18},{48,32},{50,2},{1,17}... | collective-permute-start | bytes 786440 | tf_op jit(solution)/shard_map/ppermute | solution.py:756
  239.0 21.2 %collective-permute-start.32 = (bf16[2,384,512]{2,1,0:T(8,128)(2,1)}, bf16[2,384,512]{2,1,0:T(8,128)(2,1)S(1)}, u32[]{:S(2)}, u32[]{:S(2)}) collective-permute-start(bf16[2,384,512]{2,1,0:T(8,128)(2,1)} %shard_map.370.refs_4_), channel_id=1, source_target_pairs={{0,48},{2,18},{16,32},{18,2},{32,16},{34,50},{48,0},{50,34},{1,49}... | collective-permute-start | bytes 2359304 | tf_op jit(solution)/shard_map/ppermute | solution.py:756
  239.1 14.8 %collective-permute-start.34 = (bf16[2,32,2560]{2,1,0:T(8,128)(2,1)S(1)}, bf16[2,32,2560]{2,1,0:T(8,128)(2,1)S(1)}, u32[]{:S(2)}, u32[]{:S(2)}) collective-permute-start(bf16[2,32,2560]{2,1,0:T(8,128)(2,1)S(1)} %copy-done.69), channel_id=1, source_target_pairs={{0,48},{2,18},{16,32},{18,2},{32,16},{34,50},{48,0},{50,34},{1,49}... | collective-permute-start | bytes 983048 | tf_op jit(solution)/shard_map/ppermute | solution.py:756
  257.4 9.7 %collective-permute-start.36 = (bf16[288,512]{1,0:T(8,128)(2,1)}, bf16[288,512]{1,0:T(8,128)(2,1)S(1)}, u32[]{:S(2)}, u32[]{:S(2)}) collective-permute-start(bf16[288,512]{1,0:T(8,128)(2,1)} %get-tuple-element.149.refs_3_), channel_id=1, source_target_pairs={{0,1},{2,67},{1,0},{3,66},{64,65},{66,3},{65,64},{67,2},{4,5},{6,7... | collective-permute-start | bytes 884744 | tf_op jit(solution)/shard_map/ppermute | solution.py:756
  259.4 7.6 %collective-permute-start.30 = (bf16[2,32,1024]{2,1,0:T(8,128)(2,1)S(1)}, bf16[2,32,1024]{2,1,0:T(8,128)(2,1)S(1)}, u32[]{:S(2)}, u32[]{:S(2)}) collective-permute-start(bf16[2,32,1024]{2,1,0:T(8,128)(2,1)S(1)} %copy-done.54), channel_id=1, source_target_pairs={{0,12},{2,6},{4,8},{6,2},{8,4},{10,14},{12,0},{14,10},{1,13},{3,7}... | collective-permute-start | bytes 393224 | tf_op jit(solution)/shard_map/ppermute | solution.py:756
  265.7 8.0 %collective-permute-start.35 = (bf16[2,2,96,512]{3,2,1,0:T(8,128)(2,1)}, bf16[2,2,96,512]{3,2,1,0:T(8,128)(2,1)S(1)}, u32[]{:S(2)}, u32[]{:S(2)}) collective-permute-start(bf16[2,2,96,512]{3,2,1,0:T(8,128)(2,1)} %get-tuple-element.151.refs_2_), channel_id=1, source_target_pairs={{0,4},{2,14},{4,0},{6,10},{8,12},{10,6},{12,8},{14,2},{1,5},{3,15}... | collective-permute-start | bytes 1179656 | tf_op jit(solution)/shard_map/ppermute | solution.py:756
  269.8 8.0 %collective-permute-start.38 = (bf16[288,512]{1,0:T(8,128)(2,1)}, bf16[288,512]{1,0:T(8,128)(2,1)S(1)}, u32[]{:S(2)}, u32[]{:S(2)}) collective-permute-start(bf16[288,512]{1,0:T(8,128)(2,1)} %shard_map.374.refs_2_.refs_0_), channel_id=1, source_target_pairs={{0,64},{64,0},{1,65},{65,1},{2,66},{66,2},{3,67},{67,3},{4,68},{68... | collective-permute-start | bytes 884744 | tf_op jit(solution)/shard_map/ppermute | solution.py:885
  280.4 111.5 %all-gather.9.cloned.1.call-start = ((), (), s32[]{:S(2)}) async-start(), calls=%async_computation.1 | async-start | bytes 8110080 | tf_op jit(solution)/shard_map/all_gather | solution.py:888
  (83 other events, 484.7 us)
Sparse Core Ops, SparseCore 0:
  19.1 63.1 all-gather.6
  280.5 57.0 all-gather.10
  340.5 51.3 all-gather.8

commit v3 on v2

--- a/solution.py
+++ b/solution.py
@@ -82,15 +82,16 @@
     return result
 
 
-def gate(value, *after):
+def gate(values, *after):
+    n = len(values)
     anywhere = pl.BlockSpec(memory_space=pl.ANY)
     return pl.pallas_call(
         lambda *refs: None,
-        out_shape=jax.ShapeDtypeStruct(value.shape, value.dtype),
-        in_specs=[anywhere] * (1 + len(after)),
-        out_specs=anywhere,
-        input_output_aliases={0: 0},
-    )(value, *after)
+        out_shape=[jax.ShapeDtypeStruct(v.shape, v.dtype) for v in values],
+        in_specs=[anywhere] * (n + len(after)),
+        out_specs=[anywhere] * n,
+        input_output_aliases={i: i for i in range(n)},
+    )(*values, *after)
 
 
 def whole(a):
@@ -133,14 +134,14 @@
     return ref[i : i + 1, :]
 
 
-def pack(vectors, w_in, w_out, conv_w, scalars):
-    n_in, n_out, n_conv = (w.shape[0] // 32 for w in (w_in, w_out, conv_w))
+def pack(vectors, w_in, w_out, scalars):
+    n_in, n_out = (w.shape[0] // 32 for w in (w_in, w_out))
     chunks = FF // D
-    rows = n_out + n_in * chunks + n_conv
+    rows = n_out + n_in * chunks
     half = D // 2
 
     def kernel(_, *refs):
-        wi, wo, wc, piece, flat = refs[-5:]
+        wi, wo, piece, flat = refs[-4:]
         flat[...] = jnp.zeros_like(flat)
         for i, ref in enumerate(refs[:8]):
             flat[i : i + 1, :half] = ref[...].astype(f32).reshape(1, half)
@@ -148,7 +149,6 @@
         piece[:n_out, :] = wo[...]
         for i in range(chunks):
             piece[n_out + i * n_in : n_out + (i + 1) * n_in, :] = wi[:, i * D : (i + 1) * D]
-        piece[n_out + n_in * chunks : rows, :] = wc[...]
         piece[rows:, :] = flat[...].astype(bf16)
 
     out = shape((rows + 16, D), bf16)
@@ -159,35 +159,34 @@
         [whole(v) for v in vectors]
         + [
             pl.BlockSpec((w.shape[0] // 32, w.shape[1]), lambda j, s: (s[0], 0))
-            for w in (w_in, w_out, conv_w)
+            for w in (w_in, w_out)
         ],
         whole(out),
         scalars,
-        (*vectors, w_in, w_out, conv_w),
+        (*vectors, w_in, w_out),
         [pltpu.VMEM((16, D), f32)],
     )
 
 
-def pack_rows(w_kv, w_q, w_r, w_o, scalars):
-    n = w_q.shape[0] // 2
-
-    def kernel(_, kv, q, r, o, kv_out, out):
+def pack_rows(w_kv, w_q, w_r, w_o, conv_w, scalars):
+    n, n_conv = w_q.shape[0] // 2, conv_w.shape[0] // 2
+
+    def kernel(_, kv, q, r, o, conv, kv_out, out, conv_out):
         kv_out[...] = kv[...]
         for i, ref in enumerate((q, r, o)):
             out[i] = ref[...]
-
-    out = (shape((n, 2 * D), bf16), shape((3, n, D), bf16))
+        conv_out[...] = conv[...]
+
+    args = (w_kv, w_q, w_r, w_o, conv_w)
+    out = (shape((n, 2 * D), bf16), shape((3, n, D), bf16), shape((n_conv, D), bf16))
     return call(
         kernel,
         out,
         (1,),
-        [
-            pl.BlockSpec((n, w.shape[1]), lambda j, s: (s[0], 0))
-            for w in (w_kv, w_q, w_r, w_o)
-        ],
+        [pl.BlockSpec((w.shape[0] // 2, w.shape[1]), lambda j, s: (s[0], 0)) for w in args],
         [whole(o) for o in out],
         scalars,
-        (w_kv, w_q, w_r, w_o),
+        args,
     )
 
 
@@ -254,113 +253,108 @@
     )
 
 
-PAIR = 2
-STEPS = H // PAIR
-
-
-def head(rows, row_block=0, first=0):
-    return pl.BlockSpec((rows, PAIR * HD), lambda h, s: (row_block, first // PAIR + h))
-
-
-def vec_head(rows=1):
-    return pl.BlockSpec((rows, PAIR * HD), lambda h, s: (0, h))
-
-
-def each_head(body):
-    for i in range(PAIR):
-        body(i, slice(i * HD, (i + 1) * HD))
+def head(n, rows, row_block=0, first=0):
+    return pl.BlockSpec((rows, n * HD), lambda h, s: (row_block, first // n + h))
+
+
+def columns_of(n):
+    return [slice(i * HD, (i + 1) * HD) for i in range(n)]
 
 
 def attend(queries, key_value, relative, vectors, none):
+    n = 2
+
     def kernel(_, q, k, v, rel, vec, probs, out):
         pad = jnp.zeros((PAD - KEYS, HD), bf16)
-        row = lax.broadcasted_iota(jnp.int32, (T, PAD), 0)
-        col = lax.broadcasted_iota(jnp.int32, (T, PAD), 1)
-        seen = col <= row + (KEYS - T)
-
-        def body(i, cut):
-            content = ((q[:, cut] + vec[BIAS_U : BIAS_U + 1, cut]) * FACTOR).astype(bf16)
-            located = ((q[:, cut] + vec[BIAS_V : BIAS_V + 1, cut]) * FACTOR).astype(bf16)
-            raw = dot_t(located, jnp.concatenate([rel[:, cut], pad], axis=0))
-            raw = pltpu.roll(raw, PAD - T + 1, 1, stride=1, stride_axis=0)
-            s = dot_t(content, jnp.concatenate([k[:, cut], pad], axis=0)) + raw
-            p = softmax(jnp.where(seen, s, -1e30))
-            probs[i] = p
-            low = p.astype(bf16)
-            out[:, cut] = dot(low, jnp.concatenate([v[:, cut], pad], axis=0)).astype(bf16)
-
-        each_head(body)
+        i = lax.broadcasted_iota(jnp.int32, (T, PAD), 0)
+        j = lax.broadcasted_iota(jnp.int32, (T, PAD), 1)
+        seen = j <= i + (KEYS - T)
+        cuts = columns_of(n)
+        content = [((q[:, c] + vec[BIAS_U : BIAS_U + 1, c]) * FACTOR).astype(bf16) for c in cuts]
+        located = [((q[:, c] + vec[BIAS_V : BIAS_V + 1, c]) * FACTOR).astype(bf16) for c in cuts]
+        raw = [
+            dot_t(x, jnp.concatenate([rel[:, c], pad], axis=0)) for x, c in zip(located, cuts)
+        ]
+        near = [dot_t(x, jnp.concatenate([k[:, c], pad], axis=0)) for x, c in zip(content, cuts)]
+        raw = [pltpu.roll(x, PAD - T + 1, 1, stride=1, stride_axis=0) for x in raw]
+        p = [softmax(jnp.where(seen, a + b, -1e30)) for a, b in zip(near, raw)]
+        for h, c in enumerate(cuts):
+            probs[h] = p[h]
+            value = jnp.concatenate([v[:, c], pad], axis=0)
+            out[:, c] = dot(p[h].astype(bf16), value).astype(bf16)
 
     return call(
         kernel,
         (shape((H, T, PAD), f32), shape((T, D), bf16)),
-        (STEPS,),
-        [head(T), head(KEYS), head(KEYS, 0, H), head(KEYS), vec_head(8)],
-        [pl.BlockSpec((PAIR, T, PAD), lambda h, s: (h, 0, 0)), head(T)],
+        (H // n,),
+        [head(n, T), head(n, KEYS), head(n, KEYS, 0, H), head(n, KEYS), head(n, 8)],
+        [pl.BlockSpec((n, T, PAD), lambda h, s: (h, 0, 0)), head(n, T)],
         none,
         (queries, key_value, key_value, relative, vectors),
     )
 
 
 def attend_back(queries, key_value, relative, vectors, probs, d_attended, scalars):
+    n = 2
+
     def kernel(s, q, k, v, rel, vec, probs, d_att, d_kv, mine, give, d_rel, d_q, d_bu, d_bv):
         pad = jnp.zeros((PAD - KEYS, HD), bf16)
-        row = lax.broadcasted_iota(jnp.int32, (T, T), 0)
-        col = lax.broadcasted_iota(jnp.int32, (T, T), 1)
-        flip = jnp.where(row + col == T - 1, 1.0, 0.0).astype(bf16)
-
-        def body(i, cut):
-            content = ((q[:, cut] + vec[BIAS_U : BIAS_U + 1, cut]) * FACTOR).astype(bf16)
-            located = ((q[:, cut] + vec[BIAS_V : BIAS_V + 1, cut]) * FACTOR).astype(bf16)
-            p, da = probs[i], d_att[:, cut]
-            d_p = dot_t(da, jnp.concatenate([v[:, cut], pad], axis=0))
-            d_v = t_dot(p.astype(bf16), da)[:KEYS].astype(bf16)
-            d_s = (p * (d_p - jnp.sum(p * d_p, axis=-1, keepdims=True))).astype(bf16)
-            d_c = dot(d_s, jnp.concatenate([k[:, cut], pad], axis=0)) * FACTOR
-            d_k = t_dot(d_s, content)[:KEYS].astype(bf16)
-            d_kv[0, :, cut] = d_k
-            d_kv[1, :, cut] = d_v
-            mine[:, cut] = jnp.where(s[0] == 0, d_k, d_v)
-            give[:, cut] = jnp.where(s[0] == 0, d_v, d_k)
-            d_raw = pltpu.roll(dot(flip, d_s), 0, 1, stride=1, stride_axis=0)
-            d_raw = dot(flip, d_raw.astype(bf16)).astype(bf16)
-            d_l = dot(d_raw, jnp.concatenate([rel[:, cut], pad], axis=0)) * FACTOR
-            d_rel[:, cut] = t_dot(d_raw, located)[:KEYS].astype(bf16)
-            d_q[:, cut] = (d_c + d_l).astype(bf16)
-            d_bu[:, cut] = jnp.sum(d_c, axis=0, keepdims=True)
-            d_bv[:, cut] = jnp.sum(d_l, axis=0, keepdims=True)
-
-        each_head(body)
+        i = lax.broadcasted_iota(jnp.int32, (T, T), 0)
+        j = lax.broadcasted_iota(jnp.int32, (T, T), 1)
+        flip = jnp.where(i + j == T - 1, 1.0, 0.0).astype(bf16)
+        cuts = columns_of(n)
+        content = [((q[:, c] + vec[BIAS_U : BIAS_U + 1, c]) * FACTOR).astype(bf16) for c in cuts]
+        located = [((q[:, c] + vec[BIAS_V : BIAS_V + 1, c]) * FACTOR).astype(bf16) for c in cuts]
+        da = [d_att[:, c] for c in cuts]
+        d_p = [dot_t(x, jnp.concatenate([v[:, c], pad], axis=0)) for x, c in zip(da, cuts)]
+        d_v = [t_dot(probs[h].astype(bf16), x)[:KEYS].astype(bf16) for h, x in enumerate(da)]
+        d_s = []
+        for h, x in enumerate(d_p):
+            p = probs[h]
+            d_s.append((p * (x - jnp.sum(p * x, axis=-1, keepdims=True))).astype(bf16))
+        d_raw = [dot(flip, x) for x in d_s]
+        d_c = [
+            dot(x, jnp.concatenate([k[:, c], pad], axis=0)) * FACTOR for x, c in zip(d_s, cuts)
+        ]
+        d_k = [t_dot(x, y)[:KEYS].astype(bf16) for x, y in zip(d_s, content)]
+        d_raw = [pltpu.roll(x, 0, 1, stride=1, stride_axis=0).astype(bf16) for x in d_raw]
+        d_raw = [dot(flip, x).astype(bf16) for x in d_raw]
+        d_l = [
+            dot(x, jnp.concatenate([rel[:, c], pad], axis=0)) * FACTOR for x, c in zip(d_raw, cuts)
+        ]
+        for h, c in enumerate(cuts):
+            d_rel[:, c] = t_dot(d_raw[h], located[h])[:KEYS].astype(bf16)
+            d_kv[0, :, c] = d_k[h]
+            d_kv[1, :, c] = d_v[h]
+            mine[:, c] = jnp.where(s[0] == 0, d_k[h], d_v[h])
+            give[:, c] = jnp.where(s[0] == 0, d_v[h], d_k[h])
+            d_q[:, c] = (d_c[h] + d_l[h]).astype(bf16)
+            d_bu[:, c] = jnp.sum(d_c[h], axis=0, keepdims=True)
+            d_bv[:, c] = jnp.sum(d_l[h], axis=0, keepdims=True)
 
     return call(
         kernel,
-        (
-            shape((2, KEYS, D), bf16),
-            shape((KEYS, D), bf16),
-            shape((KEYS, D), bf16),
-            shape((KEYS, D), bf16),
-            shape((T, D), bf16),
-            shape((1, D), f32),
-            shape((1, D), f32),
-        ),
-        (STEPS,),
+        (shape((2, KEYS, D), bf16),)
+        + (shape((KEYS, D), bf16),) * 3
+        + (shape((T, D), bf16), shape((1, D), f32), shape((1, D), f32)),
+        (H // n,),
         [
-            head(T),
-            head(KEYS),
-            head(KEYS, 0, H),
-            head(KEYS),
-            vec_head(8),
-            pl.BlockSpec((PAIR, T, PAD), lambda h, s: (h, 0, 0)),
-            head(T),
+            head(n, T),
+            head(n, KEYS),
+            head(n, KEYS, 0, H),
+            head(n, KEYS),
+            head(n, 8),
+            pl.BlockSpec((n, T, PAD), lambda h, s: (h, 0, 0)),
+            head(n, T),
         ],
         [
-            pl.BlockSpec((2, KEYS, PAIR * HD), lambda h, s: (0, 0, h)),
-            head(KEYS),
-            head(KEYS),
-            head(KEYS),
-            head(T),
-            vec_head(),
-            vec_head(),
+            pl.BlockSpec((2, KEYS, n * HD), lambda h, s: (0, 0, h)),
+            head(n, KEYS),
+            head(n, KEYS),
+            head(n, KEYS),
+            head(n, T),
+            head(n, 1),
+            head(n, 1),
         ],
         scalars,
         (queries, key_value, key_value, relative, vectors, probs, d_attended),
@@ -402,37 +396,27 @@
     def kernel(s, n2, res, cot, wi0, wi1, wo0, wo1, bi, vec, hid, dpre, mixed, dn2, dbi, acc, back):
         j = pl.program_id(0)
         n = natural(j, s)
+
+        @pl.when(j == 0)
+        def _():
+            acc[...] = jnp.zeros_like(acc)
+            back[...] = jnp.zeros_like(back)
+
+        wo = jnp.where(j < HALF, wo0[...], wo1[...].reshape(UNITS, D))
         win = jnp.concatenate([wi0[...], wi1[...].reshape(D // 2, UNITS)], axis=0)
         pre = dot(n2[...], win) + bi[pl.ds(n, 1), :]
-        t = jnp.tanh(K_NORM * (pre + 0.044715 * (pre * pre * pre)))
-        hidden = (0.5 * pre * (1.0 + t)).astype(bf16)
-        slope = 0.5 * (1.0 + t) + (0.5 * K_NORM) * pre * (1.0 - t * t) * (
-            1.0 + (3 * 0.044715) * (pre * pre)
-        )
+        d_hidden = dot_t(cot[...], wo)
+        square = pre * pre
+        t = jnp.tanh(K_NORM * pre * (1.0 + 0.044715 * square))
+        gate_ = 0.5 * (1.0 + t)
+        hidden = (pre * gate_).astype(bf16)
+        slope = gate_ + (0.5 * K_NORM) * pre * (1.0 - t * t) * (1.0 + (3 * 0.044715) * square)
+        d_pre = (d_hidden * slope).astype(bf16)
         hid[...] = hidden
-
-        def rest(wo, start):
-            d_pre = (dot_t(cot[...], wo) * slope).astype(bf16)
-            dpre[...] = d_pre
-            dbi[pl.ds(n, 1), :] = jnp.sum(d_pre.astype(f32), axis=0, keepdims=True)
-            if start:
-                acc[...] = dot(hidden, wo)
-                back[...] = dot_t(d_pre, win)
-            else:
-                acc[...] += dot(hidden, wo)
-                back[...] += dot_t(d_pre, win)
-
-        @pl.when(j == 0)
-        def _():
-            rest(wo0[...], True)
-
-        @pl.when((j > 0) & (j < HALF))
-        def _():
-            rest(wo0[...], False)
-
-        @pl.when(j >= HALF)
-        def _():
-            rest(wo1[...].reshape(UNITS, D), False)
+        dpre[...] = d_pre
+        dbi[pl.ds(n, 1), :] = jnp.sum(d_pre.astype(f32), axis=0, keepdims=True)
+        acc[...] += dot(hidden, wo)
+        back[...] += dot_t(d_pre, win)
 
         @pl.when(j == 2 * HALF - 1)
         def _():
@@ -503,35 +487,46 @@
     steps = 4
     wide, slim = 2 * D // steps, D // steps
 
-    def kernel(s, dkv, dq, kw, qw, comp, mem, tok, vec, dres, dtok, dg, db, acc, nat):
+    def kernel(s, dkv, dq, kw, qw, comp, mem, tok, vec, dres, dtok, dg, db, acc, nat, xh, rs):
         j = pl.program_id(0)
 
-        @pl.when(j == 0)
-        def _():
-            acc[...] = dot_t(dkv[0], kw[...])
-
-        @pl.when(j > 0)
-        def _():
-            acc[...] += dot_t(dkv[0], kw[...])
-
-        acc[2 * T :, :] += dot_t(dq[...], qw[...])
+        def product(start):
+            value = dot_t(dkv[0], kw[...])
+            if start:
+                acc[...] = value
+            else:
+                acc[...] += value
+            acc[2 * T :, :] += dot_t(dq[...], qw[...])
+
+        for block, ref in enumerate((comp, mem, tok)):
+
+            @pl.when(j == block)
+            def _(block=block, ref=ref):
+                product(block == 0)
+                for i in range(0, T, 32):
+                    xhat, r = center_scale(ref[i : i + 32, :].astype(f32))
+                    xh[block * T + i : block * T + i + 32, :] = xhat
+                    if block == 2:
+                        rs[i : i + 32, :] = jnp.broadcast_to(r, (32, HD))
 
         @pl.when(j == steps - 1)
         def _():
+            product(False)
             natural_columns(nat, acc, s, THIRDS)
             gain = row(vec, LN1_G)
-            sum_g = jnp.zeros((1, D), f32)
-            sum_b = jnp.zeros((1, D), f32)
-            for block, ref in enumerate((comp, mem, tok)):
-                for i in range(0, T, 32):
-                    xhat, r = center_scale(ref[i : i + 32, :].astype(f32))
-                    dn = nat[block * T + i : block * T + i + 32, :]
-                    sum_g += jnp.sum(dn * xhat, axis=0, keepdims=True)
-                    sum_b += jnp.sum(dn, axis=0, keepdims=True)
-                    if block == 2:
-                        dtok[i : i + 32, :] = dres[i : i + 32, :] + norm_back(xhat, r, gain, dn)
-            dg[...] = sum_g
-            db[...] = sum_b
+            sum_g = jnp.zeros((8, D), f32)
+            sum_b = jnp.zeros((8, D), f32)
+            for i in range(0, KEYS, 32):
+                dn, xhat = nat[i : i + 32, :], xh[i : i + 32, :]
+                both = dn * xhat
+                sum_g += (both[:8] + both[8:16]) + (both[16:24] + both[24:])
+                sum_b += (dn[:8] + dn[8:16]) + (dn[16:24] + dn[24:])
+                if i >= 2 * T:
+                    k = i - 2 * T
+                    r = rs[k : k + 32, :1]
+                    dtok[k : k + 32, :] = dres[k : k + 32, :] + norm_back(xhat, r, gain, dn)
+            dg[...] = jnp.sum(sum_g, axis=0, keepdims=True)
+            db[...] = jnp.sum(sum_b, axis=0, keepdims=True)
 
     rest = (compressed, memory, tokens, vectors, d_res)
     out = (shape((T, D), f32), shape((1, D), f32), shape((1, D), f32))
@@ -549,25 +544,22 @@
         [whole(o) for o in out],
         offsets,
         (d_kv, d_q, w_kv, w_q, *rest),
-        [pltpu.VMEM((KEYS, D), f32), pltpu.VMEM((KEYS, D), f32)],
-    )
-
-
-def compress(oldest, conv_w, spread, vectors, offsets):
+        [pltpu.VMEM((KEYS, D), f32)] * 3 + [pltpu.VMEM((T, HD), f32)],
+    )
+
+
+def compress(oldest, pieces, vectors, offsets):
     block = 256
     rows = T // 3
-    n = conv_w.shape[0] // 32
-    skip = (spread.shape[1] - n) // 16
-
-    def kernel(s, x, own, w0, w1, w2, vec, compact, normed, x_rel, natural):
+
+    def kernel(s, x, w0, w1, w2, vec, compact, normed, x_rel, natural):
         j = pl.program_id(0)
 
         @pl.when(j == 0)
         def _():
-            x_rel[...] = relative_columns(x, s, (3 * D // 2, 3 * D // 2))
-
-        other = jnp.concatenate([w0[...], w1[...], w2[...]], axis=1).reshape(32 * n, block)
-        w = jnp.concatenate([own[...], other], axis=0)
+            x_rel[...] = relative_columns(x, s, (3 * D // 2, 3 * D // 4, 3 * D // 4))
+
+        w = jnp.concatenate([w0[...], w1[...], w2[...]], axis=0)
         here = pl.ds(at(j * block), block)
         compact[:, here] = dot(x_rel[...], w) + vec[CONV_B : CONV_B + 1, here]
 
@@ -577,7 +569,7 @@
             natural[...] = (xhat * row(vec, LN1_G) + row(vec, LN1_B)).astype(bf16)
             start = 0
             for i, width in enumerate(THIRDS):
-                normed[:, start : start + width] = natural[:, pl.ds(at(s[2 + i]), width)]
+                normed[:, start : start + width] = natural[:, pl.ds(at(s[3 + i]), width)]
                 start += width
 
     out = (shape((rows, D), f32), shape((rows, D), bf16))
@@ -585,49 +577,54 @@
         kernel,
         out,
         (D // block,),
-        [whole(oldest), pl.BlockSpec((conv_w.shape[0], block), lambda j, s: (0, j))]
-        + [
-            pl.BlockSpec((32, 16, block), lambda j, s, i=i: (0, skip + i, j))
-            for i in range(n // 16)
-        ]
+        [whole(oldest)]
+        + [pl.BlockSpec((w.shape[0], block), lambda j, s: (0, j)) for w in pieces]
         + [whole(vectors)],
         [whole(o) for o in out],
         offsets,
-        (oldest, conv_w) + (spread,) * (n // 16) + (vectors,),
+        (oldest, *pieces, vectors),
         [pltpu.VMEM((rows, 3 * D), bf16), pltpu.VMEM((rows, D), bf16)],
     )
 
 
 def reconstruct(queries, key_value, comp_pair, none):
     rows = T // 3
+    n = 4
 
     def kernel(_, q, k, v, ck, cv, loss, dck, dcv):
+        cuts = columns_of(n)
+        asking = [(q[:, c] * FACTOR).astype(bf16) for c in cuts]
+        far = [dot_t(x, k[:, c]) for x, c in zip(asking, cuts)]
+        near = [dot_t(x, ck[:, c]) for x, c in zip(asking, cuts)]
+        p = [softmax(x).astype(bf16) for x in far]
+        gp = [softmax(x) for x in near]
+        low = [x.astype(bf16) for x in gp]
+        miss = [dot(p[h], v[:, c]) - dot(low[h], cv[:, c]) for h, c in enumerate(cuts)]
+        total = sum(jnp.sum(x * x, axis=0, keepdims=True) for x in miss)
+        d_guess = [((-2.0 / (T * D)) * x).astype(bf16) for x in miss]
+        d_gp = [dot_t(x, cv[:, c]) for x, c in zip(d_guess, cuts)]
+        d_gs = [
+            (x * (y - jnp.sum(x * y, axis=-1, keepdims=True))).astype(bf16)
+            for x, y in zip(gp, d_gp)
+        ]
+        for h, c in enumerate(cuts):
+            dcv[:, c] = t_dot(low[h], d_guess[h]).astype(bf16)
+            dck[:, c] = t_dot(d_gs[h], asking[h]).astype(bf16)
+
         @pl.when(pl.program_id(0) == 0)
         def _():
-            loss[...] = jnp.zeros_like(loss)
-
-        def body(i, cut):
-            asking = (q[:, cut] * FACTOR).astype(bf16)
-            cvh = cv[:, cut]
-            p = softmax(dot_t(asking, k[:, cut])).astype(bf16)
-            gp = softmax(dot_t(asking, ck[:, cut]))
-            low = gp.astype(bf16)
-            miss = dot(p, v[:, cut]) - dot(low, cvh)
-            loss[...] += jnp.sum(miss * miss, axis=0, keepdims=True)
-            d_guess = ((-2.0 / (T * D)) * miss).astype(bf16)
-            d_gp = dot_t(d_guess, cvh)
-            dcv[:, cut] = t_dot(low, d_guess).astype(bf16)
-            d_gs = (gp * (d_gp - jnp.sum(gp * d_gp, axis=-1, keepdims=True))).astype(bf16)
-            dck[:, cut] = t_dot(d_gs, asking).astype(bf16)
-
-        each_head(body)
+            loss[...] = total
+
+        @pl.when(pl.program_id(0) > 0)
+        def _():
+            loss[...] += total
 
     return call(
         kernel,
         (shape((1, HD), f32), shape((rows, D), bf16), shape((rows, D), bf16)),
-        (STEPS,),
-        [head(T), head(T, 1), head(T, 1, H), head(rows), head(rows, 0, H)],
-        [pl.BlockSpec((1, HD), lambda h, s: (0, 0)), head(rows), head(rows)],
+        (H // n,),
+        [head(n, T), head(n, T, 1), head(n, T, 1, H), head(n, rows), head(n, rows, 0, H)],
+        [pl.BlockSpec((1, HD), lambda h, s: (0, 0)), head(n, rows), head(n, rows)],
         none,
         (queries, key_value, key_value, comp_pair, comp_pair),
     )
@@ -659,14 +656,14 @@
 
 
 def weight_grads(groups, scalars):
-    in_specs, args, outs, out_specs, layout = [], [], [], [], []
+    in_specs, args, outs, out_specs, layout, scratch = [], [], [], [], [], []
     for ring, jobs in groups:
         first = 1 if ring == "x" else 5
         block = jobs[0][0][0].shape[1] // 8
-        widths = []
+        plan = []
         for xs, row_block, rows, dys, ready in jobs:
             width = dys[0].shape[1] // (1 if ready else 2)
-            widths.append(width)
+            plan.append((width, rows, len(xs)))
             for x in xs:
                 for y in range(2):
                     in_specs.append(
@@ -681,36 +678,53 @@
                     pl.BlockSpec((rows, width), lambda q, s, r=ready: (0, 0 if r else s[0]))
                 )
                 args.append(dy)
-        dims = (1, 2, block, sum(widths))
+            scratch.append(pltpu.VMEM((rows * len(xs), width), bf16))
+        dims = (1, 2, block, sum(p[0] for p in plan))
         outs += [shape((2, *dims[1:]), bf16)] * 2
         out_specs += [
             pl.BlockSpec(dims, lambda q, s: (jnp.minimum(q, 1), 0, 0, 0)),
             pl.BlockSpec(dims, lambda q, s: (jnp.maximum(q - 2, 0), 0, 0, 0)),
         ]
-        layout.append(widths)
+        layout.append(plan)
+    n_in, n_out = len(in_specs), len(outs)
 
     def kernel(s, *refs):
+        ins, results, joined = refs[:n_in], refs[n_in : n_in + n_out], refs[n_in + n_out :]
         q = pl.program_id(0)
-        place = 0
-        results = refs[len(in_specs) :]
-        for i, widths in enumerate(layout):
+
+        @pl.when(q == 0)
+        def _():
+            place, k = 0, 0
+            for plan in layout:
+                for _, rows, n in plan:
+                    da, db = ins[place + 2 * n], ins[place + 2 * n + 1]
+                    if n == 2:
+                        joined[k][:rows, :] = da[...]
+                        joined[k][rows:, :] = db[...]
+                    else:
+                        joined[k][...] = (da[...].astype(f32) + db[...].astype(f32)).astype(bf16)
+                    place += 2 * n + 2
+                    k += 1
+
+        place, k = 0, 0
+        for i, plan in enumerate(layout):
             send, keep = results[2 * i : 2 * i + 2]
             block = send.shape[2]
             start = 0
-            for width in widths:
-                a0, a1, b0, b1, da, db = (r[...] for r in refs[place : place + 6])
-                place += 6
-                x = jnp.concatenate(
-                    [jnp.concatenate([a0, a1], axis=1), jnp.concatenate([b0, b1], axis=1)], axis=0
-                )
-                value = t_dot(x, jnp.concatenate([da, db], axis=0)).astype(bf16)
-                value = value.reshape(2, block, width)
+            for width, rows, n in plan:
+                x = jnp.concatenate([r[...] for r in ins[place : place + 2]], axis=1)
+                if n == 2:
+                    other = jnp.concatenate([r[...] for r in ins[place + 2 : place + 4]], axis=1)
+                    x = jnp.concatenate([x, other], axis=0)
+                value = t_dot(x, joined[k][...]).astype(bf16).reshape(2, block, width)
                 cut = slice(start, start + width)
                 send[0, :, :, cut] = jnp.where(q < 2, value, send[0, :, :, cut])
                 keep[0, :, :, cut] = value
                 start += width
-
-    flat = call(kernel, tuple(outs), (4,), in_specs, out_specs, scalars, args)
+                place += 2 * n + 2
+                k += 1
+
+    flat = call(kernel, tuple(outs), (4,), in_specs, out_specs, scalars, args, scratch)
     return [(flat[2 * i], flat[2 * i + 1]) for i in range(len(groups))]
 
 
@@ -771,60 +785,78 @@
         self.ring, self.other = ring, "z" if ring == "x" else "x"
         send, self.keep = pair
         self.got = exchange(send, ring, (1, 3))
-
-
-def onward(flows, none):
+        self.before = None
+
+    def kept(self, which):
+        if self.before is None:
+            dims = (1, *self.keep.shape[1:])
+            return [pl.BlockSpec(dims, lambda j, s: (which, 0, 0, 0))], [self.keep]
+        return self.before(2 + which)
+
+
+def onward(flows, cuts):
+    in_specs, args, counts = [], [], []
+    for f in flows:
+        specs, arrays = f.kept(1)
+        dims = (1, *f.got.shape[1:])
+        in_specs += specs + [pl.BlockSpec(dims, lambda j, s: (1, 0, 0, 0))]
+        args += arrays + [f.got]
+        counts.append(len(arrays) + 1)
+    out = tuple(shape(f.got.shape[1:], bf16) for f in flows)
+
     def kernel(_, *refs):
-        n = len(flows)
-        for i in range(n):
-            keep, got = refs[2 * i : 2 * i + 2]
-            refs[2 * n + i][0] = (keep[0, 0].astype(f32) + got[0, 0].astype(f32)).astype(bf16)
-
-    dims = [f.keep.shape[2:] for f in flows]
-    sums = call(
-        kernel,
-        tuple(shape((2, *d), bf16) for d in dims),
-        (2,),
-        [pl.BlockSpec((1, 1, *d), lambda y, s: (1, y, 0, 0)) for d in dims for _ in range(2)],
-        [pl.BlockSpec((1, *d), lambda y, s: (y, 0, 0)) for d in dims],
-        none,
-        [a for f in flows for a in (f.keep, f.got)],
-    )
+        k = 0
+        for i, n in enumerate(counts):
+            total = sum(value_of(r) for r in refs[k : k + n])
+            refs[len(args) + i][...] = total.astype(bf16)
+            k += n
+
+    sums = call(kernel, out, (1,), in_specs, [whole(o) for o in out], cuts, args)
     for f, v in zip(flows, sums):
         f.last = exchange(v, f.ring, (3, 1))
 
 
+def value_of(ref):
+    return (ref[0] if len(ref.shape) == 4 else ref[...]).astype(f32)
+
+
 def turn(flows, cuts):
     in_specs, outs, out_specs, args = [], [], [], []
-    for f in flows:
+
+    def parts(f, index):
         first = 1 if f.other == "x" else 5
         rows, columns = f.keep.shape[2] // 4, f.keep.shape[3]
-        in_specs += [
-            pl.BlockSpec((1, 2, rows, columns), lambda q, s, i=first: (0, 0, s[i + q], 0))
-        ] * 2 + [pl.BlockSpec((2, rows, columns), lambda q, s, i=first: (0, s[i + q], 0))]
-        args += [f.keep, f.got, f.last]
-        dims = (1, 2, rows, columns)
-        outs += [shape((2, *dims[1:]), bf16), shape((2, *dims[1:]), f32)]
-        out_specs += [
-            pl.BlockSpec(dims, lambda q, s: (jnp.minimum(q, 1), 0, 0, 0)),
-            pl.BlockSpec(dims, lambda q, s: (jnp.maximum(q - 2, 0), 0, 0, 0)),
-        ]
+        arrays = [f.keep, f.got, f.last]
+
+        def spec(pick):
+            four = pl.BlockSpec((1, 2, rows, columns), lambda j, s: (0, 0, s[first + pick(j)], 0))
+            three = pl.BlockSpec((2, rows, columns), lambda j, s: (0, s[first + pick(j)], 0))
+            return [four, four, three]
+
+        return spec(index), arrays
+
+    for f in flows:
+        specs, arrays = parts(f, lambda j: j)
+        in_specs += specs
+        args += arrays
+        dims = (1, 2, f.keep.shape[2] // 4, f.keep.shape[3])
+        outs.append(shape((2, *dims[1:]), bf16))
+        out_specs.append(pl.BlockSpec(dims, lambda j, s: (j, 0, 0, 0)))
 
     def kernel(_, *refs):
-        n = len(flows)
-        q = pl.program_id(0)
-        for i in range(n):
-            keep, got, last = refs[3 * i : 3 * i + 3]
-            send, kept = refs[3 * n + 2 * i : 3 * n + 2 * i + 2]
-            value = keep[0].astype(f32) + got[0].astype(f32) + last[...].astype(f32)
-            send[0] = jnp.where(q < 2, value.astype(bf16), send[0])
-            kept[0] = value
-
-    out = call(kernel, tuple(outs), (4,), in_specs, out_specs, cuts, args)
-    for i, f in enumerate(flows):
+        for i in range(len(flows)):
+            total = sum(value_of(r) for r in refs[3 * i : 3 * i + 3])
+            refs[len(args) + i][0] = total.astype(bf16)
+
+    sends = call(kernel, tuple(outs), (2,), in_specs, out_specs, cuts, args)
+    for f, send in zip(flows, sends):
+        whole_parts = parts(f, lambda j: 2)[1]
+        f.before = lambda which, f=f, arrays=whole_parts, made=[
+            parts(f, lambda j: 2)[0],
+            parts(f, lambda j: 3)[0],
+        ]: (made[which - 2], arrays)
         f.ring = f.other
-        f.keep = out[2 * i + 1]
-        f.got = exchange(out[2 * i], f.ring, (1, 3))
+        f.got = exchange(send, f.ring, (1, 3))
 
 
 def add(a, b, none):
@@ -836,47 +868,41 @@
 
 
 class Finish:
-    def __init__(self, flows, extra, scalars):
-        sizes = [(f.keep.shape[2], f.keep.shape[3] // STEP) for f in flows]
-        rows = sum(u * n for u, n in sizes) + sum(e.shape[1] for e in extra)
+    def __init__(self, flows, extra, cuts):
+        in_specs, args, sizes = [], [], []
+        for f in flows:
+            specs, arrays = f.kept(0)
+            dims = (1, *f.got.shape[1:])
+            in_specs += specs + [pl.BlockSpec(dims, lambda j, s: (0, 0, 0, 0)), whole(f.last)]
+            args += arrays + [f.got, f.last]
+            sizes.append((len(arrays) + 2, f.got.shape[2], f.got.shape[3] // STEP))
+        in_specs += [whole(e) for e in extra]
+        args += extra
+        rows = sum(u * n for _, u, n in sizes) + sum(e.shape[1] for e in extra)
 
         def kernel(s, *refs):
             send, mine = refs[-2:]
-            zero = s[0] == 0
-            start = 0
-            for i, (u, n) in enumerate(sizes):
-                keep, got, last = refs[3 * i : 3 * i + 3]
-                v = [
-                    keep[0, y].astype(f32) + got[0, y].astype(f32) + last[y].astype(f32)
-                    for y in range(2)
-                ]
+            zero = s[9] == 0
+            start, k = 0, 0
+            for count, u, n in sizes:
+                v = sum(value_of(r) for r in refs[k : k + count])
                 near = jnp.where(zero, v[0], v[1])
                 away = jnp.where(zero, v[1], v[0]).astype(bf16)
-                for k in range(n):
-                    cut = slice(k * STEP, (k + 1) * STEP)
+                for i in range(n):
+                    cut = slice(i * STEP, (i + 1) * STEP)
                     mine[start : start + u, :] = near[:, cut]
                     send[start : start + u, :] = away[:, cut]
                     start += u
-            for ref in refs[3 * len(sizes) : -2]:
+                k += count
+            for ref in refs[k:-2]:
                 u = ref.shape[1]
                 mine[start : start + u, :] = jnp.where(zero, ref[0], ref[1])
                 send[start : start + u, :] = jnp.where(zero, ref[1], ref[0]).astype(bf16)
                 start += u
 
-        in_specs, args = [], []
-        for f in flows:
-            dims = (1, *f.keep.shape[1:])
-            in_specs += [pl.BlockSpec(dims, lambda j, s: (0, 0, 0, 0))] * 2 + [whole(f.last)]
-            args += [f.keep, f.got, f.last]
         out = (shape((rows, STEP), bf16), shape((rows, STEP), f32))
         send, self.mine = call(
-            kernel,
-            out,
-            (1,),
-            in_specs + [whole(e) for e in extra],
-            [whole(o) for o in out],
-            scalars,
-            args + list(extra),
+            kernel, out, (1,), in_specs, [whole(o) for o in out], cuts, args
         )
         self.got = exchange(send, "y", (1, 3))
 
@@ -930,21 +956,21 @@
         (ln1_g, ln1_b, bias_u, bias_v, ln2_g, ln2_b, b_out, conv_b, b_in),
         w_in,
         w_out,
-        conv_w,
         ints(spot),
     )
     piece_got = exchange(piece, "y", (1, 3))
 
-    kv_part, small = pack_rows(w_kv, w_q, w_r, w_o, ints(core))
+    kv_part, small, conv_part = pack_rows(w_kv, w_q, w_r, w_o, conv_w, ints(core))
     kv_got = exchange(kv_part, "y", (1, 3))
     small_got = exchange(small, "y", (1, 3))
+    conv_got = exchange(conv_part, "y", (1, 3))
 
     def joined(w, got, twin):
         return jnp.concatenate([w, got, twin], axis=0)
 
     spread = lax.all_gather(piece_got[:-16], ("x", "z", "c"), axis=0)
     thirds_d = ints(*thirds(D))
-    thirds_c = ints(yl * (3 * D // 2), (1 - yl) * (3 * D // 2), *thirds(D))
+    thirds_c = ints(*thirds(3 * D), *thirds(D))
     sinus_table = sinusoid(KEYS, D).astype(bf16)
     sinus_rel = jnp.concatenate(
         [
@@ -958,11 +984,10 @@
 
     normed, normed_rel, oldest = first_norm(compressed, memory, tokens, vectors, thirds_d)
     both_normed, both_oldest, both_cot = both(normed), both(oldest), both(cotangent)
-    kv_got = gate(kv_got, normed)
+    kv_got, small_got = gate((kv_got, small_got), normed)
     kv_whole = joined(w_kv, kv_got, core_swap(kv_got))
     key_value = dot(normed_rel, kv_whole).astype(bf16)
     line.hold(key_value)
-    small_got = gate(small_got, key_value)
     small_twin = core_swap(small_got)
     q_whole, r_whole, o_whole = [
         joined(w, small_got[i], small_twin[i]) for i, w in enumerate((w_q, w_r, w_o))
@@ -980,7 +1005,7 @@
         cuts += [first, far, own, second]
         rels.append([own, first, second, far])
         twins.append([own, second, first, far])
-    cuts = ints(core, *cuts)
+    cuts = ints(core, *cuts, yl)
 
     def flows(groups):
         pairs = weight_grads(groups, cuts)
@@ -990,6 +1015,8 @@
         normed2_rel, residual, cotangent, w_in, w_out, spread, b_in, vectors, ints(yl)
     )
     both_hidden, both_pre = both(hidden), both(d_pre)
+    (conv_got,) = gate((conv_got,), hidden)
+    conv_pieces = (conv_w, conv_got, core_swap(conv_got))
     d_residual, d_branch, d_attended, d_ln2_g, d_ln2_b, d_b_out = second_norm_back(
         cotangent, d_normed2, residual, vectors, o_whole, thirds_d
     )
@@ -1006,7 +1033,7 @@
     both_kv = (my_kv, core_swap(give_kv))
     both_q, both_rel = both(d_queries), both(d_relative)
 
-    compact, comp_normed = compress(oldest, conv_w, spread, vectors, thirds_c)
+    compact, comp_normed = compress(oldest, conv_pieces, vectors, thirds_c)
     comp_pair = dot(comp_normed, kv_whole).astype(bf16)
     compressed_next = jnp.concatenate([compressed[T // 3 :], compact], axis=0)
     near = flows(
@@ -1016,35 +1043,33 @@
                 "z",
                 [
                     (both_normed, 2, T, both_q, False),
-                    ((sinus_table, sinus_table), 0, KEYS, both_rel, False),
+                    ((sinus_table,), 0, KEYS, both_rel, False),
                 ],
             ),
         ]
     )
     loss, d_ck, d_cv = reconstruct(queries, key_value, comp_pair, none)
     recon_loss = jnp.sum(loss) / (T * D)
-    onward(large, none)
+    onward(large, cuts)
     d_compact, d_conv_b = compress_back(d_ck, d_cv, kv_whole, compact, vectors, thirds_d)
     both_compact = both(d_compact)
-    onward(near, none)
+    onward(near, cuts)
     conv = flows([("x", [(both_oldest, 0, T // 3, both_compact, False)])])
     turn(large, cuts)
-    turn(near, cuts)
-    line.expect(1, *[f.got for f in near])
     d_tokens, d_ln1_g, d_ln1_b = first_norm_back(
         d_kv, d_queries, kv_whole, q_whole, compressed, memory, tokens, vectors, d_residual,
         thirds_d,
     )
-    onward(large, none)
-    onward(conv, none)
-    onward(near, none)
-    line.expect(2, *[f.last for f in near])
-    early = Finish(large, [], ints(yl))
+    turn(near, cuts)
+    line.expect(1, *[f.got for f in near])
+    onward(large, cuts)
+    onward(conv, cuts)
+    onward(near, cuts)
+    early = Finish(large, [], cuts)
     turn(conv, cuts)
     early.second(none)
-    onward(conv, none)
+    onward(conv, cuts)
     early_sums = early.gather(none)
-
     total = jnp.concatenate(
         [d_ln1_g, d_ln1_b, d_bias_u, d_bias_v, d_ln2_g, d_ln2_b, d_b_out, d_conv_b]
         + [d_b_in]
@@ -1057,7 +1082,7 @@
         ],
         axis=1,
     )
-    late = Finish([*near, *conv], [total], ints(yl))
+    late = Finish([*near, *conv], [total], cuts)
     late.second(none)
     late_sums = late.gather(none)
 

time: 424 us -> 418 us (0.986)
  Pallas kernels: 187 us -> 180 us
    pallas_call x38, Pallas kernels: 187 us -> 180 us  [call(): pl.pallas_call(body, out_shape=out, grid_spec=pltpu.PrefetchScalarGridSpe...]
    concatenate x3 -> x2, other arithmetic: 7.95 us -> 2.98 us  [joined(): return jnp.concatenate([w, got, twin], axis=0)]
    all_gather x2, waiting for transfers between devices: 67.6 us -> 62.9 us  [gather(): lax.all_gather(add(self.mine, self.far, none), ('c', 'x', 'z'), axis=0)]
    ppermute x25 -> x26, waiting for transfers between devices: 41.9 us -> 46 us  [exchange(): return lax.ppermute(v, RING[ring], pairs)]
    unnamed x144 -> x152, local copies, waits for them, and re-layouts: 17.8 us -> 21.4 us
    ppermute x25 -> x26, starting transfers between devices: 33.2 us -> 34.6 us  [exchange(): return lax.ppermute(v, RING[ring], pairs)]
  transfers between devices with their start and end apart: 44 -> 46, of which waited for: 15 -> 17; matrix products, arithmetic and copies ran while one was open for 8% -> 7% of each run, Pallas kernels for 33% -> 39%
where the time goes in v3:
time: 418 us; the launch traced here: 412 us
  Pallas kernels  180 us (43%)
  waiting for transfers between devices  124 us (30%)
  starting transfers between devices  41 us (10%)
  local copies, waits for them, and re-layouts  26 us (6%)
  between operations  16.4 us (4%)
  other arithmetic  15.7 us (4%)
  matrix products  9.42 us (2%)
    pallas_call x38, Pallas kernels, call(): pl.pallas_call(body, out_shape=out, grid_spec=pltpu.PrefetchScalarGridSpe...  180 us
    all_gather x2, waiting for transfers between devices, gather(): lax.all_gather(add(self.mine, self.far, none), ('c', 'x', 'z'), axis=0)  62.9 us
    ppermute x26, waiting for transfers between devices, exchange(): return lax.ppermute(v, RING[ring], pairs)  46 us
    ppermute x26, starting transfers between devices, exchange(): return lax.ppermute(v, RING[ring], pairs)  34.6 us
    unnamed x152, local copies, waits for them, and re-layouts  21.4 us
    dot_general x4, matrix products, dot(): return jnp.dot(a, b, preferred_element_type=f32)  9.42 us
    ppermute x2, waiting for transfers between devices, second(): self.far = lax.ppermute(self.mine, 'yh', [(0, 1), (1, 0)])  8.98 us
  transfers between devices with their start and end apart: 46, of which 17 were waited for; matrix products, arithmetic and copies ran while one was open for 7% of the time, Pallas kernels for 39%

profile of v3, /device:TPU:1, one launch (start us, length us, event | category | flops | bytes accessed | tf_op | source)
XLA Modules:
  0.0 412.1 jit_solution(7036734329223125282)
XLA Ops:
  12.7 4.3 %collective-permute-done.refs_1_ = bf16[144,1024]{1,0:T(8,128)(2,1)S(1)} collective-permute-done((bf16[144,1024]{1,0:T(8,128)(2,1)}, bf16[144,1024]{1,0:T(8,128)(2,1)S(1)}, u32[]{:S(2)}, u32[]{:S(2)}) %collective-permute-start) | collective-permute-done | bytes 294944 | tf_op jit(solution)/shard_map/ppermute | solution.py:770
  17.8 4.3 %shard_map.348 = (bf16[256,2048]{1,0:T(8,128)(2,1)}, bf16[3,256,1024]{2,1,0:T(8,128)(2,1)}, bf16[768,1024]{1,0:T(8,128)(2,1)}) custom-call(s32[1]{0:T(128)} %bitcast.8.s, bf16[512,2048]{1,0:T(8,128)(2,1)} %refs_0_.3, bf16[512,1024]{1,0:T(8,128)(2,1)} %refs_1_.4, bf16[512,1024]{1,0:T(8,128)(2,1)} %refs_2_.3, bf16[512,1024]{1,0:T(8,128)(2,1)} %refs_3_.4, ...), custom_call_target="tpu_custom_call" | custom-call | flops 1 | bytes 1 | tf_op jit(solution)/shard_map/pallas_call | solution.py:68
  25.5 4.7 %fusion.10 = (bf16[576,512]{1,0:T(8,128)(2,1)S(1)}, bf16[576,512]{1,0:T(8,128)(2,1)S(1)}) fusion(f32[512]{0:T(512)S(1)} %negate_power_fusion, f32[576]{0:T(1024)S(1)} %subtract_convert_fusion), kind=kLoop, calls=%fused_computation.21 | loop fusion | flops 884736 | bytes 1184000 | tf_op jit(solution)/shard_map/convert.1
  34.4 4.6 %shard_map.350 = (bf16[576,1024]{1,0:T(8,128)(2,1)}, bf16[576,1024]{1,0:T(8,128)(2,1)}, bf16[64,3072]{1,0:T(8,128)(2,1)}) custom-call(s32[3]{0:T(128)} %pad_add_fusion.s, f32[192,1024]{1,0:T(8,128)} %bitcast.88, f32[192,1024]{1,0:T(8,128)} %bitcast.97, bf16[192,1024]{1,0:T(8,128)(2,1)} %bitcast.90, ...), custom_call_target="tpu_custom_call" | custom-call | flops 1 | bytes 1 | tf_op jit(solution)/shard_map/pallas_call | solution.py:68
  39.0 15.1 %collective-permute-done.1.refs_0_ = bf16[256,2048]{1,0:T(8,128)(2,1)S(1)} collective-permute-done((bf16[256,2048]{1,0:T(8,128)(2,1)}, bf16[256,2048]{1,0:T(8,128)(2,1)S(1)}, u32[]{:S(2)}, u32[]{:S(2)}) %collective-permute-start.1) | collective-permute-done | bytes 1048608 | tf_op jit(solution)/shard_map/ppermute | solution.py:770
  61.4 3.9 convolution_convert_fusion.refs_1_.refs_2_.refs_6_
  70.7 7.3 %shard_map.352 = (f32[8,192,640]{2,1,0:T(8,128)}, bf16[192,1024]{1,0:T(8,128)(2,1)}) custom-call(s32[1]{0:T(128)} %constant.10.clone.1.s, f32[192,1024]{1,0:T(8,128)} %fusion.12.refs_0_.refs_7_, bf16[576,2048]{1,0:T(8,128)(2,1)} %convolution_convert_fusion.refs_1_.refs_2_.refs_6_, bf16[576,2048]{1,0:T(8,128)(2,1)} %convolution_convert_fusion.refs_1_.refs_2_.refs_6_, ...), custom_call_target="tpu_custom_call" | custom-call | flops 1 | bytes 1 | tf_op jit(solution)/shard_map/pallas_call | solution.py:68
  79.5 4.1 %shard_map.353 = (f32[192,1024]{1,0:T(8,128)}, bf16[192,1024]{1,0:T(8,128)(2,1)}, bf16[192,1024]{1,0:T(8,128)(2,1)}) custom-call(s32[3]{0:T(128)} %pad_add_fusion.s, bf16[192,1024]{1,0:T(8,128)(2,1)} %get-tuple-element.96.refs_0_.refs_12_.refs_13_, bf16[1024,1024]{1,0:T(8,128)(2,1)} %pad_maximum_fusion.1.refs_1_.refs_4_, bf16[192,1024]{1,0:T(8,128)(2,1)} %bitcast.91, ...), custom_call_target="tpu_custom_call" | custom-call | flops 1 | bytes 1 | tf_op jit(solution)/shard_map/pallas_call | solution.py:68
  83.7 16.4 %shard_map.354 = (bf16[192,4096]{1,0:T(8,128)(2,1)}, bf16[192,4096]{1,0:T(8,128)(2,1)}, bf16[192,1024]{1,0:T(8,128)(2,1)}, f32[192,1024]{1,0:T(8,128)}, f32[4,1024]{1,0:T(4,128)}) custom-call(s32[1]{0:T(128)} %bitcast.s, bf16[192,1024]{1,0:T(8,128)(2,1)} %get-tuple-element.98.refs_0_, f32[192,1024]{1,0:T(8,128)} %get-tuple-element.99.refs_1_.refs_9_.refs_2_, ...), custom_call_target="tpu_custom_call" | custom-call | flops 1 | bytes 1 | tf_op jit(solution)/shard_map/pallas_call | solution.py:68
  101.2 4.8 %collective-permute-done.8.refs_5_ = bf16[192,1024]{1,0:T(8,128)(2,1)S(1)} collective-permute-done((bf16[192,1024]{1,0:T(8,128)(2,1)S(1)}, bf16[192,1024]{1,0:T(8,128)(2,1)S(1)}, u32[]{:S(2)}, u32[]{:S(2)}) %collective-permute-start.8) | collective-permute-done | bytes 393248 | tf_op jit(solution)/shard_map/ppermute | solution.py:758
  106.5 5.0 %shard_map.356 = (f32[192,1024]{1,0:T(8,128)}, bf16[192,1024]{1,0:T(8,128)(2,1)}, bf16[192,1024]{1,0:T(8,128)(2,1)}, f32[1,1024]{1,0:T(1,128)}, f32[1,1024]{1,0:T(1,128)}, /*index=5*/f32[1,1024]{1,0:T(1,128)}) custom-call(s32[3]{0:T(128)} %pad_add_fusion.s, bf16[192,1024]{1,0:T(8,128)(2,1)} %bitcast.94, f32[192,1024]{1,0:T(8,128)} %get-tuple-element.105.refs_1_, ...), custom_call_target="tpu_custom_call" | custom-call | flops 1 | bytes 1 | tf_op jit(solution)/shard_map/pallas_call | solution.py:68
  115.6 11.6 %shard_map.357 = (bf16[2,2,512,512]{3,2,1,0:T(8,128)(2,1)}, bf16[2,2,512,512]{3,2,1,0:T(8,128)(2,1)}, bf16[2,2,128,2560]{3,2,1,0:T(8,128)(2,1)}, bf16[2,2,128,2560]{3,2,1,0:T(8,128)(2,1)}) custom-call(s32[10]{0:T(128)} %stack.86.s, bf16[192,4096]{1,0:T(8,128)(2,1)} %get-tuple-element.104.refs_1_.refs_5_.refs_0_, ...), custom_call_target="tpu_custom_call" | custom-call | flops 1 | bytes 1 | tf_op jit(solution)/shard_map/pallas_call | solution.py:68
  127.2 3.9 collective-permute-start.18
  133.7 8.9 %shard_map.358 = (bf16[2,576,1024]{2,1,0:T(8,128)(2,1)}, bf16[576,1024]{1,0:T(8,128)(2,1)}, bf16[576,1024]{1,0:T(8,128)(2,1)}, bf16[576,1024]{1,0:T(8,128)(2,1)}...) custom-call(s32[1]{0:T(128)} %bitcast.8.s, f32[192,1024]{1,0:T(8,128)} %fusion.12.refs_0_.refs_7_, ...), custom_call_target="tpu_custom_call" | custom-call | flops 1 | bytes 1 | tf_op jit(solution)/shard_map/pallas_call | solution.py:68
  146.3 6.1 %shard_map.359 = (f32[64,1024]{1,0:T(8,128)}, bf16[64,1024]{1,0:T(8,128)(2,1)}) custom-call(s32[6]{0:T(128)} %stack.77.s, bf16[64,3072]{1,0:T(8,128)(2,1)} %get-tuple-element.102.refs_0_.refs_1_, bf16[1536,1024]{1,0:T(8,128)(2,1)} %refs_1_.5, bf16[768,1024]{1,0:T(8,128)(2,1)} %shard_map.355.refs_2_, bf16[768,1024]{1,0:T(8,128)(2,1)} %collective-permute-done.6.refs_3_, ...), custom_call_target="tpu_custom_call" | custom-call | flops 1 | bytes 1 | tf_op jit(solution)/shard_map/pallas_call | solution.py:68
  153.4 10.8 %shard_map.360 = (bf16[2,2,128,1024]{3,2,1,0:T(8,128)(2,1)}, bf16[2,2,128,1024]{3,2,1,0:T(8,128)(2,1)}, bf16[2,2,128,1024]{3,2,1,0:T(8,128)(2,1)}, bf16[2,2,128,1024]{3,2,1,0:T(8,128)(2,1)}) custom-call(s32[10]{0:T(128)} %stack.86.s, bf16[576,1024]{1,0:T(8,128)(2,1)} %get-tuple-element.93.refs_2_.refs_5_.refs_0_.refs_1_.refs_6_.refs_7_, ...), custom_call_target="tpu_custom_call" | custom-call | flops 1 | bytes 1 | tf_op jit(solution)/shard_map/pallas_call | solution.py:68
  166.9 4.6 %shard_map.361 = (f32[1,128]{1,0:T(1,128)}, bf16[64,1024]{1,0:T(8,128)(2,1)}, bf16[64,1024]{1,0:T(8,128)(2,1)}) custom-call(s32[1]{0:T(128)} %constant.10.clone.1.s, f32[192,1024]{1,0:T(8,128)} %fusion.12.refs_0_.refs_7_, bf16[576,2048]{1,0:T(8,128)(2,1)} %convolution_convert_fusion.refs_1_.refs_2_.refs_6_, ...), custom_call_target="tpu_custom_call" | custom-call | flops 1 | bytes 1 | tf_op jit(solution)/shard_map/pallas_call | solution.py:68
  172.8 4.8 %shard_map.362 = (bf16[2,512,512]{2,1,0:T(8,128)(2,1)}, bf16[2,128,2560]{2,1,0:T(8,128)(2,1)}) custom-call(s32[10]{0:T(128)} %stack.86.s, bf16[2,2,512,512]{3,2,1,0:T(8,128)(2,1)} %get-tuple-element.121.refs_0_, bf16[2,2,512,512]{3,2,1,0:T(8,128)(2,1)} %copy-done.3, bf16[2,2,128,2560]{3,2,1,0:T(8,128)(2,1)} %get-tuple-element.122.refs_2_.refs_3_.refs_4_.refs_5_, ...), custom_call_target="tpu_custom_call" | custom-call | flops 1 | bytes 1 | tf_op jit(solution)/shard_map/pallas_call | solution.py:68
  179.6 5.3 %shard_map.363 = (bf16[64,1024]{1,0:T(8,128)(2,1)}, f32[1,1024]{1,0:T(1,128)}) custom-call(s32[3]{0:T(128)} %pad_add_fusion.s, bf16[64,1024]{1,0:T(8,128)(2,1)} %get-tuple-element.126.refs_0_, bf16[64,1024]{1,0:T(8,128)(2,1)} %get-tuple-element.127.refs_1_, bf16[1024,2048]{1,0:T(8,128)(2,1)} %copy-done, f32[64,1024]{1,0:T(8,128)} %get-tuple-element.113.refs_16_.refs_3_, ...), custom_call_target="tpu_custom_call" | custom-call | flops 1 | bytes 1 | tf_op jit(solution)/shard_map/pallas_call | solution.py:68
  191.1 5.4 %shard_map.365 = (bf16[2,2,384,512]{3,2,1,0:T(8,128)(2,1)}, bf16[2,2,384,512]{3,2,1,0:T(8,128)(2,1)}) custom-call(s32[10]{0:T(128)} %stack.86.s, bf16[64,3072]{1,0:T(8,128)(2,1)} %get-tuple-element.102.refs_0_.refs_1_, bf16[64,3072]{1,0:T(8,128)(2,1)} %get-tuple-element.102.refs_0_.refs_1_, bf16[64,3072]{1,0:T(8,128)(2,1)} %copy-done.36, ...), custom_call_target="tpu_custom_call" | custom-call | flops 1 | bytes 1 | tf_op jit(solution)/shard_map/pallas_call | solution.py:68
  200.0 3.7 shard_map.366
  209.4 9.4 %shard_map.367 = (f32[192,1024]{1,0:T(8,128)}, f32[1,1024]{1,0:T(1,128)}, f32[1,1024]{1,0:T(1,128)}) custom-call(s32[3]{0:T(128)} %pad_add_fusion.s, bf16[2,576,1024]{2,1,0:T(8,128)(2,1)} %get-tuple-element.112.refs_5_.refs_0_, bf16[192,1024]{1,0:T(8,128)(2,1)} %get-tuple-element.117.refs_10_.refs_1_, bf16[1024,2048]{1,0:T(8,128)(2,1)} %copy-done, ...), custom_call_target="tpu_custom_call" | custom-call | flops 1 | bytes 1 | tf_op jit(solution)/shard_map/pallas_call | solution.py:68
  224.0 5.9 %collective-permute-done.31.refs_7_.refs_8_ = bf16[2,2,32,2560]{3,2,1,0:T(8,128)(2,1)S(1)} collective-permute-done((bf16[2,2,32,2560]{3,2,1,0:T(8,128)(2,1)}, bf16[2,2,32,2560]{3,2,1,0:T(8,128)(2,1)S(1)}, u32[]{:S(2)}, u32[]{:S(2)}) %collective-permute-start.31) | collective-permute-done | bytes 655392 | tf_op jit(solution)/shard_map/ppermute | solution.py:770
  245.5 7.9 %collective-permute-done.36.refs_9_ = bf16[2,32,2560]{2,1,0:T(8,128)(2,1)S(1)} collective-permute-done((bf16[2,32,2560]{2,1,0:T(8,128)(2,1)S(1)}, bf16[2,32,2560]{2,1,0:T(8,128)(2,1)S(1)}, u32[]{:S(2)}, u32[]{:S(2)}) %collective-permute-start.36) | collective-permute-done | bytes 327712 | tf_op jit(solution)/shard_map/ppermute | solution.py:770
  254.1 3.8 shard_map.372
  292.1 3.8 collective-permute-done.41.refs_1_
  298.5 6.8 %collective-permute-done.42.refs_1_ = bf16[240,512]{1,0:T(8,128)(2,1)S(1)} collective-permute-done((bf16[240,512]{1,0:T(8,128)(2,1)}, bf16[240,512]{1,0:T(8,128)(2,1)S(1)}, u32[]{:S(2)}, u32[]{:S(2)}) %collective-permute-start.42) | collective-permute-done | bytes 245792 | tf_op jit(solution)/shard_map/ppermute | solution.py:911
  308.8 24.9 %all-gather.11.cloned.1.call-done = bf16[9216,512]{1,0:T(8,128)(2,1)} async-done(((bf16[288,512]{1,0:T(8,128)(2,1)}), bf16[9216,512]{1,0:T(8,128)(2,1)}) %all-gather.11.cloned.1.call-update) | async-done | bytes 9437200 | tf_op jit(solution)/shard_map/all_gather | solution.py:914
  333.7 5.2 %shard_map.380.refs_1_ = f32[16,32,4096]{2,1,0:T(8,128)} custom-call(s32[1]{0:T(128)} %constant.10.clone.1.s, bf16[32,288,512]{2,1,0:T(8,128)(2,1)} %bitcast.68, bf16[32,288,512]{2,1,0:T(8,128)(2,1)} %bitcast.69, bf16[32,288,512]{2,1,0:T(8,128)(2,1)} %bitcast.70, bf16[32,288,512]{2,1,0:T(8,128)(2,1)} %bitcast.71, bf16[240,512]{1,0:T(8,128)(2,1)} %shard_map.379.refs_4_), custom_call_target="tpu_custom_call" | custom-call | flops 1 | bytes 1 | tf_op jit(solution)/shard_map/pallas_call | solution.py:68
  339.5 7.3 %shard_map.381.refs_1_ = f32[16,128,1024]{2,1,0:T(8,128)} custom-call(s32[1]{0:T(128)} %constant.10.clone.1.s, bf16[32,288,512]{2,1,0:T(8,128)(2,1)} %bitcast.72, f32[16,32,4096]{2,1,0:T(8,128)} %shard_map.380.refs_1_), custom_call_target="tpu_custom_call" | custom-call | flops 1 | bytes 1 | tf_op jit(solution)/shard_map/pallas_call | solution.py:68
  349.9 38.0 %all-gather.9.cloned.1.call-done = bf16[7680,512]{1,0:T(8,128)(2,1)} async-done(((bf16[240,512]{1,0:T(8,128)(2,1)}), bf16[7680,512]{1,0:T(8,128)(2,1)}) %all-gather.9.cloned.1.call-update) | async-done | bytes 7864336 | tf_op jit(solution)/shard_map/all_gather | solution.py:914
  389.1 5.8 %shard_map.383.refs_2_ = f32[16,96,1024]{2,1,0:T(8,128)} custom-call(s32[1]{0:T(128)} %constant.10.clone.1.s, bf16[32,240,512]{2,1,0:T(8,128)(2,1)} %bitcast.75, f32[16,32,1024]{2,1,0:T(8,128)} %shard_map.382.refs_1_), custom_call_target="tpu_custom_call" | custom-call | flops 1 | bytes 1 | tf_op jit(solution)/shard_map/pallas_call | solution.py:68
  (285 shorter events, 137.4 us)
Async XLA Ops:
  7.2 76.5 %all-gather.7.cloned.1.call-start = ((), (), s32[]{:S(2)}) async-start(), calls=%async_computation | async-start | bytes 8650752 | tf_op jit(solution)/shard_map/all_gather | solution.py:971
  17.8 315.9 %all-gather.11.cloned.1.call-start = ((), (), s32[]{:S(2)}) async-start(), calls=%async_computation.2 | async-start | bytes 9732096 | tf_op jit(solution)/shard_map/all_gather | solution.py:914
  22.1 31.9 %collective-permute-start.2 = (bf16[3,256,1024]{2,1,0:T(8,128)(2,1)}, bf16[3,256,1024]{2,1,0:T(8,128)(2,1)}, u32[]{:S(2)}, u32[]{:S(2)}) collective-permute-start(bf16[3,256,1024]{2,1,0:T(8,128)(2,1)} %get-tuple-element.92), channel_id=1, source_target_pairs={{0,1},{2,67},{1,0},{3,66},{64,65},{66,3},{65,64},{67,2},{4,5},{6,7... | collective-permute-start | bytes 4718600 | tf_op jit(solution)/shard_map/ppermute | solution.py:770
  24.8 29.2 %collective-permute-start.1 = (bf16[256,2048]{1,0:T(8,128)(2,1)}, bf16[256,2048]{1,0:T(8,128)(2,1)S(1)}, u32[]{:S(2)}, u32[]{:S(2)}) collective-permute-start(bf16[256,2048]{1,0:T(8,128)(2,1)} %get-tuple-element.89.refs_2_), channel_id=1, source_target_pairs={{0,1},{2,67},{1,0},{3,66},{64,65},{66,3},{65,64},{67,2},{4,5},{6,7... | collective-permute-start | bytes 3145736 | tf_op jit(solution)/shard_map/ppermute | solution.py:770
  55.4 50.7 %collective-permute-start.5 = (bf16[768,1024]{1,0:T(8,128)(2,1)}, bf16[768,1024]{1,0:T(8,128)(2,1)}, u32[]{:S(2)}, u32[]{:S(2)}) collective-permute-start(bf16[768,1024]{1,0:T(8,128)(2,1)} %get-tuple-element.103), channel_id=1, source_target_pairs={{0,1},{2,67},{1,0},{3,66},{64,65},{66,3},{65,64},{67,2},{4,5},{6,7... | collective-permute-start | bytes 4718600 | tf_op jit(solution)/shard_map/ppermute | solution.py:770
  100.1 14.3 %collective-permute-start.10 = (bf16[192,4096]{1,0:T(8,128)(2,1)}, bf16[192,4096]{1,0:T(8,128)(2,1)}, u32[]{:S(2)}, u32[]{:S(2)}) collective-permute-start(bf16[192,4096]{1,0:T(8,128)(2,1)} %get-tuple-element.108.refs_10_), channel_id=1, source_target_pairs={{0,2},{2,0},{1,3},{3,1},{4,6},{6,4},{5,7},{7,5},{8,10},{10,8},{9,1... | collective-permute-start | bytes 4718600 | tf_op jit(solution)/shard_map/ppermute | solution.py:758
  100.2 14.2 %collective-permute-start.7 = (bf16[192,4096]{1,0:T(8,128)(2,1)}, bf16[192,4096]{1,0:T(8,128)(2,1)S(1)}, u32[]{:S(2)}, u32[]{:S(2)}) collective-permute-start(bf16[192,4096]{1,0:T(8,128)(2,1)} %get-tuple-element.104.refs_1_.refs_5_.refs_0_), channel_id=1, source_target_pairs={{0,2},{2,0},{1,3},{3,1},{4,6},{6,4},{5,7},{7,5},{8,10},{10,8},{9,1... | collective-permute-start | bytes 4718600 | tf_op jit(solution)/shard_map/ppermute | solution.py:758
  100.8 10.8 %collective-permute-start.9 = (bf16[192,1024]{1,0:T(8,128)(2,1)S(1)}, bf16[192,1024]{1,0:T(8,128)(2,1)S(1)}, u32[]{:S(2)}, u32[]{:S(2)}) collective-permute-start(bf16[192,1024]{1,0:T(8,128)(2,1)S(1)} %copy-done.37), channel_id=1, source_target_pairs={{0,2},{2,0},{1,3},{3,1},{4,6},{6,4},{5,7},{7,5},{8,10},{10,8},{9,1... | collective-permute-start | bytes 1179656 | tf_op jit(solution)/shard_map/ppermute | solution.py:758
  106.2 36.5 %collective-permute-start.13 = (bf16[576,1024]{1,0:T(8,128)(2,1)S(1)}, bf16[576,1024]{1,0:T(8,128)(2,1)}, u32[]{:S(2)}, u32[]{:S(2)}) collective-permute-start(bf16[576,1024]{1,0:T(8,128)(2,1)S(1)} %copy-done.2), channel_id=1, source_target_pairs={{0,2},{2,0},{1,3},{3,1},{4,6},{6,4},{5,7},{7,5},{8,10},{10,8},{9,1... | collective-permute-start | bytes 3538952 | tf_op jit(solution)/shard_map/ppermute | solution.py:758
  112.4 30.8 %collective-permute-start.6 = (bf16[768,1024]{1,0:T(8,128)(2,1)}, bf16[768,1024]{1,0:T(8,128)(2,1)}, u32[]{:S(2)}, u32[]{:S(2)}) collective-permute-start(bf16[768,1024]{1,0:T(8,128)(2,1)} %shard_map.355.refs_2_), channel_id=1, source_target_pairs={{0,2},{2,0},{1,3},{3,1},{4,6},{6,4},{5,7},{7,5},{8,10},{10,8},{9,1... | collective-permute-start | bytes 4718600 | tf_op jit(solution)/shard_map/ppermute | solution.py:758
  127.2 44.4 %collective-permute-start.18 = (bf16[2,2,128,2560]{3,2,1,0:T(8,128)(2,1)}, bf16[2,2,128,2560]{3,2,1,0:T(8,128)(2,1)}, u32[]{:S(2)}, u32[]{:S(2)}) collective-permute-start(bf16[2,2,128,2560]{3,2,1,0:T(8,128)(2,1)} %get-tuple-element.123), channel_id=1, source_target_pairs={{0,4},{2,14},{4,0},{6,10},{8,12},{10,6},{12,8},{14,2},{1,5},{3,15}... | collective-permute-start | bytes 7864328 | tf_op jit(solution)/shard_map/ppermute | solution.py:770
  131.0 40.5 %collective-permute-start.17 = (bf16[2,2,512,512]{3,2,1,0:T(8,128)(2,1)}, bf16[2,2,512,512]{3,2,1,0:T(8,128)(2,1)S(1)}, u32[]{:S(2)}, u32[]{:S(2)}) collective-permute-start(bf16[2,2,512,512]{3,2,1,0:T(8,128)(2,1)} %get-tuple-element.111.refs_7_), channel_id=1, source_target_pairs={{0,16},{2,50},{16,0},{18,34},{32,48},{34,18},{48,32},{50,2},{1,17}... | collective-permute-start | bytes 6291464 | tf_op jit(solution)/shard_map/ppermute | solution.py:770
  142.6 9.8 %collective-permute-start.14 = (bf16[576,1024]{1,0:T(8,128)(2,1)}, bf16[576,1024]{1,0:T(8,128)(2,1)}, u32[]{:S(2)}, u32[]{:S(2)}) collective-permute-start(bf16[576,1024]{1,0:T(8,128)(2,1)} %get-tuple-element.116), channel_id=1, source_target_pairs={{0,2},{2,0},{1,3},{3,1},{4,6},{6,4},{5,7},{7,5},{8,10},{10,8},{9,1... | collective-permute-start | bytes 3538952 | tf_op jit(solution)/shard_map/ppermute | solution.py:758
  142.7 9.7 %collective-permute-start.16 = (bf16[576,1024]{1,0:T(8,128)(2,1)}, bf16[576,1024]{1,0:T(8,128)(2,1)S(1)}, u32[]{:S(2)}, u32[]{:S(2)}) collective-permute-start(bf16[576,1024]{1,0:T(8,128)(2,1)} %get-tuple-element.118.refs_14_), channel_id=1, source_target_pairs={{0,2},{2,0},{1,3},{3,1},{4,6},{6,4},{5,7},{7,5},{8,10},{10,8},{9,1... | collective-permute-start | bytes 3538952 | tf_op jit(solution)/shard_map/ppermute | solution.py:758
  143.2 9.2 %collective-permute-start.15 = (bf16[192,1024]{1,0:T(8,128)(2,1)}, bf16[192,1024]{1,0:T(8,128)(2,1)}, u32[]{:S(2)}, u32[]{:S(2)}) collective-permute-start(bf16[192,1024]{1,0:T(8,128)(2,1)} %get-tuple-element.117.refs_10_.refs_1_), channel_id=1, source_target_pairs={{0,2},{2,0},{1,3},{3,1},{4,6},{6,4},{5,7},{7,5},{8,10},{10,8},{9,1... | collective-permute-start | bytes 1179656 | tf_op jit(solution)/shard_map/ppermute | solution.py:758
  164.2 20.7 %collective-permute-start.23 = (bf16[2,2,128,1024]{3,2,1,0:T(8,128)(2,1)}, bf16[2,2,128,1024]{3,2,1,0:T(8,128)(2,1)S(1)}, u32[]{:S(2)}, u32[]{:S(2)}) collective-permute-start(bf16[2,2,128,1024]{3,2,1,0:T(8,128)(2,1)} %get-tuple-element.119.refs_5_), channel_id=1, source_target_pairs={{0,16},{2,50},{16,0},{18,34},{32,48},{34,18},{48,32},{50,2},{1,17}... | collective-permute-start | bytes 3145736 | tf_op jit(solution)/shard_map/ppermute | solution.py:770
  164.3 22.7 %collective-permute-start.24 = (bf16[2,2,128,1024]{3,2,1,0:T(8,128)(2,1)}, bf16[2,2,128,1024]{3,2,1,0:T(8,128)(2,1)}, u32[]{:S(2)}, u32[]{:S(2)}) collective-permute-start(bf16[2,2,128,1024]{3,2,1,0:T(8,128)(2,1)} %get-tuple-element.131), channel_id=1, source_target_pairs={{0,4},{2,14},{4,0},{6,10},{8,12},{10,6},{12,8},{14,2},{1,5},{3,15}... | collective-permute-start | bytes 3145736 | tf_op jit(solution)/shard_map/ppermute | solution.py:770
  177.6 20.3 %collective-permute-start.20 = (bf16[2,128,2560]{2,1,0:T(8,128)(2,1)}, bf16[2,128,2560]{2,1,0:T(8,128)(2,1)S(1)}, u32[]{:S(2)}, u32[]{:S(2)}) collective-permute-start(bf16[2,128,2560]{2,1,0:T(8,128)(2,1)} %get-tuple-element.125), channel_id=1, source_target_pairs={{0,12},{2,6},{4,8},{6,2},{8,4},{10,14},{12,0},{14,10},{1,13},{3,7}... | collective-permute-start | bytes 3932168 | tf_op jit(solution)/shard_map/ppermute | solution.py:770
  178.4 11.9 %collective-permute-start.21 = (bf16[64,3072]{1,0:T(8,128)(2,1)S(1)}, bf16[64,3072]{1,0:T(8,128)(2,1)S(1)}, u32[]{:S(2)}, u32[]{:S(2)}) collective-permute-start(bf16[64,3072]{1,0:T(8,128)(2,1)S(1)} %copy-done.21), channel_id=1, source_target_pairs={{0,2},{2,0},{1,3},{3,1},{4,6},{6,4},{5,7},{7,5},{8,10},{10,8},{9,1... | collective-permute-start | bytes 1179656 | tf_op jit(solution)/shard_map/ppermute | solution.py:758
  178.4 19.5 %collective-permute-start.19 = (bf16[2,512,512]{2,1,0:T(8,128)(2,1)}, bf16[2,512,512]{2,1,0:T(8,128)(2,1)S(1)}, u32[]{:S(2)}, u32[]{:S(2)}) collective-permute-start(bf16[2,512,512]{2,1,0:T(8,128)(2,1)} %get-tuple-element.124.refs_5_), channel_id=1, source_target_pairs={{0,48},{2,18},{16,32},{18,2},{32,16},{34,50},{48,0},{50,34},{1,49}... | collective-permute-start | bytes 3145736 | tf_op jit(solution)/shard_map/ppermute | solution.py:770
  196.5 37.5 %collective-permute-start.29 = (bf16[2,2,384,512]{3,2,1,0:T(8,128)(2,1)}, bf16[2,2,384,512]{3,2,1,0:T(8,128)(2,1)S(1)}, u32[]{:S(2)}, u32[]{:S(2)}) collective-permute-start(bf16[2,2,384,512]{3,2,1,0:T(8,128)(2,1)} %get-tuple-element.133.refs_6_), channel_id=1, source_target_pairs={{0,16},{2,50},{16,0},{18,34},{32,48},{34,18},{48,32},{50,2},{1,17}... | collective-permute-start | bytes 4718600 | tf_op jit(solution)/shard_map/ppermute | solution.py:770
  197.2 21.7 %collective-permute-start.25 = (bf16[2,128,1024]{2,1,0:T(8,128)(2,1)S(1)}, bf16[2,128,1024]{2,1,0:T(8,128)(2,1)S(1)}, u32[]{:S(2)}, u32[]{:S(2)}) collective-permute-start(bf16[2,128,1024]{2,1,0:T(8,128)(2,1)S(1)} %copy-done.45), channel_id=1, source_target_pairs={{0,48},{2,18},{16,32},{18,2},{32,16},{34,50},{48,0},{50,34},{1,49}... | collective-permute-start | bytes 1572872 | tf_op jit(solution)/shard_map/ppermute | solution.py:770
  197.6 21.3 %collective-permute-start.26 = (bf16[2,128,1024]{2,1,0:T(8,128)(2,1)S(1)}, bf16[2,128,1024]{2,1,0:T(8,128)(2,1)S(1)}, u32[]{:S(2)}, u32[]{:S(2)}) collective-permute-start(bf16[2,128,1024]{2,1,0:T(8,128)(2,1)S(1)} %copy-done.71), channel_id=1, source_target_pairs={{0,12},{2,6},{4,8},{6,2},{8,4},{10,14},{12,0},{14,10},{1,13},{3,7}... | collective-permute-start | bytes 1572872 | tf_op jit(solution)/shard_map/ppermute | solution.py:770
  203.7 26.2 %collective-permute-start.31 = (bf16[2,2,32,2560]{3,2,1,0:T(8,128)(2,1)}, bf16[2,2,32,2560]{3,2,1,0:T(8,128)(2,1)S(1)}, u32[]{:S(2)}, u32[]{:S(2)}) collective-permute-start(bf16[2,2,32,2560]{3,2,1,0:T(8,128)(2,1)} %get-tuple-element.140), channel_id=1, source_target_pairs={{0,16},{2,50},{16,0},{18,34},{32,48},{34,18},{48,32},{50,2},{1,17}... | collective-permute-start | bytes 1966088 | tf_op jit(solution)/shard_map/ppermute | solution.py:770
  205.3 18.6 %collective-permute-start.30 = (bf16[2,2,128,512]{3,2,1,0:T(8,128)(2,1)}, bf16[2,2,128,512]{3,2,1,0:T(8,128)(2,1)S(1)}, u32[]{:S(2)}, u32[]{:S(2)}) collective-permute-start(bf16[2,2,128,512]{3,2,1,0:T(8,128)(2,1)} %get-tuple-element.134.refs_9_), channel_id=1, source_target_pairs={{0,4},{2,14},{4,0},{6,10},{8,12},{10,6},{12,8},{14,2},{1,5},{3,15}... | collective-permute-start | bytes 1572872 | tf_op jit(solution)/shard_map/ppermute | solution.py:770
  222.9 11.1 %collective-permute-start.27 = (bf16[2,2,32,1024]{3,2,1,0:T(8,128)(2,1)}, bf16[2,2,32,1024]{3,2,1,0:T(8,128)(2,1)S(1)}, u32[]{:S(2)}, u32[]{:S(2)}) collective-permute-start(bf16[2,2,32,1024]{3,2,1,0:T(8,128)(2,1)} %get-tuple-element.137.refs_8_), channel_id=1, source_target_pairs={{0,4},{2,14},{4,0},{6,10},{8,12},{10,6},{12,8},{14,2},{1,5},{3,15}... | collective-permute-start | bytes 786440 | tf_op jit(solution)/shard_map/ppermute | solution.py:770
  222.9 11.0 %collective-permute-start.28 = (bf16[2,2,32,1024]{3,2,1,0:T(8,128)(2,1)}, bf16[2,2,32,1024]{3,2,1,0:T(8,128)(2,1)S(1)}, u32[]{:S(2)}, u32[]{:S(2)}) collective-permute-start(bf16[2,2,32,1024]{3,2,1,0:T(8,128)(2,1)} %get-tuple-element.138), channel_id=1, source_target_pairs={{0,16},{2,50},{16,0},{18,34},{32,48},{34,18},{48,32},{50,2},{1,17}... | collective-permute-start | bytes 786440 | tf_op jit(solution)/shard_map/ppermute | solution.py:770
  238.5 20.1 %collective-permute-start.34 = (bf16[2,384,512]{2,1,0:T(8,128)(2,1)}, bf16[2,384,512]{2,1,0:T(8,128)(2,1)S(1)}, u32[]{:S(2)}, u32[]{:S(2)}) collective-permute-start(bf16[2,384,512]{2,1,0:T(8,128)(2,1)} %shard_map.370.refs_8_), channel_id=1, source_target_pairs={{0,48},{2,18},{16,32},{18,2},{32,16},{34,50},{48,0},{50,34},{1,49}... | collective-permute-start | bytes 2359304 | tf_op jit(solution)/shard_map/ppermute | solution.py:770
  238.5 14.9 %collective-permute-start.36 = (bf16[2,32,2560]{2,1,0:T(8,128)(2,1)S(1)}, bf16[2,32,2560]{2,1,0:T(8,128)(2,1)S(1)}, u32[]{:S(2)}, u32[]{:S(2)}) collective-permute-start(bf16[2,32,2560]{2,1,0:T(8,128)(2,1)S(1)} %copy-done.72), channel_id=1, source_target_pairs={{0,48},{2,18},{16,32},{18,2},{32,16},{34,50},{48,0},{50,34},{1,49}... | collective-permute-start | bytes 983048 | tf_op jit(solution)/shard_map/ppermute | solution.py:770
  262.3 8.0 %collective-permute-start.37 = (bf16[2,2,96,512]{3,2,1,0:T(8,128)(2,1)}, bf16[2,2,96,512]{3,2,1,0:T(8,128)(2,1)S(1)}, u32[]{:S(2)}, u32[]{:S(2)}) collective-permute-start(bf16[2,2,96,512]{3,2,1,0:T(8,128)(2,1)} %shard_map.373.refs_2_), channel_id=1, source_target_pairs={{0,4},{2,14},{4,0},{6,10},{8,12},{10,6},{12,8},{14,2},{1,5},{3,15}... | collective-permute-start | bytes 1179656 | tf_op jit(solution)/shard_map/ppermute | solution.py:770
  267.6 8.4 %collective-permute-start.40 = (bf16[288,512]{1,0:T(8,128)(2,1)}, bf16[288,512]{1,0:T(8,128)(2,1)S(1)}, u32[]{:S(2)}, u32[]{:S(2)}) collective-permute-start(bf16[288,512]{1,0:T(8,128)(2,1)} %shard_map.374.refs_4_.refs_0_), channel_id=1, source_target_pairs={{0,64},{64,0},{1,65},{65,1},{2,66},{66,2},{3,67},{67,3},{4,68},{68... | collective-permute-start | bytes 884744 | tf_op jit(solution)/shard_map/ppermute | solution.py:911
  278.5 109.4 %all-gather.9.cloned.1.call-start = ((), (), s32[]{:S(2)}) async-start(), calls=%async_computation.1 | async-start | bytes 8110080 | tf_op jit(solution)/shard_map/all_gather | solution.py:914
  (88 other events, 510.3 us)
Sparse Core Ops, SparseCore 0:
  17.9 55.7 all-gather.6
  278.6 54.9 all-gather.10
  336.5 51.3 all-gather.8

commit v4 on v3

--- a/solution.py
+++ b/solution.py
@@ -76,7 +76,6 @@
             scratch_shapes=list(scratch),
         ),
         compiler_params=pltpu.CompilerParams(vmem_limit_bytes=56 << 20),
-        cost_estimate=pl.CostEstimate(flops=1, bytes_accessed=1, transcendentals=0),
     )(scalars, *args, *held)
     line.ran(jax.tree.leaves(result)[0])
     return result
@@ -728,30 +727,44 @@
     return [(flat[2 * i], flat[2 * i + 1]) for i in range(len(groups))]
 
 
-def widen(gathered, start, rows, columns, swapped, none):
-    u = rows // 16
-    sub = u // 32
-    chunks = columns // 2 // STEP
-    order = [x * 4 + z for z in range(4) for x in range(4)] if swapped else list(range(16))
-
-    def kernel(_, *refs):
-        out = refs[-1]
-        for k, src in enumerate(refs[:-1]):
-            for to, frm in enumerate(order):
-                out[to, :, k * STEP : (k + 1) * STEP] = src[frm].astype(f32)
-
-    return call(
+def widen(gathered, plan, none):
+    outs, specs, layout = [], [], []
+    start = 0
+    for rows, columns, ring in plan:
+        u, chunks = rows // 16, columns // 2 // STEP
+        outs.append(shape((4, 4, u, columns), f32))
+        if ring == "x":
+            specs.append(
+                pl.BlockSpec((1, 4, u, chunks * STEP), lambda c, x, s: (x, 0, 0, c))
+            )
+        else:
+            specs.append(
+                pl.BlockSpec((4, 1, u, chunks * STEP), lambda c, x, s: (0, x, 0, c))
+            )
+        layout.append((start, u, chunks, ring))
+        start += u * chunks
+
+    def kernel(_, src, *results):
+        for out, (start, u, chunks, ring) in zip(results, layout):
+            for k in range(chunks):
+                cut = slice(k * STEP, (k + 1) * STEP)
+                for z in range(4):
+                    value = src[z, start + k * u : start + (k + 1) * u, :].astype(f32)
+                    if ring == "x":
+                        out[0, z, :, cut] = value
+                    else:
+                        out[z, 0, :, cut] = value
+
+    results = call(
         kernel,
-        shape((16, u, columns), f32),
-        (sub, 2),
-        [
-            pl.BlockSpec((16, 32, STEP), lambda i, c, s, k=k: (c, start // 32 + k * sub + i, 0))
-            for k in range(chunks)
-        ],
-        pl.BlockSpec((16, 32, STEP * chunks), lambda i, c, s: (0, i, c)),
+        tuple(outs),
+        (2, 4),
+        [pl.BlockSpec((4, gathered.shape[1], STEP), lambda c, x, s: (c * 4 + x, 0, 0))],
+        specs,
         none,
-        (gathered,) * chunks,
-    ).reshape(rows, columns)
+        (gathered,),
+    )
+    return [r.reshape(rows, columns) for r, (rows, columns, _) in zip(results, plan)]
 
 
 def core_swap(v):
@@ -789,8 +802,8 @@
 
     def kept(self, which):
         if self.before is None:
-            dims = (1, *self.keep.shape[1:])
-            return [pl.BlockSpec(dims, lambda j, s: (which, 0, 0, 0))], [self.keep]
+            dims = (1, 1, *self.keep.shape[2:])
+            return [pl.BlockSpec(dims, lambda y, s: (which, y, 0, 0))], [self.keep]
         return self.before(2 + which)
 
 
@@ -798,8 +811,8 @@
     in_specs, args, counts = [], [], []
     for f in flows:
         specs, arrays = f.kept(1)
-        dims = (1, *f.got.shape[1:])
-        in_specs += specs + [pl.BlockSpec(dims, lambda j, s: (1, 0, 0, 0))]
+        dims = (1, 1, *f.got.shape[2:])
+        in_specs += specs + [pl.BlockSpec(dims, lambda y, s: (1, y, 0, 0))]
         args += arrays + [f.got]
         counts.append(len(arrays) + 1)
     out = tuple(shape(f.got.shape[1:], bf16) for f in flows)
@@ -811,7 +824,15 @@
             refs[len(args) + i][...] = total.astype(bf16)
             k += n
 
-    sums = call(kernel, out, (1,), in_specs, [whole(o) for o in out], cuts, args)
+    sums = call(
+        kernel,
+        out,
+        (2,),
+        in_specs,
+        [pl.BlockSpec((1, *o.shape[1:]), lambda y, s: (y, 0, 0)) for o in out],
+        cuts,
+        args,
+    )
     for f, v in zip(flows, sums):
         f.last = exchange(v, f.ring, (3, 1))
 
@@ -823,23 +844,14 @@
 def turn(flows, cuts):
     in_specs, outs, out_specs, args = [], [], [], []
 
-    def parts(f, index):
+    for f in flows:
         first = 1 if f.other == "x" else 5
         rows, columns = f.keep.shape[2] // 4, f.keep.shape[3]
-        arrays = [f.keep, f.got, f.last]
-
-        def spec(pick):
-            four = pl.BlockSpec((1, 2, rows, columns), lambda j, s: (0, 0, s[first + pick(j)], 0))
-            three = pl.BlockSpec((2, rows, columns), lambda j, s: (0, s[first + pick(j)], 0))
-            return [four, four, three]
-
-        return spec(index), arrays
-
-    for f in flows:
-        specs, arrays = parts(f, lambda j: j)
-        in_specs += specs
-        args += arrays
-        dims = (1, 2, f.keep.shape[2] // 4, f.keep.shape[3])
+        four = pl.BlockSpec((1, 2, rows, columns), lambda j, s, i=first: (0, 0, s[i + j], 0))
+        three = pl.BlockSpec((2, rows, columns), lambda j, s, i=first: (0, s[i + j], 0))
+        in_specs += [four, four, three]
+        args += [f.keep, f.got, f.last]
+        dims = (1, 2, rows, columns)
         outs.append(shape((2, *dims[1:]), bf16))
         out_specs.append(pl.BlockSpec(dims, lambda j, s: (j, 0, 0, 0)))
 
@@ -850,13 +862,22 @@
 
     sends = call(kernel, tuple(outs), (2,), in_specs, out_specs, cuts, args)
     for f, send in zip(flows, sends):
-        whole_parts = parts(f, lambda j: 2)[1]
-        f.before = lambda which, f=f, arrays=whole_parts, made=[
-            parts(f, lambda j: 2)[0],
-            parts(f, lambda j: 3)[0],
-        ]: (made[which - 2], arrays)
+        f.before = halves_of(f)
         f.ring = f.other
         f.got = exchange(send, f.ring, (1, 3))
+
+
+def halves_of(f):
+    arrays = [f.keep, f.got, f.last]
+    first = 1 if f.other == "x" else 5
+    rows, columns = f.keep.shape[2] // 4, f.keep.shape[3]
+
+    def quarter(which):
+        four = pl.BlockSpec((1, 1, rows, columns), lambda y, s: (0, y, s[first + which], 0))
+        three = pl.BlockSpec((1, rows, columns), lambda y, s: (y, s[first + which], 0))
+        return [four, four, three], arrays
+
+    return quarter
 
 
 def add(a, b, none):
@@ -870,39 +891,53 @@
 class Finish:
     def __init__(self, flows, extra, cuts):
         in_specs, args, sizes = [], [], []
+        def half(spec):
+            return pl.BlockSpec(
+                spec.block_shape, lambda j, s: spec.index_map(lax.rem(j + s[9], 2), s)
+            )
+
         for f in flows:
             specs, arrays = f.kept(0)
-            dims = (1, *f.got.shape[1:])
-            in_specs += specs + [pl.BlockSpec(dims, lambda j, s: (0, 0, 0, 0)), whole(f.last)]
+            dims = (1, 1, *f.got.shape[2:])
+            specs = specs + [
+                pl.BlockSpec(dims, lambda y, s: (0, y, 0, 0)),
+                pl.BlockSpec((1, *f.last.shape[1:]), lambda y, s: (y, 0, 0)),
+            ]
+            in_specs += [half(spec) for spec in specs]
             args += arrays + [f.got, f.last]
             sizes.append((len(arrays) + 2, f.got.shape[2], f.got.shape[3] // STEP))
-        in_specs += [whole(e) for e in extra]
+        for e in extra:
+            in_specs.append(half(pl.BlockSpec((1, *e.shape[1:]), lambda y, s: (y, 0, 0))))
         args += extra
         rows = sum(u * n for _, u, n in sizes) + sum(e.shape[1] for e in extra)
 
-        def kernel(s, *refs):
+        def kernel(_, *refs):
             send, mine = refs[-2:]
-            zero = s[9] == 0
+            j = pl.program_id(0)
+
+            def put(here, value):
+                @pl.when(j == 0)
+                def _():
+                    mine[here, :] = value
+
+                @pl.when(j == 1)
+                def _():
+                    send[here, :] = value.astype(bf16)
+
             start, k = 0, 0
             for count, u, n in sizes:
-                v = sum(value_of(r) for r in refs[k : k + count])
-                near = jnp.where(zero, v[0], v[1])
-                away = jnp.where(zero, v[1], v[0]).astype(bf16)
+                v = sum(value_of(r) for r in refs[k : k + count])[0]
                 for i in range(n):
-                    cut = slice(i * STEP, (i + 1) * STEP)
-                    mine[start : start + u, :] = near[:, cut]
-                    send[start : start + u, :] = away[:, cut]
+                    put(slice(start, start + u), v[:, i * STEP : (i + 1) * STEP])
                     start += u
                 k += count
             for ref in refs[k:-2]:
-                u = ref.shape[1]
-                mine[start : start + u, :] = jnp.where(zero, ref[0], ref[1])
-                send[start : start + u, :] = jnp.where(zero, ref[1], ref[0]).astype(bf16)
-                start += u
+                put(slice(start, start + ref.shape[1]), ref[0])
+                start += ref.shape[1]
 
         out = (shape((rows, STEP), bf16), shape((rows, STEP), f32))
         send, self.mine = call(
-            kernel, out, (1,), in_specs, [whole(o) for o in out], cuts, args
+            kernel, out, (2,), in_specs, [whole(o) for o in out], cuts, args
         )
         self.got = exchange(send, "y", (1, 3))
 
@@ -984,18 +1019,22 @@
 
     normed, normed_rel, oldest = first_norm(compressed, memory, tokens, vectors, thirds_d)
     both_normed, both_oldest, both_cot = both(normed), both(oldest), both(cotangent)
-    kv_got, small_got = gate((kv_got, small_got), normed)
-    kv_whole = joined(w_kv, kv_got, core_swap(kv_got))
-    key_value = dot(normed_rel, kv_whole).astype(bf16)
-    line.hold(key_value)
-    small_twin = core_swap(small_got)
+    half = D // 2
+    kv_own = dot(normed_rel[:, :half], w_kv)
+    q_own = dot(normed_rel[2 * T :, :half], w_q)
+    r_own = dot(sinus_rel[:, :half], w_r)
+    kv_got, small_got = gate((kv_got, small_got), normed, kv_own, q_own, r_own)
+    kv_twin, small_twin = core_swap(kv_got), core_swap(small_got)
+    kv_whole = joined(w_kv, kv_got, kv_twin)
     q_whole, r_whole, o_whole = [
         joined(w, small_got[i], small_twin[i]) for i, w in enumerate((w_q, w_r, w_o))
     ]
-    queries = dot(normed_rel[2 * T :], q_whole)
-    relative = dot(sinus_rel, r_whole).astype(bf16)
+    key_value = (kv_own + dot(normed_rel[:, half:], kv_whole[half:])).astype(bf16)
+    queries = q_own + dot(normed_rel[2 * T :, half:], q_whole[half:])
+    relative = (r_own + dot(sinus_rel[:, half:], r_whole[half:])).astype(bf16)
     line.hold(queries, relative)
     probs, attended = attend(queries, key_value, relative, vectors, none)
+    line.hold(both_normed[1], both_oldest[1], both_cot[1])
     residual, normed2, normed2_rel = out_and_norm(attended, o_whole, tokens, vectors, thirds_d)
     both_n2, both_att = both(normed2), both(attended)
 
@@ -1036,7 +1075,12 @@
     compact, comp_normed = compress(oldest, conv_pieces, vectors, thirds_c)
     comp_pair = dot(comp_normed, kv_whole).astype(bf16)
     compressed_next = jnp.concatenate([compressed[T // 3 :], compact], axis=0)
-    near = flows(
+    loss, d_ck, d_cv = reconstruct(queries, key_value, comp_pair, none)
+    recon_loss = jnp.sum(loss) / (T * D)
+    d_compact, d_conv_b = compress_back(d_ck, d_cv, kv_whole, compact, vectors, thirds_d)
+    both_compact = both(d_compact)
+    onward(large, cuts)
+    small = flows(
         [
             ("x", [(both_normed, 0, KEYS, both_kv, True)]),
             (
@@ -1046,30 +1090,22 @@
                     ((sinus_table,), 0, KEYS, both_rel, False),
                 ],
             ),
+            ("x", [(both_oldest, 0, T // 3, both_compact, False)]),
         ]
     )
-    loss, d_ck, d_cv = reconstruct(queries, key_value, comp_pair, none)
-    recon_loss = jnp.sum(loss) / (T * D)
-    onward(large, cuts)
-    d_compact, d_conv_b = compress_back(d_ck, d_cv, kv_whole, compact, vectors, thirds_d)
-    both_compact = both(d_compact)
-    onward(near, cuts)
-    conv = flows([("x", [(both_oldest, 0, T // 3, both_compact, False)])])
     turn(large, cuts)
     d_tokens, d_ln1_g, d_ln1_b = first_norm_back(
         d_kv, d_queries, kv_whole, q_whole, compressed, memory, tokens, vectors, d_residual,
         thirds_d,
     )
-    turn(near, cuts)
-    line.expect(1, *[f.got for f in near])
     onward(large, cuts)
-    onward(conv, cuts)
-    onward(near, cuts)
+    onward(small, cuts)
     early = Finish(large, [], cuts)
-    turn(conv, cuts)
+    turn(small, cuts)
     early.second(none)
-    onward(conv, cuts)
+    onward(small, cuts)
     early_sums = early.gather(none)
+
     total = jnp.concatenate(
         [d_ln1_g, d_ln1_b, d_bias_u, d_bias_v, d_ln2_g, d_ln2_b, d_b_out, d_conv_b]
         + [d_b_in]
@@ -1082,17 +1118,19 @@
         ],
         axis=1,
     )
-    late = Finish([*near, *conv], [total], cuts)
+    late = Finish(small, [total], cuts)
     late.second(none)
+    line.hold(early_sums)
     late_sums = late.gather(none)
 
-    g_in = widen(early_sums, 128, D // 2, FF, True, none)
-    g_out = widen(early_sums, 0, FF // 2, D, False, none)
-    g_o = widen(early_sums, 256, D // 2, D, True, none)
-    g_conv = widen(late_sums, 128, 3 * D // 2, D, False, none)
-    g_kv = widen(late_sums, 0, D // 2, 2 * D, False, none)
-    g_q = widen(late_sums, 64, D // 2, D, True, none)
-    g_r = widen(late_sums, 96, D // 2, D, True, none)
+    g_out, g_in, g_o = widen(
+        early_sums, [(FF // 2, D, "x"), (D // 2, FF, "z"), (D // 2, D, "z")], none
+    )
+    g_kv, g_q, g_r, g_conv = widen(
+        late_sums,
+        [(D // 2, 2 * D, "x"), (D // 2, D, "z"), (D // 2, D, "z"), (3 * D // 2, D, "x")],
+        none,
+    )
     half = jnp.sum(late_sums[:, 224:236].astype(f32), axis=0)
     t_ln1_g, t_ln1_b, t_bu, t_bv, t_ln2_g, t_ln2_b, t_bout, t_convb = [half[i] for i in range(8)]
     t_bin = half[8:].reshape(-1)

time: 418 us -> 426 us (1.019)
  Pallas kernels: 180 us -> 160 us
  waiting for transfers between devices: 124 us -> 137 us
  matrix products: 9.42 us -> 18.9 us
    pallas_call x38 -> x29, Pallas kernels: 180 us -> 160 us  [call(): pl.pallas_call(body, out_shape=out, grid_spec=pltpu.PrefetchScalarGridSpe...]
    dot_general x4 -> x7, matrix products: 9.42 us -> 18.9 us  [dot(): return jnp.dot(a, b, preferred_element_type=f32)]
    ppermute x26, waiting for transfers between devices: 46 us -> 52.4 us  [exchange(): return lax.ppermute(v, RING[ring], pairs)]
    all_gather x2, waiting for transfers between devices: 62.9 us -> 69.1 us  [gather(): lax.all_gather(add(self.mine, self.far, none), ('c', 'x', 'z'), axis=0)]
    unnamed x152 -> x150, local copies, waits for them, and re-layouts: 21.4 us -> 22.4 us
  transfers between devices with their start and end apart: 46 -> 46, of which waited for: 17 -> 18; matrix products, arithmetic and copies ran while one was open for 7% -> 10% of each run, Pallas kernels for 39% -> 30%
where the time goes in v4:
time: 426 us; the launch traced here: 419 us
  Pallas kernels  160 us (38%)
  waiting for transfers between devices  137 us (32%)
  starting transfers between devices  42.1 us (10%)
  local copies, waits for them, and re-layouts  28.6 us (7%)
  matrix products  18.9 us (4%)
  between operations  16.6 us (4%)
  other arithmetic  15.5 us (4%)
    pallas_call x29, Pallas kernels, call(): pl.pallas_call(body, out_shape=out, grid_spec=pltpu.PrefetchScalarGridSpe...  160 us
    all_gather x2, waiting for transfers between devices, gather(): lax.all_gather(add(self.mine, self.far, none), ('c', 'x', 'z'), axis=0)  69.1 us
    ppermute x26, waiting for transfers between devices, exchange(): return lax.ppermute(v, RING[ring], pairs)  52.4 us
    ppermute x26, starting transfers between devices, exchange(): return lax.ppermute(v, RING[ring], pairs)  35.4 us
    unnamed x150, local copies, waits for them, and re-layouts  22.4 us
    dot_general x7, matrix products, dot(): return jnp.dot(a, b, preferred_element_type=f32)  18.9 us
  transfers between devices with their start and end apart: 46, of which 18 were waited for; matrix products, arithmetic and copies ran while one was open for 10% of the time, Pallas kernels for 30%

profile of v4, /device:TPU:1, one launch (start us, length us, event | category | flops | bytes accessed | tf_op | source)
XLA Modules:
  0.0 419.0 jit_solution(17994862858726756777)
XLA Ops:
  12.7 4.3 %collective-permute-done.refs_1_ = bf16[144,1024]{1,0:T(8,128)(2,1)S(1)} collective-permute-done((bf16[144,1024]{1,0:T(8,128)(2,1)}, bf16[144,1024]{1,0:T(8,128)(2,1)S(1)}, u32[]{:S(2)}, u32[]{:S(2)}) %collective-permute-start) | collective-permute-done | bytes 294944 | tf_op jit(solution)/shard_map/ppermute | solution.py:783
  17.8 4.3 %shard_map.348 = (bf16[256,2048]{1,0:T(8,128)(2,1)}, bf16[3,256,1024]{2,1,0:T(8,128)(2,1)}, bf16[768,1024]{1,0:T(8,128)(2,1)}) custom-call(s32[1]{0:T(128)} %bitcast.8.s, bf16[512,2048]{1,0:T(8,128)(2,1)} %refs_0_.3, bf16[512,1024]{1,0:T(8,128)(2,1)} %refs_1_.4, bf16[512,1024]{1,0:T(8,128)(2,1)} %refs_2_.3, bf16[512,1024]{1,0:T(8,128)(2,1)} %refs_3_.4, ...), custom_call_target="tpu_custom_call" | custom-call | tf_op jit(solution)/shard_map/pallas_call | solution.py:68
  24.9 4.7 %fusion.4 = (bf16[576,512]{1,0:T(8,128)(2,1)S(1)}, bf16[576,512]{1,0:T(8,128)(2,1)S(1)}) fusion(f32[512]{0:T(512)S(1)} %negate_power_fusion, f32[576]{0:T(1024)S(1)} %subtract_convert_fusion), kind=kLoop, calls=%fused_computation.19 | loop fusion | flops 884736 | bytes 1184000 | tf_op jit(solution)/shard_map/convert.1
  35.6 4.7 %shard_map.350 = (bf16[576,1024]{1,0:T(8,128)(2,1)}, bf16[576,1024]{1,0:T(8,128)(2,1)}, bf16[64,3072]{1,0:T(8,128)(2,1)}) custom-call(s32[3]{0:T(128)} %pad_add_fusion.s, f32[192,1024]{1,0:T(8,128)} %bitcast.77, f32[192,1024]{1,0:T(8,128)} %bitcast.86, bf16[192,1024]{1,0:T(8,128)(2,1)} %bitcast.79, ...), custom_call_target="tpu_custom_call" | custom-call | tf_op jit(solution)/shard_map/pallas_call | solution.py:68
  46.2 8.0 %collective-permute-done.2.refs_1_ = bf16[3,256,1024]{2,1,0:T(8,128)(2,1)} collective-permute-done((bf16[3,256,1024]{2,1,0:T(8,128)(2,1)}, bf16[3,256,1024]{2,1,0:T(8,128)(2,1)}, u32[]{:S(2)}, u32[]{:S(2)}) %collective-permute-start.2) | collective-permute-done | bytes 1572896 | tf_op jit(solution)/shard_map/ppermute | solution.py:783
  58.5 5.0 %collective-permute-done.4 = bf16[256,2048]{1,0:T(8,128)(2,1)S(1)} collective-permute-done((bf16[256,2048]{1,0:T(8,128)(2,1)}, bf16[256,2048]{1,0:T(8,128)(2,1)S(1)}, u32[]{:S(2)}, u32[]{:S(2)}) %collective-permute-start.4) | collective-permute-done | bytes 1048608 | tf_op jit(solution)/shard_map/ppermute | solution.py:771
  64.6 5.3 %add_convert_fusion.refs_1_.refs_2_ = bf16[576,2048]{1,0:T(8,128)(2,1)} fusion(f32[576,2048]{1,0:T(8,128)} %fusion.16.refs_3_, bf16[256,2048]{1,0:T(8,128)(2,1)S(1)} %collective-permute-done.4, bf16[256,2048]{1,0:T(8,128)(2,1)S(1)} %copy-done.11, bf16[576,1024]{1,0:T(8,128)(2,1)S(1)} %copy-done.33), kind=kOutput, calls=%fused_computation | convolution fusion | flops 1214513152 | bytes 9764864 | tf_op jit(solution)/shard_map/dot_general | solution.py:30
  75.1 7.4 %shard_map.352 = (f32[8,192,640]{2,1,0:T(8,128)}, bf16[192,1024]{1,0:T(8,128)(2,1)}) custom-call(s32[1]{0:T(128)} %constant.10.clone.1.s, f32[192,1024]{1,0:T(8,128)} %convolution_add_fusion.refs_0_.refs_6_, bf16[576,2048]{1,0:T(8,128)(2,1)} %add_convert_fusion.refs_1_.refs_2_, bf16[576,2048]{1,0:T(8,128)(2,1)} %add_convert_fusion.refs_1_.refs_2_, ...), custom_call_target="tpu_custom_call" | custom-call | tf_op jit(solution)/shard_map/pallas_call | solution.py:68
  85.1 4.1 shard_map.353
  89.2 15.5 %shard_map.354 = (bf16[192,4096]{1,0:T(8,128)(2,1)}, bf16[192,4096]{1,0:T(8,128)(2,1)}, bf16[192,1024]{1,0:T(8,128)(2,1)}, f32[192,1024]{1,0:T(8,128)}, f32[4,1024]{1,0:T(4,128)}) custom-call(s32[1]{0:T(128)} %bitcast.s, bf16[192,1024]{1,0:T(8,128)(2,1)} %get-tuple-element.109.refs_0_, f32[192,1024]{1,0:T(8,128)} %get-tuple-element.110.refs_1_.refs_9_.refs_2_, ...), custom_call_target="tpu_custom_call" | custom-call | tf_op jit(solution)/shard_map/pallas_call | solution.py:68
  108.7 5.0 %shard_map.356 = (f32[192,1024]{1,0:T(8,128)}, bf16[192,1024]{1,0:T(8,128)(2,1)}, bf16[192,1024]{1,0:T(8,128)(2,1)}, f32[1,1024]{1,0:T(1,128)}, f32[1,1024]{1,0:T(1,128)}, /*index=5*/f32[1,1024]{1,0:T(1,128)}) custom-call(s32[3]{0:T(128)} %pad_add_fusion.s, bf16[192,1024]{1,0:T(8,128)(2,1)} %bitcast.84, f32[192,1024]{1,0:T(8,128)} %get-tuple-element.115.refs_1_, ...), custom_call_target="tpu_custom_call" | custom-call | tf_op jit(solution)/shard_map/pallas_call | solution.py:68
  116.9 11.6 %shard_map.357 = (bf16[2,2,512,512]{3,2,1,0:T(8,128)(2,1)}, bf16[2,2,512,512]{3,2,1,0:T(8,128)(2,1)}, bf16[2,2,128,2560]{3,2,1,0:T(8,128)(2,1)}, bf16[2,2,128,2560]{3,2,1,0:T(8,128)(2,1)}) custom-call(s32[10]{0:T(128)} %stack.86.s, bf16[192,4096]{1,0:T(8,128)(2,1)} %get-tuple-element.114.refs_1_.refs_5_.refs_0_, ...), custom_call_target="tpu_custom_call" | custom-call | tf_op jit(solution)/shard_map/pallas_call | solution.py:68
  128.5 4.5 %collective-permute-start.16 = (bf16[2,2,128,2560]{3,2,1,0:T(8,128)(2,1)}, bf16[2,2,128,2560]{3,2,1,0:T(8,128)(2,1)S(1)}, u32[]{:S(2)}, u32[]{:S(2)}) collective-permute-start(bf16[2,2,128,2560]{3,2,1,0:T(8,128)(2,1)} %get-tuple-element.129), channel_id=1, source_target_pairs={{0,4},{2,14},{4,0},{6,10},{8,12},{10,6},{12,8},{14,2},{1,5},{3,15}... | collective-permute-start | bytes 7864328 | tf_op jit(solution)/shard_map/ppermute | solution.py:783
  138.3 8.9 %shard_map.358 = (bf16[2,576,1024]{2,1,0:T(8,128)(2,1)}, bf16[576,1024]{1,0:T(8,128)(2,1)}, bf16[576,1024]{1,0:T(8,128)(2,1)}, bf16[576,1024]{1,0:T(8,128)(2,1)}...) custom-call(s32[1]{0:T(128)} %bitcast.8.s, f32[192,1024]{1,0:T(8,128)} %convolution_add_fusion.refs_0_.refs_6_, ...), custom_call_target="tpu_custom_call" | custom-call | tf_op jit(solution)/shard_map/pallas_call | solution.py:68
  149.3 6.8 %shard_map.359 = (f32[64,1024]{1,0:T(8,128)}, bf16[64,1024]{1,0:T(8,128)(2,1)}) custom-call(s32[6]{0:T(128)} %stack.77.s, bf16[64,3072]{1,0:T(8,128)(2,1)} %get-tuple-element.108.refs_0_.refs_16_.refs_17_, bf16[1536,1024]{1,0:T(8,128)(2,1)} %refs_1_.5, bf16[768,1024]{1,0:T(8,128)(2,1)} %shard_map.355.refs_2_, ...), custom_call_target="tpu_custom_call" | custom-call | tf_op jit(solution)/shard_map/pallas_call | solution.py:68
  158.6 4.6 %shard_map.360 = (f32[1,128]{1,0:T(1,128)}, bf16[64,1024]{1,0:T(8,128)(2,1)}, bf16[64,1024]{1,0:T(8,128)(2,1)}) custom-call(s32[1]{0:T(128)} %constant.10.clone.1.s, f32[192,1024]{1,0:T(8,128)} %convolution_add_fusion.refs_0_.refs_6_, bf16[576,2048]{1,0:T(8,128)(2,1)} %add_convert_fusion.refs_1_.refs_2_, bf16[576,2048]{1,0:T(8,128)(2,1)} %add_convert_fusion.refs_1_.refs_2_, ...), custom_call_target="tpu_custom_call" | custom-call | tf_op jit(solution)/shard_map/pallas_call | solution.py:68
  163.2 5.3 %shard_map.361 = (bf16[64,1024]{1,0:T(8,128)(2,1)}, f32[1,1024]{1,0:T(1,128)}) custom-call(s32[3]{0:T(128)} %pad_add_fusion.s, bf16[64,1024]{1,0:T(8,128)(2,1)} %get-tuple-element.130.refs_0_, bf16[64,1024]{1,0:T(8,128)(2,1)} %get-tuple-element.131.refs_1_, bf16[1024,2048]{1,0:T(8,128)(2,1)} %copy-done, f32[64,1024]{1,0:T(8,128)} %get-tuple-element.123.refs_5_.refs_3_, ...), custom_call_target="tpu_custom_call" | custom-call | tf_op jit(solution)/shard_map/pallas_call | solution.py:68
  170.0 4.3 %shard_map.362 = (bf16[2,512,512]{2,1,0:T(8,128)(2,1)}, bf16[2,128,2560]{2,1,0:T(8,128)(2,1)}) custom-call(s32[10]{0:T(128)} %stack.86.s, bf16[2,2,512,512]{3,2,1,0:T(8,128)(2,1)} %get-tuple-element.127.refs_0_, bf16[2,2,512,512]{3,2,1,0:T(8,128)(2,1)} %collective-permute-done.15.refs_1_, ...), custom_call_target="tpu_custom_call" | custom-call | tf_op jit(solution)/shard_map/pallas_call | solution.py:68
  178.6 12.0 %shard_map.363 = (bf16[2,2,128,1024]{3,2,1,0:T(8,128)(2,1)}, bf16[2,2,128,1024]{3,2,1,0:T(8,128)(2,1)}, bf16[2,2,128,1024]{3,2,1,0:T(8,128)(2,1)}, bf16[2,2,128,...) custom-call(s32[10]{0:T(128)} %stack.86.s, ...), custom_call_target="tpu_custom_call" | custom-call | tf_op jit(solution)/shard_map/pallas_call | solution.py:68
  198.0 3.7 shard_map.364
  206.0 9.5 %shard_map.365 = (f32[192,1024]{1,0:T(8,128)}, f32[1,1024]{1,0:T(1,128)}, f32[1,1024]{1,0:T(1,128)}) custom-call(s32[3]{0:T(128)} %pad_add_fusion.s, bf16[2,576,1024]{2,1,0:T(8,128)(2,1)} %get-tuple-element.122.refs_5_.refs_0_, bf16[192,1024]{1,0:T(8,128)(2,1)} %get-tuple-element.126.refs_10_.refs_1_, bf16[1024,2048]{1,0:T(8,128)(2,1)} %copy-done, ...), custom_call_target="tpu_custom_call" | custom-call | tf_op jit(solution)/shard_map/pallas_call | solution.py:68
  215.5 14.1 %collective-permute-done.27.refs_7_.refs_8_ = bf16[2,2,32,2560]{3,2,1,0:T(8,128)(2,1)S(1)} collective-permute-done((bf16[2,2,32,2560]{3,2,1,0:T(8,128)(2,1)}, bf16[2,2,32,2560]{3,2,1,0:T(8,128)(2,1)S(1)}, u32[]{:S(2)}, u32[]{:S(2)}) %collective-permute-start.27) | collective-permute-done | bytes 655392 | tf_op jit(solution)/shard_map/ppermute | solution.py:783
  235.5 3.9 shard_map.367
  242.9 9.9 %collective-permute-done.31.refs_4_ = bf16[2,128,512]{2,1,0:T(8,128)(2,1)S(1)} collective-permute-done((bf16[2,128,512]{2,1,0:T(8,128)(2,1)S(1)}, bf16[2,128,512]{2,1,0:T(8,128)(2,1)S(1)}, u32[]{:S(2)}, u32[]{:S(2)}) %collective-permute-start.31) | collective-permute-done | bytes 262176 | tf_op jit(solution)/shard_map/ppermute | solution.py:783
  255.0 3.8 shard_map.368
  273.7 4.7 %collective-permute-done.33.refs_3_ = bf16[2,2,32,1024]{3,2,1,0:T(8,128)(2,1)S(1)} collective-permute-done((bf16[2,2,32,1024]{3,2,1,0:T(8,128)(2,1)}, bf16[2,2,32,1024]{3,2,1,0:T(8,128)(2,1)S(1)}, u32[]{:S(2)}, u32[]{:S(2)}) %collective-permute-start.33) | collective-permute-done | bytes 262176 | tf_op jit(solution)/shard_map/ppermute | solution.py:783
  297.8 5.5 %collective-permute-done.41.refs_1_ = bf16[240,512]{1,0:T(8,128)(2,1)S(1)} collective-permute-done((bf16[240,512]{1,0:T(8,128)(2,1)}, bf16[240,512]{1,0:T(8,128)(2,1)S(1)}, u32[]{:S(2)}, u32[]{:S(2)}) %collective-permute-start.41) | collective-permute-done | bytes 245792 | tf_op jit(solution)/shard_map/ppermute | solution.py:783
  306.7 7.7 %collective-permute-done.42.refs_1_ = bf16[240,512]{1,0:T(8,128)(2,1)S(1)} collective-permute-done((bf16[240,512]{1,0:T(8,128)(2,1)}, bf16[240,512]{1,0:T(8,128)(2,1)S(1)}, u32[]{:S(2)}, u32[]{:S(2)}) %collective-permute-start.42) | collective-permute-done | bytes 245792 | tf_op jit(solution)/shard_map/ppermute | solution.py:946
  314.4 30.0 %all-gather.9.cloned.1.call-done = bf16[9216,512]{1,0:T(8,128)(2,1)} async-done(((bf16[288,512]{1,0:T(8,128)(2,1)}), bf16[9216,512]{1,0:T(8,128)(2,1)}) %all-gather.9.cloned.1.call-update) | async-done | bytes 9437200 | tf_op jit(solution)/shard_map/all_gather | solution.py:949
  348.6 11.0 %shard_map.376 = (f32[4,4,128,1024]{3,2,1,0:T(8,128)}, f32[4,4,32,4096]{3,2,1,0:T(8,128)}, f32[4,4,32,1024]{3,2,1,0:T(8,128)}) custom-call(s32[1]{0:T(128)} %constant.10.clone.1.s, bf16[32,288,512]{2,1,0:T(8,128)(2,1)} %bitcast.71, bf16[240,512]{1,0:T(8,128)(2,1)} %shard_map.375.refs_1_), custom_call_target="tpu_custom_call" | custom-call | tf_op jit(solution)/shard_map/pallas_call | solution.py:68
  359.6 39.1 %all-gather.11.cloned.1.call-done = bf16[7680,512]{1,0:T(8,128)(2,1)} async-done(((bf16[240,512]{1,0:T(8,128)(2,1)}), bf16[7680,512]{1,0:T(8,128)(2,1)}) %all-gather.11.cloned.1.call-update) | async-done | bytes 7864336 | tf_op jit(solution)/shard_map/all_gather | solution.py:949
  400.4 9.8 %shard_map.377 = (f32[4,4,32,2048]{3,2,1,0:T(8,128)}, f32[4,4,32,1024]{3,2,1,0:T(8,128)}, f32[4,4,32,1024]{3,2,1,0:T(8,128)}, f32[4,4,96,1024]{3,2,1,0:T(8,128)}) custom-call(s32[1]{0:T(128)} %constant.10.clone.1.s, bf16[32,240,512]{2,1,0:T(8,128)(2,1)} %bitcast.75, f32[4,4,128,1024]{3,2,1,0:T(8,128)} %get-tuple-element.171.refs_1_), custom_call_target="tpu_custom_call" | custom-call | tf_op jit(solution)/shard_map/pallas_call | solution.py:68
  (277 shorter events, 123.4 us)
Async XLA Ops:
  7.2 82.0 %all-gather.7.cloned.1.call-start = ((), (), s32[]{:S(2)}) async-start(), calls=%async_computation | async-start | bytes 8650752 | tf_op jit(solution)/shard_map/all_gather | solution.py:1006
  17.8 326.6 %all-gather.9.cloned.1.call-start = ((), (), s32[]{:S(2)}) async-start(), calls=%async_computation.1 | async-start | bytes 9732096 | tf_op jit(solution)/shard_map/all_gather | solution.py:949
  22.1 24.0 %collective-permute-start.1 = (bf16[256,2048]{1,0:T(8,128)(2,1)}, bf16[256,2048]{1,0:T(8,128)(2,1)S(1)}, u32[]{:S(2)}, u32[]{:S(2)}) collective-permute-start(bf16[256,2048]{1,0:T(8,128)(2,1)} %get-tuple-element.99.refs_2_), channel_id=1, source_target_pairs={{0,1},{2,67},{1,0},{3,66},{64,65},{66,3},{65,64},{67,2},{4,5},{6,7... | collective-permute-start | bytes 3145736 | tf_op jit(solution)/shard_map/ppermute | solution.py:783
  24.8 29.4 %collective-permute-start.2 = (bf16[3,256,1024]{2,1,0:T(8,128)(2,1)}, bf16[3,256,1024]{2,1,0:T(8,128)(2,1)}, u32[]{:S(2)}, u32[]{:S(2)}) collective-permute-start(bf16[3,256,1024]{2,1,0:T(8,128)(2,1)} %get-tuple-element.102), channel_id=1, source_target_pairs={{0,1},{2,67},{1,0},{3,66},{64,65},{66,3},{65,64},{67,2},{4,5},{6,7... | collective-permute-start | bytes 4718600 | tf_op jit(solution)/shard_map/ppermute | solution.py:783
  54.2 15.7 %collective-permute-start.3 = (bf16[3,256,1024]{2,1,0:T(8,128)(2,1)}, bf16[3,256,1024]{2,1,0:T(8,128)(2,1)S(1)}, u32[]{:S(2)}, u32[]{:S(2)}) collective-permute-start(bf16[3,256,1024]{2,1,0:T(8,128)(2,1)} %get-tuple-element.104), channel_id=1, source_target_pairs={{0,2},{2,0},{1,3},{3,1},{4,6},{6,4},{5,7},{7,5},{8,10},{10,8},{9,1... | collective-permute-start | bytes 4718600 | tf_op jit(solution)/shard_map/ppermute | solution.py:771
  54.8 29.2 %collective-permute-start.7 = (bf16[192,1024]{1,0:T(8,128)(2,1)}, bf16[192,1024]{1,0:T(8,128)(2,1)}, u32[]{:S(2)}, u32[]{:S(2)}) collective-permute-start(bf16[192,1024]{1,0:T(8,128)(2,1)} %bitcast.82), channel_id=1, source_target_pairs={{0,2},{2,0},{1,3},{3,1},{4,6},{6,4},{5,7},{7,5},{8,10},{10,8},{9,1... | collective-permute-start | bytes 1179656 | tf_op jit(solution)/shard_map/ppermute | solution.py:771
  55.5 28.6 %collective-permute-start.5 = (bf16[576,1024]{1,0:T(8,128)(2,1)S(1)}, bf16[576,1024]{1,0:T(8,128)(2,1)S(1)}, u32[]{:S(2)}, u32[]{:S(2)}) collective-permute-start(bf16[576,1024]{1,0:T(8,128)(2,1)S(1)} %copy-done.1), channel_id=1, source_target_pairs={{0,2},{2,0},{1,3},{3,1},{4,6},{6,4},{5,7},{7,5},{8,10},{10,8},{9,1... | collective-permute-start | bytes 3538952 | tf_op jit(solution)/shard_map/ppermute | solution.py:771
  55.9 28.2 %collective-permute-start.6 = (bf16[64,3072]{1,0:T(8,128)(2,1)S(1)}, bf16[64,3072]{1,0:T(8,128)(2,1)}, u32[]{:S(2)}, u32[]{:S(2)}) collective-permute-start(bf16[64,3072]{1,0:T(8,128)(2,1)S(1)} %copy-done.30), channel_id=1, source_target_pairs={{0,2},{2,0},{1,3},{3,1},{4,6},{6,4},{5,7},{7,5},{8,10},{10,8},{9,1... | collective-permute-start | bytes 1179656 | tf_op jit(solution)/shard_map/ppermute | solution.py:771
  104.7 10.9 %collective-permute-start.10 = (bf16[192,4096]{1,0:T(8,128)(2,1)}, bf16[192,4096]{1,0:T(8,128)(2,1)S(1)}, u32[]{:S(2)}, u32[]{:S(2)}) collective-permute-start(bf16[192,4096]{1,0:T(8,128)(2,1)} %get-tuple-element.114.refs_1_.refs_5_.refs_0_), channel_id=1, source_target_pairs={{0,2},{2,0},{1,3},{3,1},{4,6},{6,4},{5,7},{7,5},{8,10},{10,8},{9,1... | collective-permute-start | bytes 4718600 | tf_op jit(solution)/shard_map/ppermute | solution.py:771
  105.0 10.6 %collective-permute-start.12 = (bf16[192,4096]{1,0:T(8,128)(2,1)}, bf16[192,4096]{1,0:T(8,128)(2,1)}, u32[]{:S(2)}, u32[]{:S(2)}) collective-permute-start(bf16[192,4096]{1,0:T(8,128)(2,1)} %get-tuple-element.118.refs_10_), channel_id=1, source_target_pairs={{0,2},{2,0},{1,3},{3,1},{4,6},{6,4},{5,7},{7,5},{8,10},{10,8},{9,1... | collective-permute-start | bytes 4718600 | tf_op jit(solution)/shard_map/ppermute | solution.py:771
  105.3 30.4 %collective-permute-start.8 = (bf16[768,1024]{1,0:T(8,128)(2,1)}, bf16[768,1024]{1,0:T(8,128)(2,1)}, u32[]{:S(2)}, u32[]{:S(2)}) collective-permute-start(bf16[768,1024]{1,0:T(8,128)(2,1)} %get-tuple-element.113), channel_id=1, source_target_pairs={{0,1},{2,67},{1,0},{3,66},{64,65},{66,3},{65,64},{67,2},{4,5},{6,7... | collective-permute-start | bytes 4718600 | tf_op jit(solution)/shard_map/ppermute | solution.py:783
  128.5 39.9 %collective-permute-start.16 = (bf16[2,2,128,2560]{3,2,1,0:T(8,128)(2,1)}, bf16[2,2,128,2560]{3,2,1,0:T(8,128)(2,1)S(1)}, u32[]{:S(2)}, u32[]{:S(2)}) collective-permute-start(bf16[2,2,128,2560]{3,2,1,0:T(8,128)(2,1)} %get-tuple-element.129), channel_id=1, source_target_pairs={{0,4},{2,14},{4,0},{6,10},{8,12},{10,6},{12,8},{14,2},{1,5},{3,15}... | collective-permute-start | bytes 7864328 | tf_op jit(solution)/shard_map/ppermute | solution.py:783
  133.0 35.4 %collective-permute-start.15 = (bf16[2,2,512,512]{3,2,1,0:T(8,128)(2,1)}, bf16[2,2,512,512]{3,2,1,0:T(8,128)(2,1)}, u32[]{:S(2)}, u32[]{:S(2)}) collective-permute-start(bf16[2,2,512,512]{3,2,1,0:T(8,128)(2,1)} %get-tuple-element.121.refs_7_), channel_id=1, source_target_pairs={{0,16},{2,50},{16,0},{18,34},{32,48},{34,18},{48,32},{50,2},{1,17}... | collective-permute-start | bytes 6291464 | tf_op jit(solution)/shard_map/ppermute | solution.py:783
  135.7 13.6 %collective-permute-start.9 = (bf16[768,1024]{1,0:T(8,128)(2,1)}, bf16[768,1024]{1,0:T(8,128)(2,1)}, u32[]{:S(2)}, u32[]{:S(2)}) collective-permute-start(bf16[768,1024]{1,0:T(8,128)(2,1)} %shard_map.355.refs_2_), channel_id=1, source_target_pairs={{0,2},{2,0},{1,3},{3,1},{4,6},{6,4},{5,7},{7,5},{8,10},{10,8},{9,1... | collective-permute-start | bytes 4718600 | tf_op jit(solution)/shard_map/ppermute | solution.py:771
  147.2 30.6 %collective-permute-start.19 = (bf16[576,1024]{1,0:T(8,128)(2,1)}, bf16[576,1024]{1,0:T(8,128)(2,1)}, u32[]{:S(2)}, u32[]{:S(2)}) collective-permute-start(bf16[576,1024]{1,0:T(8,128)(2,1)} %get-tuple-element.136), channel_id=1, source_target_pairs={{0,2},{2,0},{1,3},{3,1},{4,6},{6,4},{5,7},{7,5},{8,10},{10,8},{9,1... | collective-permute-start | bytes 3538952 | tf_op jit(solution)/shard_map/ppermute | solution.py:771
  147.8 30.1 %collective-permute-start.21 = (bf16[576,1024]{1,0:T(8,128)(2,1)}, bf16[576,1024]{1,0:T(8,128)(2,1)}, u32[]{:S(2)}, u32[]{:S(2)}) collective-permute-start(bf16[576,1024]{1,0:T(8,128)(2,1)} %get-tuple-element.137.refs_14_), channel_id=1, source_target_pairs={{0,2},{2,0},{1,3},{3,1},{4,6},{6,4},{5,7},{7,5},{8,10},{10,8},{9,1... | collective-permute-start | bytes 3538952 | tf_op jit(solution)/shard_map/ppermute | solution.py:771
  174.3 21.7 %collective-permute-start.18 = (bf16[2,128,2560]{2,1,0:T(8,128)(2,1)}, bf16[2,128,2560]{2,1,0:T(8,128)(2,1)S(1)}, u32[]{:S(2)}, u32[]{:S(2)}) collective-permute-start(bf16[2,128,2560]{2,1,0:T(8,128)(2,1)} %get-tuple-element.134), channel_id=1, source_target_pairs={{0,12},{2,6},{4,8},{6,2},{8,4},{10,14},{12,0},{14,10},{1,13},{3,7}... | collective-permute-start | bytes 3932168 | tf_op jit(solution)/shard_map/ppermute | solution.py:783
  176.6 19.3 %collective-permute-start.17 = (bf16[2,512,512]{2,1,0:T(8,128)(2,1)}, bf16[2,512,512]{2,1,0:T(8,128)(2,1)S(1)}, u32[]{:S(2)}, u32[]{:S(2)}) collective-permute-start(bf16[2,512,512]{2,1,0:T(8,128)(2,1)} %get-tuple-element.133.refs_22_), channel_id=1, source_target_pairs={{0,48},{2,18},{16,32},{18,2},{32,16},{34,50},{48,0},{50,34},{1,49}... | collective-permute-start | bytes 3145736 | tf_op jit(solution)/shard_map/ppermute | solution.py:783
  190.6 43.1 %collective-permute-start.25 = (bf16[2,2,384,512]{3,2,1,0:T(8,128)(2,1)}, bf16[2,2,384,512]{3,2,1,0:T(8,128)(2,1)S(1)}, u32[]{:S(2)}, u32[]{:S(2)}) collective-permute-start(bf16[2,2,384,512]{3,2,1,0:T(8,128)(2,1)} %get-tuple-element.145), channel_id=1, source_target_pairs={{0,16},{2,50},{16,0},{18,34},{32,48},{34,18},{48,32},{50,2},{1,17}... | collective-permute-start | bytes 4718600 | tf_op jit(solution)/shard_map/ppermute | solution.py:783
  192.2 41.5 %collective-permute-start.23 = (bf16[2,2,128,1024]{3,2,1,0:T(8,128)(2,1)}, bf16[2,2,128,1024]{3,2,1,0:T(8,128)(2,1)S(1)}, u32[]{:S(2)}, u32[]{:S(2)}) collective-permute-start(bf16[2,2,128,1024]{3,2,1,0:T(8,128)(2,1)} %get-tuple-element.138.refs_6_), channel_id=1, source_target_pairs={{0,16},{2,50},{16,0},{18,34},{32,48},{34,18},{48,32},{50,2},{1,17}... | collective-permute-start | bytes 3145736 | tf_op jit(solution)/shard_map/ppermute | solution.py:783
  193.3 40.4 %collective-permute-start.24 = (bf16[2,2,128,1024]{3,2,1,0:T(8,128)(2,1)}, bf16[2,2,128,1024]{3,2,1,0:T(8,128)(2,1)S(1)}, u32[]{:S(2)}, u32[]{:S(2)}) collective-permute-start(bf16[2,2,128,1024]{3,2,1,0:T(8,128)(2,1)} %get-tuple-element.143), channel_id=1, source_target_pairs={{0,4},{2,14},{4,0},{6,10},{8,12},{10,6},{12,8},{14,2},{1,5},{3,15}... | collective-permute-start | bytes 3145736 | tf_op jit(solution)/shard_map/ppermute | solution.py:783
  201.6 28.0 %collective-permute-start.27 = (bf16[2,2,32,2560]{3,2,1,0:T(8,128)(2,1)}, bf16[2,2,32,2560]{3,2,1,0:T(8,128)(2,1)S(1)}, u32[]{:S(2)}, u32[]{:S(2)}) collective-permute-start(bf16[2,2,32,2560]{3,2,1,0:T(8,128)(2,1)} %get-tuple-element.146), channel_id=1, source_target_pairs={{0,16},{2,50},{16,0},{18,34},{32,48},{34,18},{48,32},{50,2},{1,17}... | collective-permute-start | bytes 1966088 | tf_op jit(solution)/shard_map/ppermute | solution.py:783
  202.3 13.2 %collective-permute-start.26 = (bf16[2,2,128,512]{3,2,1,0:T(8,128)(2,1)}, bf16[2,2,128,512]{3,2,1,0:T(8,128)(2,1)S(1)}, u32[]{:S(2)}, u32[]{:S(2)}) collective-permute-start(bf16[2,2,128,512]{3,2,1,0:T(8,128)(2,1)} %get-tuple-element.139.refs_9_), channel_id=1, source_target_pairs={{0,4},{2,14},{4,0},{6,10},{8,12},{10,6},{12,8},{14,2},{1,5},{3,15}... | collective-permute-start | bytes 1572872 | tf_op jit(solution)/shard_map/ppermute | solution.py:783
  239.4 20.5 %collective-permute-start.30 = (bf16[2,384,512]{2,1,0:T(8,128)(2,1)}, bf16[2,384,512]{2,1,0:T(8,128)(2,1)S(1)}, u32[]{:S(2)}, u32[]{:S(2)}) collective-permute-start(bf16[2,384,512]{2,1,0:T(8,128)(2,1)} %get-tuple-element.150), channel_id=1, source_target_pairs={{0,48},{2,18},{16,32},{18,2},{32,16},{34,50},{48,0},{50,34},{1,49}... | collective-permute-start | bytes 2359304 | tf_op jit(solution)/shard_map/ppermute | solution.py:783
  239.9 14.3 %collective-permute-start.32 = (bf16[2,32,2560]{2,1,0:T(8,128)(2,1)S(1)}, bf16[2,32,2560]{2,1,0:T(8,128)(2,1)S(1)}, u32[]{:S(2)}, u32[]{:S(2)}) collective-permute-start(bf16[2,32,2560]{2,1,0:T(8,128)(2,1)S(1)} %copy-done.72), channel_id=1, source_target_pairs={{0,48},{2,18},{16,32},{18,2},{32,16},{34,50},{48,0},{50,34},{1,49}... | collective-permute-start | bytes 983048 | tf_op jit(solution)/shard_map/ppermute | solution.py:783
  240.9 19.0 %collective-permute-start.28 = (bf16[2,128,1024]{2,1,0:T(8,128)(2,1)}, bf16[2,128,1024]{2,1,0:T(8,128)(2,1)S(1)}, u32[]{:S(2)}, u32[]{:S(2)}) collective-permute-start(bf16[2,128,1024]{2,1,0:T(8,128)(2,1)} %get-tuple-element.148.refs_10_), channel_id=1, source_target_pairs={{0,48},{2,18},{16,32},{18,2},{32,16},{34,50},{48,0},{50,34},{1,49}... | collective-permute-start | bytes 1572872 | tf_op jit(solution)/shard_map/ppermute | solution.py:783
  241.4 18.5 %collective-permute-start.29 = (bf16[2,128,1024]{2,1,0:T(8,128)(2,1)}, bf16[2,128,1024]{2,1,0:T(8,128)(2,1)S(1)}, u32[]{:S(2)}, u32[]{:S(2)}) collective-permute-start(bf16[2,128,1024]{2,1,0:T(8,128)(2,1)} %get-tuple-element.149), channel_id=1, source_target_pairs={{0,12},{2,6},{4,8},{6,2},{8,4},{10,14},{12,0},{14,10},{1,13},{3,7}... | collective-permute-start | bytes 1572872 | tf_op jit(solution)/shard_map/ppermute | solution.py:783
  242.5 10.3 %collective-permute-start.31 = (bf16[2,128,512]{2,1,0:T(8,128)(2,1)S(1)}, bf16[2,128,512]{2,1,0:T(8,128)(2,1)S(1)}, u32[]{:S(2)}, u32[]{:S(2)}) collective-permute-start(bf16[2,128,512]{2,1,0:T(8,128)(2,1)S(1)} %copy-done.54), channel_id=1, source_target_pairs={{0,12},{2,6},{4,8},{6,2},{8,4},{10,14},{12,0},{14,10},{1,13},{3,7}... | collective-permute-start | bytes 786440 | tf_op jit(solution)/shard_map/ppermute | solution.py:783
  258.8 9.0 %collective-permute-start.36 = (bf16[288,512]{1,0:T(8,128)(2,1)}, bf16[288,512]{1,0:T(8,128)(2,1)S(1)}, u32[]{:S(2)}, u32[]{:S(2)}) collective-permute-start(bf16[288,512]{1,0:T(8,128)(2,1)} %get-tuple-element.152.refs_9_), channel_id=1, source_target_pairs={{0,1},{2,67},{1,0},{3,66},{64,65},{66,3},{65,64},{67,2},{4,5},{6,7... | collective-permute-start | bytes 884744 | tf_op jit(solution)/shard_map/ppermute | solution.py:783
  265.2 13.4 %collective-permute-start.35 = (bf16[2,2,96,512]{3,2,1,0:T(8,128)(2,1)}, bf16[2,2,96,512]{3,2,1,0:T(8,128)(2,1)S(1)}, u32[]{:S(2)}, u32[]{:S(2)}) collective-permute-start(bf16[2,2,96,512]{3,2,1,0:T(8,128)(2,1)} %get-tuple-element.155), channel_id=1, source_target_pairs={{0,4},{2,14},{4,0},{6,10},{8,12},{10,6},{12,8},{14,2},{1,5},{3,15}... | collective-permute-start | bytes 1179656 | tf_op jit(solution)/shard_map/ppermute | solution.py:783
  270.5 12.6 %collective-permute-start.40 = (bf16[288,512]{1,0:T(8,128)(2,1)}, bf16[288,512]{1,0:T(8,128)(2,1)S(1)}, u32[]{:S(2)}, u32[]{:S(2)}) collective-permute-start(bf16[288,512]{1,0:T(8,128)(2,1)} %shard_map.370.refs_12_.refs_0_), channel_id=1, source_target_pairs={{0,64},{64,0},{1,65},{65,1},{2,66},{66,2},{3,67},{67,3},{4,68},{68... | collective-permute-start | bytes 884744 | tf_op jit(solution)/shard_map/ppermute | solution.py:946
  285.7 113.0 %all-gather.11.cloned.1.call-start = ((), (), s32[]{:S(2)}) async-start(), calls=%async_computation.2 | async-start | bytes 8110080 | tf_op jit(solution)/shard_map/all_gather | solution.py:949
  (87 other events, 487.0 us)
Sparse Core Ops, SparseCore 0:
  17.9 55.6 all-gather.6
  285.8 58.5 all-gather.8
  347.3 51.3 all-gather.10

commit v5 on v4

--- a/solution.py
+++ b/solution.py
@@ -226,7 +226,7 @@
 
 
 def first_norm(compressed, memory, tokens, vectors, offsets):
-    def kernel(s, comp, mem, tok, vec, out, out_rel, old):
+    def kernel(s, comp, mem, tok, vec, out, out_rel, old, old_quarters):
         gain, bias = row(vec, LN1_G), row(vec, LN1_B)
 
         def part(ref, base):
@@ -244,9 +244,19 @@
         for tap in range(3):
             take = jnp.where(col == 3 * line_of + tap, 1.0, 0.0).astype(bf16)
             old[:, tap * D : (tap + 1) * D] = dot(take, low).astype(bf16)
+        width = 3 * D // 8
+        for q in range(4):
+            for y in range(2):
+                begin = y * 3 * D // 2 + q * width
+                old_quarters[q, :, y * width : (y + 1) * width] = old[:, begin : begin + width]
 
     args = (compressed, memory, tokens, vectors)
-    out = (shape((KEYS, D), bf16), shape((KEYS, D), bf16), shape((T // 3, 3 * D), bf16))
+    out = (
+        shape((KEYS, D), bf16),
+        shape((KEYS, D), bf16),
+        shape((T // 3, 3 * D), bf16),
+        shape((4, T // 3, 3 * D // 4), bf16),
+    )
     return call(
         kernel, out, (1,), [whole(a) for a in args], [whole(o) for o in out], offsets, args
     )
@@ -727,6 +737,27 @@
     return [(flat[2 * i], flat[2 * i + 1]) for i in range(len(groups))]
 
 
+def conv_grad(x, x_twin, dy, dy_twin, scalars):
+    rows, columns = x.shape[1] // 2, D // 2
+
+    def kernel(s, xa, xb, da, db, out):
+        both = jnp.concatenate([xa[...], xb[...]], axis=0)
+        total = t_dot(both, jnp.concatenate([da[...], db[...]], axis=0))
+        out[...] = total.reshape(2, rows, columns)
+
+    half = pl.BlockSpec((dy.shape[0], columns), lambda j, s: (0, s[0]))
+    out = shape((2, rows, columns), f32)
+    return call(
+        kernel,
+        out,
+        (1,),
+        [whole(x), whole(x_twin), half, half],
+        whole(out),
+        scalars,
+        (x, x_twin, dy, dy_twin),
+    )
+
+
 def widen(gathered, plan, none):
     outs, specs, layout = [], [], []
     start = 0
@@ -794,11 +825,15 @@
 
 
 class Flow:
-    def __init__(self, ring, pair):
+    def __init__(self, ring, pair, done=None):
         self.ring, self.other = ring, "z" if ring == "x" else "x"
-        send, self.keep = pair
-        self.got = exchange(send, ring, (1, 3))
-        self.before = None
+        self.before, self.result = None, done
+        if done is None:
+            send, self.keep = pair
+            self.got = exchange(send, ring, (1, 3))
+
+    def sources(self):
+        return [self.keep, self.got, self.last] if self.result is None else [self.result]
 
     def kept(self, which):
         if self.before is None:
@@ -844,21 +879,26 @@
 def turn(flows, cuts):
     in_specs, outs, out_specs, args = [], [], [], []
 
+    counts = []
     for f in flows:
         first = 1 if f.other == "x" else 5
-        rows, columns = f.keep.shape[2] // 4, f.keep.shape[3]
+        arrays = f.sources()
+        rows, columns = arrays[0].shape[-2] // 4, arrays[0].shape[-1]
         four = pl.BlockSpec((1, 2, rows, columns), lambda j, s, i=first: (0, 0, s[i + j], 0))
         three = pl.BlockSpec((2, rows, columns), lambda j, s, i=first: (0, s[i + j], 0))
-        in_specs += [four, four, three]
-        args += [f.keep, f.got, f.last]
+        in_specs += [four if a.ndim == 4 else three for a in arrays]
+        args += arrays
+        counts.append(len(arrays))
         dims = (1, 2, rows, columns)
         outs.append(shape((2, *dims[1:]), bf16))
         out_specs.append(pl.BlockSpec(dims, lambda j, s: (j, 0, 0, 0)))
 
     def kernel(_, *refs):
-        for i in range(len(flows)):
-            total = sum(value_of(r) for r in refs[3 * i : 3 * i + 3])
+        k = 0
+        for i, n in enumerate(counts):
+            total = sum(value_of(r) for r in refs[k : k + n])
             refs[len(args) + i][0] = total.astype(bf16)
+            k += n
 
     sends = call(kernel, tuple(outs), (2,), in_specs, out_specs, cuts, args)
     for f, send in zip(flows, sends):
@@ -868,14 +908,14 @@
 
 
 def halves_of(f):
-    arrays = [f.keep, f.got, f.last]
+    arrays = f.sources()
     first = 1 if f.other == "x" else 5
-    rows, columns = f.keep.shape[2] // 4, f.keep.shape[3]
+    rows, columns = arrays[0].shape[-2] // 4, arrays[0].shape[-1]
 
     def quarter(which):
         four = pl.BlockSpec((1, 1, rows, columns), lambda y, s: (0, y, s[first + which], 0))
         three = pl.BlockSpec((1, rows, columns), lambda y, s: (y, s[first + which], 0))
-        return [four, four, three], arrays
+        return [four if a.ndim == 4 else three for a in arrays], arrays
 
     return quarter
 
@@ -1017,24 +1057,29 @@
     line.hold(sinus_rel)
     vectors, b_in = unpack(piece, piece_got, ints(yl))
 
-    normed, normed_rel, oldest = first_norm(compressed, memory, tokens, vectors, thirds_d)
-    both_normed, both_oldest, both_cot = both(normed), both(oldest), both(cotangent)
-    half = D // 2
-    kv_own = dot(normed_rel[:, :half], w_kv)
-    q_own = dot(normed_rel[2 * T :, :half], w_q)
-    r_own = dot(sinus_rel[:, :half], w_r)
-    kv_got, small_got = gate((kv_got, small_got), normed, kv_own, q_own, r_own)
+    normed, normed_rel, oldest, old_quarters = first_norm(compressed, memory, tokens, vectors, thirds_d)
+    both_normed, both_cot = both(normed), both(cotangent)
+    own, first, far, second = quarters(place["x"], core)
+    got = exchange(
+        jnp.stack([pick(old_quarters, first, 0), pick(old_quarters, far, 0)]), "x", (1, 3)
+    )
+    got_far = exchange(jnp.stack([pick(old_quarters, second, 0), got[1]]), "x", (3, 1))
+    old_ring = jnp.concatenate([pick(old_quarters, own, 0), got[0], got_far[0], got_far[1]])
+    old_twin = core_swap(old_ring)
+    kv_got, small_got = gate((kv_got, small_got), normed)
     kv_twin, small_twin = core_swap(kv_got), core_swap(small_got)
     kv_whole = joined(w_kv, kv_got, kv_twin)
     q_whole, r_whole, o_whole = [
         joined(w, small_got[i], small_twin[i]) for i, w in enumerate((w_q, w_r, w_o))
     ]
-    key_value = (kv_own + dot(normed_rel[:, half:], kv_whole[half:])).astype(bf16)
-    queries = q_own + dot(normed_rel[2 * T :, half:], q_whole[half:])
-    relative = (r_own + dot(sinus_rel[:, half:], r_whole[half:])).astype(bf16)
+    key_value = dot(normed_rel, kv_whole).astype(bf16)
+    line.hold(key_value)
+    queries = dot(normed_rel[2 * T :], q_whole)
+    relative = dot(sinus_rel, r_whole).astype(bf16)
     line.hold(queries, relative)
+    line.hold(got)
     probs, attended = attend(queries, key_value, relative, vectors, none)
-    line.hold(both_normed[1], both_oldest[1], both_cot[1])
+    line.hold(both_normed[1], both_cot[1], got_far)
     residual, normed2, normed2_rel = out_and_norm(attended, o_whole, tokens, vectors, thirds_d)
     both_n2, both_att = both(normed2), both(attended)
 
@@ -1050,6 +1095,7 @@
         pairs = weight_grads(groups, cuts)
         return [Flow(ring, pair) for (ring, _), pair in zip(groups, pairs)]
 
+    line.hold(old_twin)
     hidden, d_pre, mixed_out, d_normed2, d_b_in = feed_forward(
         normed2_rel, residual, cotangent, w_in, w_out, spread, b_in, vectors, ints(yl)
     )
@@ -1077,10 +1123,13 @@
     compressed_next = jnp.concatenate([compressed[T // 3 :], compact], axis=0)
     loss, d_ck, d_cv = reconstruct(queries, key_value, comp_pair, none)
     recon_loss = jnp.sum(loss) / (T * D)
+    line.hold(both_kv[1], both_q[1], both_rel[1])
     d_compact, d_conv_b = compress_back(d_ck, d_cv, kv_whole, compact, vectors, thirds_d)
-    both_compact = both(d_compact)
+    ring_got = exchange(d_compact, "x", (1, 3))
+    line.hold(ring_got)
     onward(large, cuts)
-    small = flows(
+    ring_pair = jnp.concatenate([d_compact, ring_got])
+    near = flows(
         [
             ("x", [(both_normed, 0, KEYS, both_kv, True)]),
             (
@@ -1090,21 +1139,28 @@
                     ((sinus_table,), 0, KEYS, both_rel, False),
                 ],
             ),
-            ("x", [(both_oldest, 0, T // 3, both_compact, False)]),
         ]
     )
+    pair_got = exchange(ring_pair, "x", (3, 1))
+    line.hold(pair_got)
     turn(large, cuts)
+    compact_ring = jnp.concatenate([ring_pair, pair_got])
     d_tokens, d_ln1_g, d_ln1_b = first_norm_back(
         d_kv, d_queries, kv_whole, q_whole, compressed, memory, tokens, vectors, d_residual,
         thirds_d,
     )
+    line.hold(compact_ring)
     onward(large, cuts)
-    onward(small, cuts)
+    conv = Flow(
+        "x", None, conv_grad(old_ring, old_twin, compact_ring, core_swap(compact_ring), cuts)
+    )
     early = Finish(large, [], cuts)
-    turn(small, cuts)
+    onward(near, cuts)
     early.second(none)
-    onward(small, cuts)
+    late_flows = [*near, conv]
+    turn(late_flows, cuts)
     early_sums = early.gather(none)
+    onward(late_flows, cuts)
 
     total = jnp.concatenate(
         [d_ln1_g, d_ln1_b, d_bias_u, d_bias_v, d_ln2_g, d_ln2_b, d_b_out, d_conv_b]
@@ -1118,7 +1174,7 @@
         ],
         axis=1,
     )
-    late = Finish(small, [total], cuts)
+    late = Finish(late_flows, [total], cuts)
     late.second(none)
     line.hold(early_sums)
     late_sums = late.gather(none)

time: 426 us -> 400 us (0.939)
  waiting for transfers between devices: 137 us -> 111 us
  matrix products: 18.9 us -> 10.2 us
  starting transfers between devices: 42.1 us -> 46.7 us
    all_gather x2, waiting for transfers between devices: 69.1 us -> 57.2 us  [gather(): lax.all_gather(add(self.mine, self.far, none), ('c', 'x', 'z'), axis=0)]
    dot_general x7 -> x4, matrix products: 18.9 us -> 10.2 us  [dot(): return jnp.dot(a, b, preferred_element_type=f32)]
    ppermute x15, waiting for transfers between devices: 7.74 us -> 1.22 us  [core_swap(): return lax.ppermute(v, 'c', [(0, 1), (1, 0)])]
    ppermute x26 -> x28, waiting for transfers between devices: 52.4 us -> 46.8 us  [exchange(): return lax.ppermute(v, RING[ring], pairs)]
    ppermute x26 -> x28, starting transfers between devices: 35.4 us -> 36.3 us  [exchange(): return lax.ppermute(v, RING[ring], pairs)]
    pallas_call x29 -> x30, Pallas kernels: 160 us -> 161 us  [call(): pl.pallas_call(body, out_shape=out, grid_spec=pltpu.PrefetchScalarGridSpe...]
    unnamed x150 -> x156, local copies, waits for them, and re-layouts: 22.4 us -> 22.2 us
  transfers between devices with their start and end apart: 46 -> 48, of which waited for: 18 -> 18; matrix products, arithmetic and copies ran while one was open for 10% -> 9% of each run, Pallas kernels for 30% -> 32%
where the time goes in v5:
time: 400 us; the launch traced here: 393 us
  Pallas kernels  161 us (40%)
  waiting for transfers between devices  111 us (28%)
  starting transfers between devices  46.7 us (12%)
  local copies, waits for them, and re-layouts  31.3 us (8%)
  between operations  16.7 us (4%)
  other arithmetic  16.2 us (4%)
  matrix products  10.2 us (3%)
    pallas_call x30, Pallas kernels, call(): pl.pallas_call(body, out_shape=out, grid_spec=pltpu.PrefetchScalarGridSpe...  161 us
    all_gather x2, waiting for transfers between devices, gather(): lax.all_gather(add(self.mine, self.far, none), ('c', 'x', 'z'), axis=0)  57.2 us
    ppermute x28, waiting for transfers between devices, exchange(): return lax.ppermute(v, RING[ring], pairs)  46.8 us
    ppermute x28, starting transfers between devices, exchange(): return lax.ppermute(v, RING[ring], pairs)  36.3 us
    unnamed x156, local copies, waits for them, and re-layouts  22.2 us
    dot_general x4, matrix products, dot(): return jnp.dot(a, b, preferred_element_type=f32)  10.2 us
    ppermute x15, starting transfers between devices, core_swap(): return lax.ppermute(v, 'c', [(0, 1), (1, 0)])  8.38 us
  transfers between devices with their start and end apart: 48, of which 18 were waited for; matrix products, arithmetic and copies ran while one was open for 9% of the time, Pallas kernels for 32%

profile of v5, /device:TPU:1, one launch (start us, length us, event | category | flops | bytes accessed | tf_op | source)
XLA Modules:
  0.0 392.9 jit_solution(14495502543650198161)
XLA Ops:
  12.7 4.3 %collective-permute-done.refs_1_ = bf16[144,1024]{1,0:T(8,128)(2,1)S(1)} collective-permute-done((bf16[144,1024]{1,0:T(8,128)(2,1)}, bf16[144,1024]{1,0:T(8,128)(2,1)S(1)}, u32[]{:S(2)}, u32[]{:S(2)}) %collective-permute-start) | collective-permute-done | bytes 294944 | tf_op jit(solution)/shard_map/ppermute | solution.py:814
  17.8 4.3 %shard_map.348 = (bf16[256,2048]{1,0:T(8,128)(2,1)}, bf16[3,256,1024]{2,1,0:T(8,128)(2,1)}, bf16[768,1024]{1,0:T(8,128)(2,1)}) custom-call(s32[1]{0:T(128)} %bitcast.8.s, bf16[512,2048]{1,0:T(8,128)(2,1)} %refs_0_.3, bf16[512,1024]{1,0:T(8,128)(2,1)} %refs_1_.4, bf16[512,1024]{1,0:T(8,128)(2,1)} %refs_2_.3, bf16[512,1024]{1,0:T(8,128)(2,1)} %refs_3_.4, ...), custom_call_target="tpu_custom_call" | custom-call | tf_op jit(solution)/shard_map/pallas_call | solution.py:68
  24.9 4.7 %fusion.10 = (bf16[576,512]{1,0:T(8,128)(2,1)S(1)}, bf16[576,512]{1,0:T(8,128)(2,1)S(1)}) fusion(f32[512]{0:T(512)S(1)} %negate_power_fusion, f32[576]{0:T(1024)S(1)} %subtract_convert_fusion), kind=kLoop, calls=%fused_computation.21 | loop fusion | flops 884736 | bytes 1184000 | tf_op jit(solution)/shard_map/convert.1
  34.1 4.9 %shard_map.350 = (bf16[576,1024]{1,0:T(8,128)(2,1)}, bf16[576,1024]{1,0:T(8,128)(2,1)}, bf16[64,3072]{1,0:T(8,128)(2,1)}, bf16[4,64,768]{2,1,0:T(8,128)(2,1)}) custom-call(s32[3]{0:T(128)} %pad_add_fusion.s, f32[192,1024]{1,0:T(8,128)} %bitcast.83, f32[192,1024]{1,0:T(8,128)} %bitcast.92, bf16[192,1024]{1,0:T(8,128)(2,1)} %bitcast.85, ...), custom_call_target="tpu_custom_call" | custom-call | tf_op jit(solution)/shard_map/pallas_call | solution.py:68
  48.3 6.0 %collective-permute-done.2.refs_1_ = bf16[3,256,1024]{2,1,0:T(8,128)(2,1)} collective-permute-done((bf16[3,256,1024]{2,1,0:T(8,128)(2,1)}, bf16[3,256,1024]{2,1,0:T(8,128)(2,1)}, u32[]{:S(2)}, u32[]{:S(2)}) %collective-permute-start.2) | collective-permute-done | bytes 1572896 | tf_op jit(solution)/shard_map/ppermute | solution.py:814
  62.5 3.9 convolution_convert_fusion.refs_1_.refs_2_.refs_6_
  72.1 7.3 %shard_map.352 = (f32[8,192,640]{2,1,0:T(8,128)}, bf16[192,1024]{1,0:T(8,128)(2,1)}) custom-call(s32[1]{0:T(128)} %constant.24.clone.1.s, f32[192,1024]{1,0:T(8,128)} %fusion.12.refs_0_.refs_7_, bf16[576,2048]{1,0:T(8,128)(2,1)} %convolution_convert_fusion.refs_1_.refs_2_.refs_6_, bf16[576,2048]{1,0:T(8,128)(2,1)} %convolution_convert_fusion.refs_1_.refs_2_.refs_6_, ...), custom_call_target="tpu_custom_call" | custom-call | tf_op jit(solution)/shard_map/pallas_call | solution.py:68
  82.1 4.1 %shard_map.353 = (f32[192,1024]{1,0:T(8,128)}, bf16[192,1024]{1,0:T(8,128)(2,1)}, bf16[192,1024]{1,0:T(8,128)(2,1)}) custom-call(s32[3]{0:T(128)} %pad_add_fusion.s, bf16[192,1024]{1,0:T(8,128)(2,1)} %get-tuple-element.105.refs_0_.refs_12_.refs_13_, bf16[1024,1024]{1,0:T(8,128)(2,1)} %pad_maximum_fusion.1.refs_1_.refs_4_, bf16[192,1024]{1,0:T(8,128)(2,1)} %bitcast.86, ...), custom_call_target="tpu_custom_call" | custom-call | tf_op jit(solution)/shard_map/pallas_call | solution.py:68
  87.0 15.5 %shard_map.354 = (bf16[192,4096]{1,0:T(8,128)(2,1)}, bf16[192,4096]{1,0:T(8,128)(2,1)}, bf16[192,1024]{1,0:T(8,128)(2,1)}, f32[192,1024]{1,0:T(8,128)}, f32[4,1024]{1,0:T(4,128)}) custom-call(s32[1]{0:T(128)} %bitcast.s, bf16[192,1024]{1,0:T(8,128)(2,1)} %get-tuple-element.107.refs_0_, f32[192,1024]{1,0:T(8,128)} %get-tuple-element.108.refs_1_.refs_9_.refs_2_, ...), custom_call_target="tpu_custom_call" | custom-call | tf_op jit(solution)/shard_map/pallas_call | solution.py:68
  106.1 5.0 %shard_map.356 = (f32[192,1024]{1,0:T(8,128)}, bf16[192,1024]{1,0:T(8,128)(2,1)}, bf16[192,1024]{1,0:T(8,128)(2,1)}, f32[1,1024]{1,0:T(1,128)}, f32[1,1024]{1,0:T(1,128)}, /*index=5*/f32[1,1024]{1,0:T(1,128)}) custom-call(s32[3]{0:T(128)} %pad_add_fusion.s, bf16[192,1024]{1,0:T(8,128)(2,1)} %bitcast.89, f32[192,1024]{1,0:T(8,128)} %get-tuple-element.114.refs_1_, ...), custom_call_target="tpu_custom_call" | custom-call | tf_op jit(solution)/shard_map/pallas_call | solution.py:68
  114.4 11.6 %shard_map.357 = (bf16[2,2,512,512]{3,2,1,0:T(8,128)(2,1)}, bf16[2,2,512,512]{3,2,1,0:T(8,128)(2,1)}, bf16[2,2,128,2560]{3,2,1,0:T(8,128)(2,1)}, bf16[2,2,128,2560]{3,2,1,0:T(8,128)(2,1)}) custom-call(s32[10]{0:T(128)} %stack.97.s, bf16[192,4096]{1,0:T(8,128)(2,1)} %get-tuple-element.113.refs_1_.refs_5_.refs_0_, ...), custom_call_target="tpu_custom_call" | custom-call | tf_op jit(solution)/shard_map/pallas_call | solution.py:68
  126.0 3.9 collective-permute-start.18
  130.1 3.7 collective-permute-start.17
  133.7 8.9 %shard_map.358 = (bf16[2,576,1024]{2,1,0:T(8,128)(2,1)}, bf16[576,1024]{1,0:T(8,128)(2,1)}, bf16[576,1024]{1,0:T(8,128)(2,1)}, bf16[576,1024]{1,0:T(8,128)(2,1)}...) custom-call(s32[1]{0:T(128)} %bitcast.8.s, f32[192,1024]{1,0:T(8,128)} %fusion.12.refs_0_.refs_7_, ...), custom_call_target="tpu_custom_call" | custom-call | tf_op jit(solution)/shard_map/pallas_call | solution.py:68
  143.9 6.6 %shard_map.359 = (f32[64,1024]{1,0:T(8,128)}, bf16[64,1024]{1,0:T(8,128)(2,1)}) custom-call(s32[6]{0:T(128)} %stack.88.s, bf16[64,3072]{1,0:T(8,128)(2,1)} %get-tuple-element.111.refs_0_, bf16[1536,1024]{1,0:T(8,128)(2,1)} %refs_1_.5, bf16[768,1024]{1,0:T(8,128)(2,1)} %shard_map.355.refs_2_, bf16[768,1024]{1,0:T(8,128)(2,1)} %collective-permute-done.11.refs_3_, ...), custom_call_target="tpu_custom_call" | custom-call | tf_op jit(solution)/shard_map/pallas_call | solution.py:68
  153.0 4.6 %shard_map.360 = (f32[1,128]{1,0:T(1,128)}, bf16[64,1024]{1,0:T(8,128)(2,1)}, bf16[64,1024]{1,0:T(8,128)(2,1)}) custom-call(s32[1]{0:T(128)} %constant.24.clone.1.s, f32[192,1024]{1,0:T(8,128)} %fusion.12.refs_0_.refs_7_, bf16[576,2048]{1,0:T(8,128)(2,1)} %convolution_convert_fusion.refs_1_.refs_2_.refs_6_, ...), custom_call_target="tpu_custom_call" | custom-call | tf_op jit(solution)/shard_map/pallas_call | solution.py:68
  157.6 5.3 %shard_map.361 = (bf16[64,1024]{1,0:T(8,128)(2,1)}, f32[1,1024]{1,0:T(1,128)}) custom-call(s32[3]{0:T(128)} %pad_add_fusion.s, bf16[64,1024]{1,0:T(8,128)(2,1)} %get-tuple-element.129.refs_0_, bf16[64,1024]{1,0:T(8,128)(2,1)} %get-tuple-element.130.refs_1_, bf16[1024,2048]{1,0:T(8,128)(2,1)} %copy-done, f32[64,1024]{1,0:T(8,128)} %get-tuple-element.122.refs_5_.refs_3_, ...), custom_call_target="tpu_custom_call" | custom-call | tf_op jit(solution)/shard_map/pallas_call | solution.py:68
  163.2 4.9 %collective-permute-done.22.refs_5_ = bf16[64,1024]{1,0:T(8,128)(2,1)S(1)} collective-permute-done((bf16[64,1024]{1,0:T(8,128)(2,1)}, bf16[64,1024]{1,0:T(8,128)(2,1)S(1)}, u32[]{:S(2)}, u32[]{:S(2)}) %collective-permute-start.22) | collective-permute-done | bytes 131104 | tf_op jit(solution)/shard_map/ppermute | solution.py:814
  169.6 4.3 %shard_map.362 = (bf16[2,512,512]{2,1,0:T(8,128)(2,1)}, bf16[2,128,2560]{2,1,0:T(8,128)(2,1)}) custom-call(s32[10]{0:T(128)} %stack.97.s, bf16[2,2,512,512]{3,2,1,0:T(8,128)(2,1)} %get-tuple-element.126.refs_0_, bf16[2,2,512,512]{3,2,1,0:T(8,128)(2,1)} %collective-permute-done.17.refs_1_, ...), custom_call_target="tpu_custom_call" | custom-call | tf_op jit(solution)/shard_map/pallas_call | solution.py:68
  177.7 10.4 %shard_map.363 = (bf16[2,2,128,1024]{3,2,1,0:T(8,128)(2,1)}, bf16[2,2,128,1024]{3,2,1,0:T(8,128)(2,1)}, bf16[2,2,128,1024]{3,2,1,0:T(8,128)(2,1)}, bf16[2,2,128,1024]{3,2,1,0:T(8,128)(2,1)}) custom-call(s32[10]{0:T(128)} %stack.97.s, bf16[576,1024]{1,0:T(8,128)(2,1)} %get-tuple-element.101.refs_2_.refs_5_.refs_0_.refs_1_.refs_6_.refs_7_, ...), custom_call_target="tpu_custom_call" | custom-call | tf_op jit(solution)/shard_map/pallas_call | solution.py:68
  193.1 3.7 shard_map.364
  205.8 9.4 %shard_map.365 = (f32[192,1024]{1,0:T(8,128)}, f32[1,1024]{1,0:T(1,128)}, f32[1,1024]{1,0:T(1,128)}) custom-call(s32[3]{0:T(128)} %pad_add_fusion.s, bf16[2,576,1024]{2,1,0:T(8,128)(2,1)} %get-tuple-element.121.refs_5_.refs_0_, bf16[192,1024]{1,0:T(8,128)(2,1)} %get-tuple-element.125.refs_10_.refs_1_, bf16[1024,2048]{1,0:T(8,128)(2,1)} %copy-done, ...), custom_call_target="tpu_custom_call" | custom-call | tf_op jit(solution)/shard_map/pallas_call | solution.py:68
  223.3 3.7 shard_map.367.refs_10_.refs_6_.refs_8_
  228.9 3.8 shard_map.368
  259.0 5.9 %collective-permute-done.36.refs_3_ = bf16[2,2,32,1024]{3,2,1,0:T(8,128)(2,1)S(1)} collective-permute-done((bf16[2,2,32,1024]{3,2,1,0:T(8,128)(2,1)}, bf16[2,2,32,1024]{3,2,1,0:T(8,128)(2,1)S(1)}, u32[]{:S(2)}, u32[]{:S(2)}) %collective-permute-start.36) | collective-permute-done | bytes 262176 | tf_op jit(solution)/shard_map/ppermute | solution.py:814
  272.4 7.1 %collective-permute-done.40.refs_4_ = bf16[2,32,1024]{2,1,0:T(8,128)(2,1)S(1)} collective-permute-done((bf16[2,32,1024]{2,1,0:T(8,128)(2,1)}, bf16[2,32,1024]{2,1,0:T(8,128)(2,1)S(1)}, u32[]{:S(2)}, u32[]{:S(2)}) %collective-permute-start.40) | collective-permute-done | bytes 131104 | tf_op jit(solution)/shard_map/ppermute | solution.py:814
  286.0 4.9 %collective-permute-done.43.refs_1_ = bf16[240,512]{1,0:T(8,128)(2,1)S(1)} collective-permute-done((bf16[240,512]{1,0:T(8,128)(2,1)}, bf16[240,512]{1,0:T(8,128)(2,1)S(1)}, u32[]{:S(2)}, u32[]{:S(2)}) %collective-permute-start.43) | collective-permute-done | bytes 245792 | tf_op jit(solution)/shard_map/ppermute | solution.py:814
  294.6 5.6 %collective-permute-done.44.refs_1_ = bf16[240,512]{1,0:T(8,128)(2,1)S(1)} collective-permute-done((bf16[240,512]{1,0:T(8,128)(2,1)}, bf16[240,512]{1,0:T(8,128)(2,1)S(1)}, u32[]{:S(2)}, u32[]{:S(2)}) %collective-permute-start.44) | collective-permute-done | bytes 245792 | tf_op jit(solution)/shard_map/ppermute | solution.py:986
  300.2 18.2 %all-gather.9.cloned.1.call-done = bf16[9216,512]{1,0:T(8,128)(2,1)} async-done(((bf16[288,512]{1,0:T(8,128)(2,1)}), bf16[9216,512]{1,0:T(8,128)(2,1)}) %all-gather.9.cloned.1.call-update) | async-done | bytes 9437200 | tf_op jit(solution)/shard_map/all_gather | solution.py:989
  322.6 11.0 %shard_map.377 = (f32[4,4,128,1024]{3,2,1,0:T(8,128)}, f32[4,4,32,4096]{3,2,1,0:T(8,128)}, f32[4,4,32,1024]{3,2,1,0:T(8,128)}) custom-call(s32[1]{0:T(128)} %constant.24.clone.1.s, bf16[32,288,512]{2,1,0:T(8,128)(2,1)} %bitcast.77, bf16[240,512]{1,0:T(8,128)(2,1)} %shard_map.376.refs_1_), custom_call_target="tpu_custom_call" | custom-call | tf_op jit(solution)/shard_map/pallas_call | solution.py:68
  333.6 39.1 %all-gather.11.cloned.1.call-done = bf16[7680,512]{1,0:T(8,128)(2,1)} async-done(((bf16[240,512]{1,0:T(8,128)(2,1)}), bf16[7680,512]{1,0:T(8,128)(2,1)}) %all-gather.11.cloned.1.call-update) | async-done | bytes 7864336 | tf_op jit(solution)/shard_map/all_gather | solution.py:989
  374.4 9.8 %shard_map.378 = (f32[4,4,32,2048]{3,2,1,0:T(8,128)}, f32[4,4,32,1024]{3,2,1,0:T(8,128)}, f32[4,4,32,1024]{3,2,1,0:T(8,128)}, f32[4,4,96,1024]{3,2,1,0:T(8,128)}) custom-call(s32[1]{0:T(128)} %constant.24.clone.1.s, bf16[32,240,512]{2,1,0:T(8,128)(2,1)} %bitcast.81, f32[4,4,128,1024]{3,2,1,0:T(8,128)} %get-tuple-element.167.refs_1_), custom_call_target="tpu_custom_call" | custom-call | tf_op jit(solution)/shard_map/pallas_call | solution.py:68
  (293 shorter events, 130.0 us)
Async XLA Ops:
  7.2 79.1 %all-gather.7.cloned.1.call-start = ((), (), s32[]{:S(2)}) async-start(), calls=%async_computation | async-start | bytes 8650752 | tf_op jit(solution)/shard_map/all_gather | solution.py:1046
  17.8 300.6 %all-gather.9.cloned.1.call-start = ((), (), s32[]{:S(2)}) async-start(), calls=%async_computation.1 | async-start | bytes 9732096 | tf_op jit(solution)/shard_map/all_gather | solution.py:989
  22.1 26.2 %collective-permute-start.1 = (bf16[256,2048]{1,0:T(8,128)(2,1)}, bf16[256,2048]{1,0:T(8,128)(2,1)}, u32[]{:S(2)}, u32[]{:S(2)}) collective-permute-start(bf16[256,2048]{1,0:T(8,128)(2,1)} %get-tuple-element.97.refs_2_), channel_id=1, source_target_pairs={{0,1},{2,67},{1,0},{3,66},{64,65},{66,3},{65,64},{67,2},{4,5},{6,7... | collective-permute-start | bytes 3145736 | tf_op jit(solution)/shard_map/ppermute | solution.py:814
  24.8 29.5 %collective-permute-start.2 = (bf16[3,256,1024]{2,1,0:T(8,128)(2,1)}, bf16[3,256,1024]{2,1,0:T(8,128)(2,1)}, u32[]{:S(2)}, u32[]{:S(2)}) collective-permute-start(bf16[3,256,1024]{2,1,0:T(8,128)(2,1)} %get-tuple-element.100), channel_id=1, source_target_pairs={{0,1},{2,67},{1,0},{3,66},{64,65},{66,3},{65,64},{67,2},{4,5},{6,7... | collective-permute-start | bytes 4718600 | tf_op jit(solution)/shard_map/ppermute | solution.py:814
  43.3 37.7 %collective-permute-start.7 = (bf16[192,1024]{1,0:T(8,128)(2,1)S(1)}, bf16[192,1024]{1,0:T(8,128)(2,1)S(1)}, u32[]{:S(2)}, u32[]{:S(2)}) collective-permute-start(bf16[192,1024]{1,0:T(8,128)(2,1)S(1)} %bitcast.91), channel_id=1, source_target_pairs={{0,2},{2,0},{1,3},{3,1},{4,6},{6,4},{5,7},{7,5},{8,10},{10,8},{9,1... | collective-permute-start | bytes 1179656 | tf_op jit(solution)/shard_map/ppermute | solution.py:802
  55.6 25.3 %collective-permute-start.6 = (bf16[576,1024]{1,0:T(8,128)(2,1)S(1)}, bf16[576,1024]{1,0:T(8,128)(2,1)S(1)}, u32[]{:S(2)}, u32[]{:S(2)}) collective-permute-start(bf16[576,1024]{1,0:T(8,128)(2,1)S(1)} %copy-done.2), channel_id=1, source_target_pairs={{0,2},{2,0},{1,3},{3,1},{4,6},{6,4},{5,7},{7,5},{8,10},{10,8},{9,1... | collective-permute-start | bytes 3538952 | tf_op jit(solution)/shard_map/ppermute | solution.py:802
  55.9 10.5 %collective-permute-start.3 = (bf16[3,256,1024]{2,1,0:T(8,128)(2,1)}, bf16[3,256,1024]{2,1,0:T(8,128)(2,1)S(1)}, u32[]{:S(2)}, u32[]{:S(2)}) collective-permute-start(bf16[3,256,1024]{2,1,0:T(8,128)(2,1)} %get-tuple-element.102), channel_id=1, source_target_pairs={{0,2},{2,0},{1,3},{3,1},{4,6},{6,4},{5,7},{7,5},{8,10},{10,8},{9,1... | collective-permute-start | bytes 4718600 | tf_op jit(solution)/shard_map/ppermute | solution.py:802
  57.2 29.1 %collective-permute-start.9 = (bf16[256,768]{1,0:T(8,128)(2,1)S(1)}, bf16[256,768]{1,0:T(8,128)(2,1)S(1)}, u32[]{:S(2)}, u32[]{:S(2)}) collective-permute-start(bf16[256,768]{1,0:T(8,128)(2,1)S(1)} %pad_maximum_fusion.4.refs_0_), channel_id=1, source_target_pairs={{0,2},{2,0},{1,3},{3,1},{4,6},{6,4},{5,7},{7,5},{8,10},{10,8},{9,1... | collective-permute-start | bytes 1179656 | tf_op jit(solution)/shard_map/ppermute | solution.py:802
  102.5 10.6 %collective-permute-start.12 = (bf16[192,4096]{1,0:T(8,128)(2,1)}, bf16[192,4096]{1,0:T(8,128)(2,1)S(1)}, u32[]{:S(2)}, u32[]{:S(2)}) collective-permute-start(bf16[192,4096]{1,0:T(8,128)(2,1)} %get-tuple-element.113.refs_1_.refs_5_.refs_0_), channel_id=1, source_target_pairs={{0,2},{2,0},{1,3},{3,1},{4,6},{6,4},{5,7},{7,5},{8,10},{10,8},{9,1... | collective-permute-start | bytes 4718600 | tf_op jit(solution)/shard_map/ppermute | solution.py:802
  102.6 10.6 %collective-permute-start.14 = (bf16[192,4096]{1,0:T(8,128)(2,1)}, bf16[192,4096]{1,0:T(8,128)(2,1)}, u32[]{:S(2)}, u32[]{:S(2)}) collective-permute-start(bf16[192,4096]{1,0:T(8,128)(2,1)} %get-tuple-element.117.refs_10_), channel_id=1, source_target_pairs={{0,2},{2,0},{1,3},{3,1},{4,6},{6,4},{5,7},{7,5},{8,10},{10,8},{9,1... | collective-permute-start | bytes 4718600 | tf_op jit(solution)/shard_map/ppermute | solution.py:802
  103.1 26.8 %collective-permute-start.10 = (bf16[768,1024]{1,0:T(8,128)(2,1)}, bf16[768,1024]{1,0:T(8,128)(2,1)}, u32[]{:S(2)}, u32[]{:S(2)}) collective-permute-start(bf16[768,1024]{1,0:T(8,128)(2,1)} %get-tuple-element.112), channel_id=1, source_target_pairs={{0,1},{2,67},{1,0},{3,66},{64,65},{66,3},{65,64},{67,2},{4,5},{6,7... | collective-permute-start | bytes 4718600 | tf_op jit(solution)/shard_map/ppermute | solution.py:814
  126.0 42.1 %collective-permute-start.18 = (bf16[2,2,128,2560]{3,2,1,0:T(8,128)(2,1)}, bf16[2,2,128,2560]{3,2,1,0:T(8,128)(2,1)S(1)}, u32[]{:S(2)}, u32[]{:S(2)}) collective-permute-start(bf16[2,2,128,2560]{3,2,1,0:T(8,128)(2,1)} %get-tuple-element.128), channel_id=1, source_target_pairs={{0,4},{2,14},{4,0},{6,10},{8,12},{10,6},{12,8},{14,2},{1,5},{3,15}... | collective-permute-start | bytes 7864328 | tf_op jit(solution)/shard_map/ppermute | solution.py:814
  129.9 13.4 %collective-permute-start.11 = (bf16[768,1024]{1,0:T(8,128)(2,1)}, bf16[768,1024]{1,0:T(8,128)(2,1)}, u32[]{:S(2)}, u32[]{:S(2)}) collective-permute-start(bf16[768,1024]{1,0:T(8,128)(2,1)} %shard_map.355.refs_2_), channel_id=1, source_target_pairs={{0,2},{2,0},{1,3},{3,1},{4,6},{6,4},{5,7},{7,5},{8,10},{10,8},{9,1... | collective-permute-start | bytes 4718600 | tf_op jit(solution)/shard_map/ppermute | solution.py:802
  130.1 38.0 %collective-permute-start.17 = (bf16[2,2,512,512]{3,2,1,0:T(8,128)(2,1)}, bf16[2,2,512,512]{3,2,1,0:T(8,128)(2,1)}, u32[]{:S(2)}, u32[]{:S(2)}) collective-permute-start(bf16[2,2,512,512]{3,2,1,0:T(8,128)(2,1)} %get-tuple-element.120.refs_7_), channel_id=1, source_target_pairs={{0,16},{2,50},{16,0},{18,34},{32,48},{34,18},{48,32},{50,2},{1,17}... | collective-permute-start | bytes 6291464 | tf_op jit(solution)/shard_map/ppermute | solution.py:814
  142.6 14.9 %collective-permute-start.19 = (bf16[576,1024]{1,0:T(8,128)(2,1)}, bf16[576,1024]{1,0:T(8,128)(2,1)}, u32[]{:S(2)}, u32[]{:S(2)}) collective-permute-start(bf16[576,1024]{1,0:T(8,128)(2,1)} %get-tuple-element.131), channel_id=1, source_target_pairs={{0,2},{2,0},{1,3},{3,1},{4,6},{6,4},{5,7},{7,5},{8,10},{10,8},{9,1... | collective-permute-start | bytes 3538952 | tf_op jit(solution)/shard_map/ppermute | solution.py:802
  142.7 14.8 %collective-permute-start.21 = (bf16[576,1024]{1,0:T(8,128)(2,1)}, bf16[576,1024]{1,0:T(8,128)(2,1)}, u32[]{:S(2)}, u32[]{:S(2)}) collective-permute-start(bf16[576,1024]{1,0:T(8,128)(2,1)} %get-tuple-element.132.refs_14_), channel_id=1, source_target_pairs={{0,2},{2,0},{1,3},{3,1},{4,6},{6,4},{5,7},{7,5},{8,10},{10,8},{9,1... | collective-permute-start | bytes 3538952 | tf_op jit(solution)/shard_map/ppermute | solution.py:802
  143.2 14.3 %collective-permute-start.20 = (bf16[192,1024]{1,0:T(8,128)(2,1)}, bf16[192,1024]{1,0:T(8,128)(2,1)}, u32[]{:S(2)}, u32[]{:S(2)}) collective-permute-start(bf16[192,1024]{1,0:T(8,128)(2,1)} %get-tuple-element.125.refs_10_.refs_1_), channel_id=1, source_target_pairs={{0,2},{2,0},{1,3},{3,1},{4,6},{6,4},{5,7},{7,5},{8,10},{10,8},{9,1... | collective-permute-start | bytes 1179656 | tf_op jit(solution)/shard_map/ppermute | solution.py:802
  174.0 17.1 %collective-permute-start.24 = (bf16[2,128,2560]{2,1,0:T(8,128)(2,1)}, bf16[2,128,2560]{2,1,0:T(8,128)(2,1)S(1)}, u32[]{:S(2)}, u32[]{:S(2)}) collective-permute-start(bf16[2,128,2560]{2,1,0:T(8,128)(2,1)} %get-tuple-element.135), channel_id=1, source_target_pairs={{0,12},{2,6},{4,8},{6,2},{8,4},{10,14},{12,0},{14,10},{1,13},{3,7}... | collective-permute-start | bytes 3932168 | tf_op jit(solution)/shard_map/ppermute | solution.py:814
  174.0 17.0 %collective-permute-start.23 = (bf16[2,512,512]{2,1,0:T(8,128)(2,1)}, bf16[2,512,512]{2,1,0:T(8,128)(2,1)S(1)}, u32[]{:S(2)}, u32[]{:S(2)}) collective-permute-start(bf16[2,512,512]{2,1,0:T(8,128)(2,1)} %get-tuple-element.134.refs_16_), channel_id=1, source_target_pairs={{0,48},{2,18},{16,32},{18,2},{32,16},{34,50},{48,0},{50,34},{1,49}... | collective-permute-start | bytes 3145736 | tf_op jit(solution)/shard_map/ppermute | solution.py:814
  175.0 16.0 %collective-permute-start.25 = (bf16[128,1024]{1,0:T(8,128)(2,1)S(1)}, bf16[128,1024]{1,0:T(8,128)(2,1)S(1)}, u32[]{:S(2)}, u32[]{:S(2)}) collective-permute-start(bf16[128,1024]{1,0:T(8,128)(2,1)S(1)} %pad_maximum_fusion.5), channel_id=1, source_target_pairs={{0,48},{2,18},{16,32},{18,2},{32,16},{34,50},{48,0},{50,34},{1,49}... | collective-permute-start | bytes 786440 | tf_op jit(solution)/shard_map/ppermute | solution.py:814
  188.2 44.9 %collective-permute-start.26 = (bf16[2,2,128,1024]{3,2,1,0:T(8,128)(2,1)}, bf16[2,2,128,1024]{3,2,1,0:T(8,128)(2,1)S(1)}, u32[]{:S(2)}, u32[]{:S(2)}) collective-permute-start(bf16[2,2,128,1024]{3,2,1,0:T(8,128)(2,1)} %get-tuple-element.137.refs_6_), channel_id=1, source_target_pairs={{0,16},{2,50},{16,0},{18,34},{32,48},{34,18},{48,32},{50,2},{1,17}... | collective-permute-start | bytes 3145736 | tf_op jit(solution)/shard_map/ppermute | solution.py:814
  196.8 20.8 %collective-permute-start.29 = (bf16[2,2,32,2560]{3,2,1,0:T(8,128)(2,1)}, bf16[2,2,32,2560]{3,2,1,0:T(8,128)(2,1)S(1)}, u32[]{:S(2)}, u32[]{:S(2)}) collective-permute-start(bf16[2,2,32,2560]{3,2,1,0:T(8,128)(2,1)} %get-tuple-element.143), channel_id=1, source_target_pairs={{0,16},{2,50},{16,0},{18,34},{32,48},{34,18},{48,32},{50,2},{1,17}... | collective-permute-start | bytes 1966088 | tf_op jit(solution)/shard_map/ppermute | solution.py:814
  197.1 36.0 %collective-permute-start.27 = (bf16[2,2,128,1024]{3,2,1,0:T(8,128)(2,1)S(1)}, bf16[2,2,128,1024]{3,2,1,0:T(8,128)(2,1)S(1)}, u32[]{:S(2)}, u32[]{:S(2)}) collective-permute-start(bf16[2,2,128,1024]{3,2,1,0:T(8,128)(2,1)S(1)} %copy-done.74), channel_id=1, source_target_pairs={{0,4},{2,14},{4,0},{6,10},{8,12},{10,6},{12,8},{14,2},{1,5},{3,15}... | collective-permute-start | bytes 3145736 | tf_op jit(solution)/shard_map/ppermute | solution.py:814
  198.6 18.9 %collective-permute-start.28 = (bf16[2,2,128,512]{3,2,1,0:T(8,128)(2,1)}, bf16[2,2,128,512]{3,2,1,0:T(8,128)(2,1)S(1)}, u32[]{:S(2)}, u32[]{:S(2)}) collective-permute-start(bf16[2,2,128,512]{3,2,1,0:T(8,128)(2,1)} %get-tuple-element.138.refs_9_), channel_id=1, source_target_pairs={{0,4},{2,14},{4,0},{6,10},{8,12},{10,6},{12,8},{14,2},{1,5},{3,15}... | collective-permute-start | bytes 1572872 | tf_op jit(solution)/shard_map/ppermute | solution.py:814
  200.8 21.7 %collective-permute-start.32 = (bf16[256,1024]{1,0:T(8,128)(2,1)S(1)}, bf16[256,1024]{1,0:T(8,128)(2,1)S(1)}, u32[]{:S(2)}, u32[]{:S(2)}) collective-permute-start(bf16[256,1024]{1,0:T(8,128)(2,1)S(1)} %constant_dynamic-update-slice_fusion.3.refs_9_.refs_2_), channel_id=1, source_target_pairs={{0,2},{2,0},{1,3},{3,1},{4,6},{6,4},{5,7},{7,5},{8,10},{10,8},{9,1... | collective-permute-start | bytes 1572872 | tf_op jit(solution)/shard_map/ppermute | solution.py:802
  242.4 8.9 %collective-permute-start.39 = (bf16[288,512]{1,0:T(8,128)(2,1)}, bf16[288,512]{1,0:T(8,128)(2,1)S(1)}, u32[]{:S(2)}, u32[]{:S(2)}) collective-permute-start(bf16[288,512]{1,0:T(8,128)(2,1)} %shard_map.370.refs_7_.refs_0_), channel_id=1, source_target_pairs={{0,64},{64,0},{1,65},{65,1},{2,66},{66,2},{3,67},{67,3},{4,68},{68... | collective-permute-start | bytes 884744 | tf_op jit(solution)/shard_map/ppermute | solution.py:986
  253.9 118.7 %all-gather.11.cloned.1.call-start = ((), (), s32[]{:S(2)}) async-start(), calls=%async_computation.2 | async-start | bytes 8110080 | tf_op jit(solution)/shard_map/all_gather | solution.py:989
  253.9 10.9 %collective-permute-start.38 = (bf16[2,2,96,512]{3,2,1,0:T(8,128)(2,1)}, bf16[2,2,96,512]{3,2,1,0:T(8,128)(2,1)S(1)}, u32[]{:S(2)}, u32[]{:S(2)}) collective-permute-start(bf16[2,2,96,512]{3,2,1,0:T(8,128)(2,1)} %get-tuple-element.152), channel_id=1, source_target_pairs={{0,4},{2,14},{4,0},{6,10},{8,12},{10,6},{12,8},{14,2},{1,5},{3,15}... | collective-permute-start | bytes 1179656 | tf_op jit(solution)/shard_map/ppermute | solution.py:814
  255.8 9.1 %collective-permute-start.36 = (bf16[2,2,32,1024]{3,2,1,0:T(8,128)(2,1)}, bf16[2,2,32,1024]{3,2,1,0:T(8,128)(2,1)S(1)}, u32[]{:S(2)}, u32[]{:S(2)}) collective-permute-start(bf16[2,2,32,1024]{3,2,1,0:T(8,128)(2,1)} %get-tuple-element.150.refs_2_), channel_id=1, source_target_pairs={{0,4},{2,14},{4,0},{6,10},{8,12},{10,6},{12,8},{14,2},{1,5},{3,15}... | collective-permute-start | bytes 786440 | tf_op jit(solution)/shard_map/ppermute | solution.py:814
  269.4 10.1 %collective-permute-start.42 = (bf16[2,96,512]{2,1,0:T(8,128)(2,1)}, bf16[2,96,512]{2,1,0:T(8,128)(2,1)S(1)}, u32[]{:S(2)}, u32[]{:S(2)}) collective-permute-start(bf16[2,96,512]{2,1,0:T(8,128)(2,1)} %get-tuple-element.155), channel_id=1, source_target_pairs={{0,12},{2,6},{4,8},{6,2},{8,4},{10,14},{12,0},{14,10},{1,13},{3,7}... | collective-permute-start | bytes 589832 | tf_op jit(solution)/shard_map/ppermute | solution.py:814
  269.4 10.0 %collective-permute-start.40 = (bf16[2,32,1024]{2,1,0:T(8,128)(2,1)}, bf16[2,32,1024]{2,1,0:T(8,128)(2,1)S(1)}, u32[]{:S(2)}, u32[]{:S(2)}) collective-permute-start(bf16[2,32,1024]{2,1,0:T(8,128)(2,1)} %get-tuple-element.153.refs_14_), channel_id=1, source_target_pairs={{0,12},{2,6},{4,8},{6,2},{8,4},{10,14},{12,0},{14,10},{1,13},{3,7}... | collective-permute-start | bytes 393224 | tf_op jit(solution)/shard_map/ppermute | solution.py:814
  270.9 8.6 %collective-permute-start.41 = (bf16[2,32,1024]{2,1,0:T(8,128)(2,1)}, bf16[2,32,1024]{2,1,0:T(8,128)(2,1)S(1)}, u32[]{:S(2)}, u32[]{:S(2)}) collective-permute-start(bf16[2,32,1024]{2,1,0:T(8,128)(2,1)} %get-tuple-element.154), channel_id=1, source_target_pairs={{0,48},{2,18},{16,32},{18,2},{32,16},{34,50},{48,0},{50,34},{1,49}... | collective-permute-start | bytes 393224 | tf_op jit(solution)/shard_map/ppermute | solution.py:814
  (91 other events, 513.9 us)
Sparse Core Ops, SparseCore 0:
  17.9 55.7 all-gather.6
  254.0 64.3 all-gather.8
  321.3 51.3 all-gather.10
